TPU v7x, 256 devices: a whole 4x4x8 slice. The times are simulated.
256 devices in a mesh: dp: 8 (over y, z_lo), space: 32 (over x, z_hi, core).
Axes of the slice: x: 4, y: 4, z: 8 (z_hi: 4, z_lo: 2; z = z_hi * 2 + z_lo), core: 2. Of those that a mesh axis runs over, the one named last changes fastest.
Arguments:
- volume: bfloat16 [8, 32, 32, 32, 384], P('dp', 'space'), may hold values from -6 to 6
- gain_one: float32 [384], replicated, may hold values from 0.5 to 1.5
- gain_two: float32 [384], replicated, may hold values from 0.5 to 1.5
- filter_in_weight: float32 [2, 6, 64, 64], replicated, may hold values from -0.75 to 0.75
- filter_in_bias: float32 [2, 6, 64], replicated, may hold values from -3 to 3
- filter_out_weight: float32 [2, 6, 64, 64], replicated, may hold values from -0.75 to 0.75
- filter_out_bias: float32 [2, 6, 64], replicated, may hold values from -3 to 3
- channel_up: bfloat16 [384, 1536], replicated, may hold values from -0.3125 to 0.3125
- channel_up_bias: float32 [1536], replicated, may hold values from -3 to 3
- channel_down: bfloat16 [1536, 384], replicated, may hold values from -0.15625 to 0.15625
- channel_down_bias: float32 [384], replicated, may hold values from -3 to 3
- cotangent: bfloat16 [8, 32, 32, 32, 384], P('dp', 'space'), may hold values from -6 to 6
Outputs:
- result: bfloat16 [8, 32, 32, 32, 384], P('dp', 'space')
- grad_volume: bfloat16 [8, 32, 32, 32, 384], P('dp', 'space')
- grad_gain_one: float32 [384], replicated
- grad_gain_two: float32 [384], replicated
- grad_filter_in_weight: float32 [2, 6, 64, 64], replicated
- grad_filter_in_bias: float32 [2, 6, 64], replicated
- grad_filter_out_weight: float32 [2, 6, 64, 64], replicated
- grad_filter_out_bias: float32 [2, 6, 64], replicated
- grad_channel_up: float32 [384, 1536], P(None, 'space')
- grad_channel_up_bias: float32 [1536], replicated
- grad_channel_down: float32 [1536, 384], P('space')
- grad_channel_down_bias: float32 [384], replicated
All inputs are finite; a program needn't handle non-finite values.
Results may differ from a plain program's by a relative error of at most 0.013.
Values sent between devices are 32-bit elements; how exact they have to be, the bound alone decides.
No kernel may reach another device: no remote copies, remote signals or barrier semaphores. Data moves between devices by JAX's collectives and lax.ppermute only.
A program may use at most 128 MiB of HBM per device.

v0:
```python
import math

import jax
import jax.numpy as jnp
from jax import lax
from jax.sharding import PartitionSpec as P

WIDTH = 384
BLOCKS = 6
BLOCK = 64
GY = 32
GZ = 32
KEEP_Y = 16
KEEP_Z = 8


EPSILON = 1e-05
SHRINK = 0.01
PRECISE = lax.Precision.HIGHEST


def layer_norm(values, gain):
    center = values - jnp.mean(values, axis=-1, keepdims=True)
    spread = jnp.mean(center * center, axis=-1, keepdims=True)
    return center * lax.rsqrt(spread + EPSILON) * gain


def complex_mix(real_part, imag_part, weight, bias):
    real_out = (
        jnp.einsum("...ni,nio->...no", real_part, weight[0], precision=PRECISE)
        - jnp.einsum("...ni,nio->...no", imag_part, weight[1], precision=PRECISE)
        + bias[0]
    )
    imag_out = (
        jnp.einsum("...ni,nio->...no", imag_part, weight[0], precision=PRECISE)
        + jnp.einsum("...ni,nio->...no", real_part, weight[1], precision=PRECISE)
        + bias[1]
    )
    return (real_out, imag_out)


def soft_shrink(values):
    return values - jnp.clip(values, -SHRINK, SHRINK)


def block_filter(spectrum, in_weight, in_bias, out_weight, out_bias):
    full_shape = spectrum.shape
    split_parts = spectrum.reshape(full_shape[:-1] + (BLOCKS, BLOCK))
    hidden_real, hidden_imag = complex_mix(split_parts[0], split_parts[1], in_weight, in_bias)
    hidden_real = jax.nn.gelu(hidden_real, approximate=True)
    hidden_imag = jax.nn.gelu(hidden_imag, approximate=True)
    out_real, out_imag = complex_mix(hidden_real, hidden_imag, out_weight, out_bias)
    return jnp.stack([soft_shrink(out_real), soft_shrink(out_imag)]).reshape(full_shape)


def tanh_gelu(values):
    return jax.nn.gelu(values, approximate=True)


def angle_table(freqs, length):
    positions = jnp.arange(length, dtype=jnp.int32)
    product = freqs[:, None] * positions[None, :] % length
    angles = product.astype(jnp.float32) * (2.0 * math.pi / length)
    return (jnp.cos(angles), jnp.sin(angles))


def kept_rows():
    return jnp.concatenate(
        [
            jnp.arange(KEEP_Y // 2, dtype=jnp.int32),
            jnp.arange(GY - KEEP_Y // 2, GY, dtype=jnp.int32),
        ]
    )


def to_spectrum(field, weight_z):
    cos_z, sin_z = angle_table(jnp.arange(KEEP_Z, dtype=jnp.int32), GZ)
    cos_y, sin_y = angle_table(kept_rows(), GY)
    real_z = jnp.einsum("bxyzc,kz->bxykc", field, cos_z, precision=PRECISE) * weight_z[:, None]
    imag_z = -jnp.einsum("bxyzc,kz->bxykc", field, sin_z, precision=PRECISE) * weight_z[:, None]
    real_y = jnp.einsum("bxykc,jy->bxjkc", real_z, cos_y, precision=PRECISE) + jnp.einsum(
        "bxykc,jy->bxjkc", imag_z, sin_y, precision=PRECISE
    )
    imag_y = jnp.einsum("bxykc,jy->bxjkc", imag_z, cos_y, precision=PRECISE) - jnp.einsum(
        "bxykc,jy->bxjkc", real_z, sin_y, precision=PRECISE
    )
    stacked = jnp.stack([real_y, imag_y])
    return stacked.reshape(stacked.shape[:3] + (KEEP_Y * KEEP_Z, stacked.shape[-1]))


def along_x(values, sign):
    length = values.shape[2]
    cos_x, sin_x = angle_table(jnp.arange(length, dtype=jnp.int32), length)

    def apply_table(table, part):
        return jnp.einsum("kx,bxmc->bkmc", table, part, precision=PRECISE)

    real_out = apply_table(cos_x, values[0]) - sign * apply_table(sin_x, values[1])
    imag_out = apply_table(cos_x, values[1]) + sign * apply_table(sin_x, values[0])
    return jnp.stack([real_out, imag_out])


def from_spectrum(values, weight_z):
    cos_z, sin_z = angle_table(jnp.arange(KEEP_Z, dtype=jnp.int32), GZ)
    cos_y, sin_y = angle_table(kept_rows(), GY)
    grid = values.reshape(values.shape[:3] + (KEEP_Y, KEEP_Z, values.shape[-1]))
    real_in = grid[0] * weight_z[:, None]
    imag_in = grid[1] * weight_z[:, None]
    real_y = jnp.einsum("jy,bxjkc->bxykc", cos_y, real_in, precision=PRECISE) - jnp.einsum(
        "jy,bxjkc->bxykc", sin_y, imag_in, precision=PRECISE
    )
    imag_y = jnp.einsum("jy,bxjkc->bxykc", cos_y, imag_in, precision=PRECISE) + jnp.einsum(
        "jy,bxjkc->bxykc", sin_y, real_in, precision=PRECISE
    )
    return jnp.einsum("kz,bxykc->bxyzc", cos_z, real_y, precision=PRECISE) - jnp.einsum(
        "kz,bxykc->bxyzc", sin_z, imag_y, precision=PRECISE
    )


def local(
    volume,
    gain_one,
    gain_two,
    filter_in_weight,
    filter_in_bias,
    filter_out_weight,
    filter_out_bias,
    channel_up,
    channel_up_bias,
    channel_down,
    channel_down_bias,
    cotangent,
):
    nspace = lax.axis_size("space")
    samples, slab_cells = (volume.shape[0], volume.shape[1])
    ortho_scale = 1.0 / math.sqrt(slab_cells * nspace * GY * GZ)
    count_tokens = samples * slab_cells * GY * GZ
    single_z = jnp.ones((KEEP_Z,), jnp.float32)
    double_z = jnp.where(jnp.arange(KEEP_Z) == 0, 1.0, 2.0).astype(jnp.float32)
    wide_volume = volume.astype(jnp.float32)
    normed, norm_one_back = jax.vjp(layer_norm, wide_volume, gain_one)
    spectrum_here = (
        along_x(
            lax.all_to_all(
                to_spectrum(normed, single_z), "space", split_axis=3, concat_axis=2, tiled=True
            ),
            -1.0,
        )
        * ortho_scale
    )
    filtered = block_filter(
        spectrum_here, filter_in_weight, filter_in_bias, filter_out_weight, filter_out_bias
    )
    inverse_x = along_x(filtered, 1.0)
    slab_modes = lax.all_to_all(inverse_x, "space", split_axis=2, concat_axis=3, tiled=True)
    mixed = wide_volume + from_spectrum(slab_modes, double_z) * ortho_scale + normed
    normed_two, norm_two_back = jax.vjp(layer_norm, mixed, gain_two)
    inputs = normed_two.astype(jnp.bfloat16).reshape(count_tokens, WIDTH)
    before = jnp.dot(inputs, channel_up, preferred_element_type=jnp.float32) + channel_up_bias
    hidden = tanh_gelu(before).astype(jnp.bfloat16)
    result = (
        (
            mixed.reshape(count_tokens, WIDTH)
            + jnp.dot(hidden, channel_down, preferred_element_type=jnp.float32)
            + channel_down_bias
        )
        .astype(jnp.bfloat16)
        .reshape(volume.shape)
    )
    upstream = cotangent.reshape(count_tokens, WIDTH)
    grad_down_bias = jnp.sum(upstream.astype(jnp.float32), axis=0)
    grad_hidden = lax.dot_general(
        upstream, channel_down, (((1,), (1,)), ((), ())), preferred_element_type=jnp.float32
    )
    gelu_back = jax.vjp(tanh_gelu, before)[1]
    grad_before = gelu_back(grad_hidden)[0].astype(jnp.bfloat16)
    grad_up_bias = jnp.sum(grad_before.astype(jnp.float32), axis=0)
    grad_inputs = lax.dot_general(
        grad_before, channel_up, (((1,), (1,)), ((), ())), preferred_element_type=jnp.float32
    )
    grad_mixed_norm, grad_gain_two = norm_two_back(grad_inputs.reshape(mixed.shape))
    grad_mixed = upstream.astype(jnp.float32).reshape(mixed.shape) + grad_mixed_norm
    received = lax.all_to_all(
        to_spectrum(grad_mixed, double_z), "space", split_axis=3, concat_axis=2, tiled=True
    )
    grad_spectrum = along_x(received, -1.0) * ortho_scale
    filter_back = jax.vjp(
        block_filter,
        spectrum_here,
        filter_in_weight,
        filter_in_bias,
        filter_out_weight,
        filter_out_bias,
    )[1]
    grad_in, grad_fw_in, grad_fb_in, grad_fw_out, grad_fb_out = filter_back(grad_spectrum)
    grad_slab_modes = lax.all_to_all(
        along_x(grad_in, 1.0), "space", split_axis=2, concat_axis=3, tiled=True
    )
    grad_normed = from_spectrum(grad_slab_modes, single_z) * ortho_scale + grad_mixed
    grad_wide, grad_gain_one = norm_one_back(grad_normed)
    grad_volume = (grad_mixed + grad_wide).astype(jnp.bfloat16)
    summed = lax.psum(
        (
            grad_gain_one,
            grad_gain_two,
            grad_fw_in,
            grad_fb_in,
            grad_fw_out,
            grad_fb_out,
            grad_up_bias,
            grad_down_bias,
        ),
        ("dp", "space"),
    )
    grad_down = lax.psum_scatter(
        lax.dot_general(
            hidden, upstream, (((0,), (0,)), ((), ())), preferred_element_type=jnp.float32
        ),
        "space",
        scatter_dimension=0,
        tiled=True,
    )
    up_term = lax.dot_general(
        inputs, grad_before, (((0,), (0,)), ((), ())), preferred_element_type=jnp.float32
    )
    grad_up = lax.psum_scatter(up_term, "space", scatter_dimension=1, tiled=True)
    grad_up, grad_down = lax.psum((grad_up, grad_down), "dp")
    return (
        result,
        grad_volume,
        summed[0],
        summed[1],
        summed[2],
        summed[3],
        summed[4],
        summed[5],
        grad_up,
        summed[6],
        grad_down,
        summed[7],
    )


def solution(mesh):
    return jax.shard_map(
        local,
        mesh=mesh,
        in_specs=(
            P("dp", "space", None, None, None),
            P(),
            P(),
            P(),
            P(),
            P(),
            P(),
            P(),
            P(),
            P(),
            P(),
            P("dp", "space", None, None, None),
        ),
        out_specs=(
            P("dp", "space", None, None, None),
            P("dp", "space", None, None, None),
            P(),
            P(),
            P(),
            P(),
            P(),
            P(),
            P(None, "space"),
            P(),
            P("space", None),
            P(),
        ),
        check_vma=False,
    )
```

profile of v0, /device:TPU:32, one launch (start us, length us, event | category | flops | bytes accessed | tf_op | source)
XLA Modules:
  0.0 517.4 jit_solution(12273574396627739214)
XLA Ops:
  8.1 1.5 convert_reduce_fusion.1
  9.6 1.5 fusion.20
  11.8 1.1 fusion.43
  12.9 1.1 fusion.37
  16.2 1.2 copy.112
  17.3 10.6 %all-to-all-start = ((f32[2,1,1,128,384]{4,2,1,0,3:T(1,128)}), f32[2,1,1,128,384]{4,2,1,0,3:T(1,128)S(1)}, u32[]{:S(2)}, u32[]{:S(2)}) async-start(f32[2,1,1,128,384]{4,2,1,0,3:T(1,128)} %copy.112), calls=%async_computation | async-start | bytes 786432 | tf_op jit(solution)/shard_map/all_to_all | solution.py:144
  28.0 16.3 %all-to-all-done = f32[2,1,1,128,384]{4,2,1,0,3:T(1,128)S(1)} async-done(((f32[2,1,1,128,384]{4,2,1,0,3:T(1,128)}), f32[2,1,1,128,384]{4,2,1,0,3:T(1,128)S(1)}, u32[]{:S(2)}, u32[]{:S(2)}) %all-to-all-start) | async-done | bytes 393248 | tf_op jit(solution)/shard_map/all_to_all | solution.py:144
  47.9 1.2 reshape.708
  51.9 1.4 fusion.149
  53.3 1.4 clamp_subtract_fusion.1
  55.5 2.4 clamp_subtract_fusion
  60.5 3.9 all-to-all-start.1
  64.7 16.1 %all-to-all-done.1 = f32[2,1,32,4,384]{4,3,1,0,2:T(4,128)S(1)} async-done(((f32[2,1,32,4,384]{4,3,1,0,2:T(4,128)}), f32[2,1,32,4,384]{4,3,1,0,2:T(4,128)S(1)}, u32[]{:S(2)}, u32[]{:S(2)}) %all-to-all-start.1) | async-done | bytes 393248 | tf_op jit(solution)/shard_map/all_to_all | solution.py:155
  83.7 1.5 fusion.161
  85.2 2.1 fusion.564
  89.0 4.9 multiply_convert_fusion
  94.0 1.7 copy-done.62
  95.7 3.2 fusion.567
  98.9 8.2 %convert_reduce_fusion = (f32[1536]{0:T(1024)}, bf16[1024,1536]{1,0:T(8,128)(2,1)S(1)}) fusion(f32[1024,1536]{1,0:T(8,128)} %get-tuple-element.91, f32[1536]{0:T(1024)} %param.23, bf16[1024,384]{1,0:T(8,128)(2,1)} %bitcast.728, bf16[1536,384]{1,0:T(8,128)(2,1)} %param.24), kind=kOutput, calls=%fused_computation.9 | convolution fusion | flops 1244133888 | bytes 11415552 | tf_op jit(solution)/shard_map/dot_general | solution.py:172
  107.1 1.8 fusion.565
  109.7 1.3 multiply_reduce_fusion
  111.0 1.4 convert_reduce_fusion.2
  116.1 1.1 copy.140
  117.3 4.1 all-to-all-start.2
  121.4 5.5 %fusion.566 = f32[384,1536]{0,1:T(8,128)} fusion(bf16[1024,384]{1,0:T(8,128)(2,1)} %bitcast.735, bf16[1024,1536]{1,0:T(8,128)(2,1)} %copy-done.61), kind=kOutput, calls=%fused_computation.623 | convolution fusion | flops 1207959552 | bytes 6291456 | tf_op jit(solution)/shard_map/dot_general | solution.py:223
  127.6 5.0 fusion.27
  132.5 5.2 %all-to-all-done.2 = f32[2,1,1,128,384]{4,2,1,0,3:T(1,128)S(1)} async-done(((f32[2,1,1,128,384]{4,2,1,0,3:T(1,128)}), f32[2,1,1,128,384]{4,2,1,0,3:T(1,128)S(1)}, u32[]{:S(2)}, u32[]{:S(2)}) %all-to-all-start.2) | async-done | bytes 393248 | tf_op jit(solution)/shard_map/all_to_all | solution.py:183
  141.6 1.0 fusion.554
  143.8 1.4 fusion.102
  145.5 1.4 fusion.117
  150.1 1.2 copy.150
  151.4 1.0 reshape.732
  152.8 1.3 fusion.71
  154.1 1.3 fusion.263
  156.9 4.8 all-to-all-start.3
  172.0 6.0 %all-to-all-done.3 = f32[2,1,32,4,384]{4,3,1,0,2:T(4,128)S(1)} async-done(((f32[2,1,32,4,384]{4,3,1,0,2:T(4,128)}), f32[2,1,32,4,384]{4,3,1,0,2:T(4,128)S(1)}, u32[]{:S(2)}, u32[]{:S(2)}) %all-to-all-start.3) | async-done | bytes 393248 | tf_op jit(solution)/shard_map/all_to_all | solution.py:196
  180.2 1.4 fusion.46
  181.6 1.5 fusion.158
  183.1 2.0 fusion.21
  185.2 1.1 copy-done.5
  186.4 1.3 fusion.19
  188.3 92.7 %reduce-scatter.3.cloned.1.call-done = f32[384,48]{0,1:T(8,128)} async-done(((f32[384,1536]{0,1:T(8,128)}), f32[384,48]{0,1:T(8,128)}) %reduce-scatter.3.cloned.1.call-update) | async-done | bytes 73744 | tf_op jit(solution)/shard_map/reduce_scatter | solution.py:226
  281.0 2.8 add_convert_fusion
  283.8 75.9 %all-reduce.14 = (f32[384]{0:T(512)}, f32[384]{0:T(512)}, f32[2,6,64]{2,1,0:T(8,128)S(1)}, f32[2,6,64]{2,1,0:T(8,128)S(1)}, f32[1536]{0:T(1024)}, /*index=5*/f32[384]{0:T(512)}) all-reduce(f32[384]{0:T(512)} %get-tuple-element.44, f32[384]{0:T(512)} %get-tuple-element.46, ...), channel_id=1, replica_groups=mesh['dp'=8,'space'=32] {'dp','space'}, use_global_device_ids=true, to_apply=%region_9.11 | all-reduce | flops 4224 | bytes 33792 | tf_op jit(solution)/shard_map/psum | solution.py:202
  360.9 65.6 %all-reduce.20.cloned.1.call-done = (f32[2,6,64,64]{3,2,1,0:T(8,128)}, f32[2,6,64,64]{3,2,1,0:T(8,128)}) async-done(((f32[2,6,64,64]{3,2,1,0:T(8,128)}, f32[2,6,64,64]{3,2,1,0:T(8,128)}), (f32[2,6,64,64]{3,2,1,0:T(8,128)}, f32[2,6,64,64]{3,2,1,0:T(8,128)})) %all-reduce.20.cloned.1.call-update) | async-done | bytes 393232 | tf_op jit(solution)/shard_map/psum | solution.py:202
  426.5 78.4 %all-reduce.22.cloned.1.call-done = (f32[384,48]{0,1:T(8,128)}, f32[48,384]{1,0:T(8,128)}) async-done(((f32[384,48]{0,1:T(8,128)}, f32[48,384]{1,0:T(8,128)}), (f32[384,48]{0,1:T(8,128)}, f32[48,384]{1,0:T(8,128)})) %all-reduce.22.cloned.1.call-update) | async-done | bytes 147472 | tf_op jit(solution)/shard_map/psum | solution.py:227
  504.9 1.8 copy.284
  506.7 1.8 copy.285
  (251 shorter events, 47.9 us)
Async XLA Ops:
  8.0 81.0 %copy-start = (bf16[384,1536]{1,0:T(8,128)(2,1)S(1)}, bf16[384,1536]{1,0:T(8,128)(2,1)}, u32[]{:S(2)}) copy-start(bf16[384,1536]{1,0:T(8,128)(2,1)} %param.22) | copy-start | bytes 3538948
  8.0 3.7 copy-start.4
  8.0 3.7 copy-start.48
  9.6 75.6 %copy-start.25 = (f32[32,32]{1,0:T(8,128)}, f32[32,32]{1,0:T(8,128)S(1)}, u32[]{:S(2)}) copy-start(f32[32,32]{1,0:T(8,128)S(1)} %broadcast_multiply_fusion.3) | copy-start | bytes 12292
  11.8 2.3 copy-start.30
  14.1 68.9 %copy-start.40 = (s32[16]{0:T(128)}, s32[16]{0:T(128)S(1)}, u32[]{:S(2)}) copy-start(s32[16]{0:T(128)S(1)} %pad_add_fusion.5) | copy-start | bytes 196
  15.9 12.0 %copy-start.54 = (f32[2,6,64]{2,0,1:T(2,128)S(1)}, f32[2,6,64]{2,0,1:T(2,128)}, u32[]{:S(2)}) copy-start(f32[2,6,64]{2,0,1:T(2,128)} %param.19) | copy-start | bytes 9220
  16.0 12.0 %copy-start.55 = (f32[2,6,64]{2,0,1:T(2,128)S(1)}, f32[2,6,64]{2,0,1:T(2,128)}, u32[]{:S(2)}) copy-start(f32[2,6,64]{2,0,1:T(2,128)} %param.21) | copy-start | bytes 9220
  17.3 27.0 %all-to-all-start = ((f32[2,1,1,128,384]{4,2,1,0,3:T(1,128)}), f32[2,1,1,128,384]{4,2,1,0,3:T(1,128)S(1)}, u32[]{:S(2)}, u32[]{:S(2)}) async-start(f32[2,1,1,128,384]{4,2,1,0,3:T(1,128)} %copy.112), calls=%async_computation | async-start | bytes 786432 | tf_op jit(solution)/shard_map/all_to_all | solution.py:144
  27.9 27.5 %copy-start.44 = (f32[1,6,64]{2,1,0:T(8,128)}, f32[1,6,64]{2,1,0:T(8,128)S(1)}, u32[]{:S(2)}) copy-start(f32[1,6,64]{2,1,0:T(8,128)S(1)} %copy.279) | copy-start | bytes 4612
  28.0 25.3 %copy-start.46 = (f32[1,6,64]{2,1,0:T(8,128)}, f32[1,6,64]{2,1,0:T(8,128)S(1)}, u32[]{:S(2)}) copy-start(f32[1,6,64]{2,1,0:T(8,128)S(1)} %copy.278) | copy-start | bytes 4612
  47.0 2.1 copy-start.10
  47.9 2.8 copy-start.6
  50.8 2.5 copy-start.12
  51.3 3.4 copy-start.15
  53.3 2.2 copy-start.13
  53.3 2.2 copy-start.20
  60.5 20.2 %all-to-all-start.1 = ((f32[2,1,32,4,384]{4,3,1,0,2:T(4,128)}), f32[2,1,32,4,384]{4,3,1,0,2:T(4,128)S(1)}, u32[]{:S(2)}, u32[]{:S(2)}) async-start(f32[2,1,32,4,384]{4,3,1,0,2:T(4,128)} %copy.127), calls=%async_computation.1 | async-start | bytes 786432 | tf_op jit(solution)/shard_map/all_to_all | solution.py:155
  64.4 123.9 %reduce-scatter.5.cloned.1.call-start = ((), (), s32[]{:S(2)}) async-start(), calls=%async_computation.7 | async-start | bytes 2433024 | tf_op jit(solution)/shard_map/reduce_scatter | solution.py:215
  64.7 17.7 %copy-start.56 = (f32[8]{0:T(128)}, f32[8]{0:T(128)S(1)}, u32[]{:S(2)}) copy-start(f32[8]{0:T(128)S(1)} %compare_select_fusion) | copy-start | bytes 100
  83.0 2.2 copy-start.31
  83.0 2.2 copy-start.49
  89.0 5.0 copy-start.24
  89.0 6.6 %copy-start.22 = (bf16[1,1,32,32,384]{4,3,2,1,0:T(8,128)(2,1)S(1)}, bf16[1,1,32,32,384]{4,3,2,1,0:T(8,128)(2,1)}, u32[]{:S(2)}) copy-start(bf16[1,1,32,32,384]{4,3,2,1,0:T(8,128)(2,1)} %param.26) | copy-start | bytes 2359300
  107.1 1.8 copy-start.61
  107.1 1.8 copy-start.52
  117.3 20.4 %all-to-all-start.2 = ((f32[2,1,1,128,384]{4,2,1,0,3:T(1,128)}), f32[2,1,1,128,384]{4,2,1,0,3:T(1,128)S(1)}, u32[]{:S(2)}, u32[]{:S(2)}) async-start(f32[2,1,1,128,384]{4,2,1,0,3:T(1,128)} %copy.140), calls=%async_computation.2 | async-start | bytes 786432 | tf_op jit(solution)/shard_map/all_to_all | solution.py:183
  121.3 159.7 %reduce-scatter.3.cloned.1.call-start = ((), (), s32[]{:S(2)}) async-start(), calls=%async_computation.6 | async-start | bytes 2433024 | tf_op jit(solution)/shard_map/reduce_scatter | solution.py:226
  140.7 1.9 copy-start.21
  142.6 2.8 copy-start.27
  156.9 6.5 %copy-start.28 = (f32[1,32,4,6,64]{4,1,2,3,0:T(8,128)S(1)}, f32[1,32,4,6,64]{4,1,2,3,0:T(8,128)}, u32[]{:S(2)}) copy-start(f32[1,32,4,6,64]{4,1,2,3,0:T(8,128)} %copy-done.27) | copy-start | bytes 589828
  156.9 21.1 %all-to-all-start.3 = ((f32[2,1,32,4,384]{4,3,1,0,2:T(4,128)}), f32[2,1,32,4,384]{4,3,1,0,2:T(4,128)S(1)}, u32[]{:S(2)}, u32[]{:S(2)}) async-start(f32[2,1,32,4,384]{4,3,1,0,2:T(4,128)} %copy.151), calls=%async_computation.3 | async-start | bytes 786432 | tf_op jit(solution)/shard_map/all_to_all | solution.py:196
  161.7 264.8 %all-reduce.20.cloned.1.call-start = ((), (), s32[]{:S(2)}) async-start(), calls=%async_computation.8 | async-start | bytes 1572864 | tf_op jit(solution)/shard_map/psum | solution.py:202
  163.5 2.6 copy-start.9
  165.2 2.5 copy-start.7
  168.5 2.0 copy-start.53
  168.5 2.6 copy-start.29
  169.3 2.1 copy-start.58
  170.2 334.7 %all-reduce.22.cloned.1.call-start = ((), (), s32[]{:S(2)}) async-start(), calls=%async_computation.9 | async-start | bytes 294912 | tf_op jit(solution)/shard_map/psum | solution.py:227
  180.2 2.9 copy-start.3
  180.2 2.9 copy-start.26
  180.2 2.9 copy-start.50
  183.1 2.1 copy-start.39
  183.1 3.2 copy-start.32
  185.2 2.5 copy-start.35
  281.0 228.7 %copy-start.1 = (bf16[384,1536]{1,0:T(8,128)(2,1)S(1)}, bf16[384,1536]{1,0:T(8,128)(2,1)}, u32[]{:S(2)}) copy-start(bf16[384,1536]{1,0:T(8,128)(2,1)} %param.22) | copy-start | bytes 3538948
  504.9 3.6 copy-start.43
  504.9 4.2 copy-start.42
  (23 other events, 26.6 us)
Sparse Core Ops, SparseCore 0:
  99.0 87.7 reduce-scatter.4
  190.7 90.2 reduce-scatter.2
Sparse Core Ops, SparseCore 1:
  170.3 256.1 all-reduce.19
  429.2 75.6 all-reduce.21
where the time goes:
time: 526 us; the launch traced here: 517 us
  waiting for transfers between devices  280 us (53%)
  matrix products  77.5 us (15%)
  blocking collectives  75.9 us (14%)
  local copies, waits for them, and re-layouts  25.2 us (5%)
  starting transfers between devices  23.9 us (5%)
  other arithmetic  17.3 us (3%)
  between operations  17.2 us (3%)
    reduce_scatter x1, waiting for transfers between devices, local(): lax.psum_scatter(up_term, 'space', scatter_dimension=1, tiled=True)  92.7 us
    psum x1, waiting for transfers between devices, local(): grad_up, grad_down = lax.psum((grad_up, grad_down), 'dp')  78.4 us
    psum x1, blocking collectives, local(): lax.psum((grad_gain_one, grad_gain_two, grad_fw_in, grad_fb_in, grad_fw_o...  75.9 us
    psum x1, waiting for transfers between devices, local(): lax.psum((grad_gain_one, grad_gain_two, grad_fw_in, grad_fb_in, grad_fw_o...  65.6 us
    all_to_all x1, waiting for transfers between devices, local(): lax.all_to_all(to_spectrum(normed, single_z), 'space', split_axis=3, conc...  16.3 us
    all_to_all x1, waiting for transfers between devices, local(): lax.all_to_all(inverse_x, 'space', split_axis=2, concat_axis=3, tiled=True)  16.1 us
    unnamed x136, local copies, waits for them, and re-layouts  12.4 us
    all_to_all x1, starting transfers between devices, local(): lax.all_to_all(to_spectrum(normed, single_z), 'space', split_axis=3, conc...  10.6 us
  transfers between devices with their start and end apart: 8, of which 7 were waited for; matrix products, arithmetic and copies ran while one was open for 13% of the time, Pallas kernels for 0%

commit v1 on v0

v1 whole, which is shorter than its diff:
```python
import functools
import math

import jax
import jax.numpy as jnp
import ml_dtypes
import numpy as np
from jax import lax
from jax.experimental import pallas as pl
from jax.experimental.pallas import tpu as pltpu
from jax.sharding import PartitionSpec as P

WIDTH = 384
BLOCKS = 6
BLOCK = 64
HIDDEN = 1536
GX = 32
GY = 32
GZ = 32
KEEP_Y = 16
KEEP_Z = 8
MODES = KEEP_Y * KEEP_Z
OWN = MODES // GX
TOKENS = GY * GZ
PAIRS = BLOCKS // 2
HBLOCK = 256
CHUNK = 256

EPSILON = 1e-05
SHRINK = 0.01
ROOT = math.sqrt(2.0 / math.pi)
CUBIC = 0.044715 * ROOT
VMEM = 60 * 1024 * 1024

BF16 = jnp.bfloat16
F32 = jnp.float32


def halves(table):
    high = table.astype(np.float32).astype(ml_dtypes.bfloat16)
    low = (table - high.astype(np.float64)).astype(np.float32).astype(ml_dtypes.bfloat16)
    return high, low


def slab_table():
    kept = np.concatenate([np.arange(KEEP_Y // 2), np.arange(GY - KEEP_Y // 2, GY)])
    ky, kz = np.repeat(kept, KEEP_Z), np.tile(np.arange(KEEP_Z), KEEP_Y)
    y, z = np.repeat(np.arange(GY), GZ), np.tile(np.arange(GZ), GY)
    steps = (ky[:, None] * y[None, :] * (GZ // math.gcd(GY, GZ)) + kz[:, None] * z[None, :] * (GY // math.gcd(GY, GZ))) % GY
    angle = 2.0 * np.pi * steps / GY
    both = np.stack([np.cos(angle), -np.sin(angle)]).reshape(2, GX, OWN, TOKENS)
    return both.transpose(1, 0, 2, 3).reshape(2 * MODES, TOKENS) / math.sqrt(TOKENS)


def cross_table():
    angle = 2.0 * np.pi * (np.outer(np.arange(GX), np.arange(GX)) % GX) / GX
    cos, sin = np.cos(angle), np.sin(angle)
    table = np.stack([np.stack([cos, sin], -1), np.stack([-sin, cos], -1)])
    full = np.einsum("rkxi,mn->rkmxin", table, np.eye(OWN))
    return full.reshape(2 * GX * OWN, GX * 2 * OWN) / math.sqrt(GX)


def dot(a, b):
    return jnp.dot(a, b, preferred_element_type=F32)


def dot_nt(a, b):
    return lax.dot_general(a, b, (((1,), (1,)), ((), ())), preferred_element_type=F32)


def dot_tn(a, b):
    return lax.dot_general(a, b, (((0,), (0,)), ((), ())), preferred_element_type=F32)


def split(value):
    high = value.astype(BF16)
    return high, (value - high.astype(F32)).astype(BF16)


def dot3(table_high, table_low, value):
    high, low = split(value)
    return dot(table_high, high) + (dot(table_low, high) + dot(table_high, low))


def dot6(a, b):
    return jnp.dot(a, b, preferred_element_type=F32, precision=lax.Precision.HIGHEST)


def normalise(values):
    center = values - jnp.mean(values, axis=-1, keepdims=True)
    rate = lax.rsqrt(jnp.mean(center * center, axis=-1, keepdims=True) + EPSILON)
    return center * rate, rate


def norm_back(grad, unit, rate):
    first = jnp.mean(grad, axis=-1, keepdims=True)
    second = jnp.mean(grad * unit, axis=-1, keepdims=True)
    return rate * (grad - first - unit * second)


def gelu_parts(value):
    square = value * value
    gate = 0.5 + 0.5 * jnp.tanh(value * (ROOT + CUBIC * square))
    active = value * gate
    slope = gate + (active - active * gate) * (2.0 * ROOT + (6.0 * CUBIC) * square)
    return active, slope


def gelu(value):
    return value * (0.5 + 0.5 * jnp.tanh(value * (ROOT + CUBIC * (value * value))))


def mode_weight(shape):
    place = lax.broadcasted_iota(jnp.int32, shape, 0) & (4 * OWN - 1)
    return jnp.where((place == 0) | (place == OWN), 1.0, 2.0).astype(F32)


def first_kernel(volume, table_high, table_low, out):
    unit, _ = normalise(volume[...].astype(F32))
    out[...] = dot3(table_high[...], table_low[...], unit)


def pair_of(value, pair):
    cut = slice(2 * BLOCK * pair, 2 * BLOCK * (pair + 1))
    return jnp.concatenate([value[: GX * OWN, cut], value[GX * OWN :, cut]], axis=1)


def filter_kernel(received, cross_high, cross_low, back_high, back_low, gain, w_in, b_in, w_out, b_out, sent, spectrum, inner, outer):
    unit_spectrum = dot3(cross_high[...], cross_low[...], received[...])
    spectrum[...] = unit_spectrum
    scaled = unit_spectrum * gain[...]
    real, imag = [], []
    for pair in range(PAIRS):
        before = dot6(pair_of(scaled, pair), w_in[pair]) + b_in[pair]
        inner[pair] = before
        after = dot6(gelu(before), w_out[pair]) + b_out[pair]
        outer[pair] = after
        shrunk = after - jnp.clip(after, -SHRINK, SHRINK)
        real.append(shrunk[:, : 2 * BLOCK])
        imag.append(shrunk[:, 2 * BLOCK :])
    filtered = jnp.concatenate([jnp.concatenate(real, axis=1), jnp.concatenate(imag, axis=1)], axis=0)
    sent[...] = dot3(back_high[...], back_low[...], filtered)


def packed_weight(grad):
    half = 2 * BLOCK
    real = grad[:half, :half] + grad[half:, half:]
    imag = grad[:half, half:] - grad[half:, :half]
    lane = lax.broadcasted_iota(jnp.int32, (BLOCK, half), 1)
    return [jnp.where(lane < BLOCK, part[:BLOCK], part[BLOCK:]) for part in (real, imag)]


def filter_back_kernel(received, cross_high, cross_low, back_high, back_low, gain, w_in, w_out, spectrum, inner, outer, sent, grad_w_in, grad_w_out, grad_b_in, grad_b_out, grad_gain):
    grad_spectrum = dot3(cross_high[...], cross_low[...], received[...])
    unit_spectrum = spectrum[...]
    scaled = unit_spectrum * gain[...]
    real, imag = [], []
    for pair in range(PAIRS):
        after = outer[pair]
        grad_out = jnp.where(jnp.abs(after) > SHRINK, pair_of(grad_spectrum, pair), 0.0)
        active, slope = gelu_parts(inner[pair])
        grad_b_out[pair] = jnp.sum(grad_out, axis=0, keepdims=True)
        grad_out = grad_out.astype(BF16)
        grad_w_out[pair, 0], grad_w_out[pair, 1] = packed_weight(dot_tn(active.astype(BF16), grad_out))
        grad_in = dot_nt(grad_out, w_out[pair].astype(BF16)) * slope
        grad_b_in[pair] = jnp.sum(grad_in, axis=0, keepdims=True)
        grad_in = grad_in.astype(BF16)
        grad_w_in[pair, 0], grad_w_in[pair, 1] = packed_weight(dot_tn(pair_of(scaled, pair).astype(BF16), grad_in))
        grad_part = dot_nt(grad_in, w_in[pair].astype(BF16))
        real.append(grad_part[:, : 2 * BLOCK])
        imag.append(grad_part[:, 2 * BLOCK :])
    grad = jnp.concatenate([jnp.concatenate(real, axis=1), jnp.concatenate(imag, axis=1)], axis=0)
    grad_gain[...] = jnp.sum(grad * unit_spectrum, axis=0, keepdims=True)
    sent[...] = dot3(back_high[...], back_low[...], grad)


def mlp_kernel(volume, cotangent, modes, table, table_turned, gain_one, gain_two, up, up_bias, down, down_bias,
               result, grad_mixed, sent, grad_weights, grad_up_bias, sums,
               mixed, unit_one, unit_two, rate_two, inputs, inputs_turned, cotangent_turned, total, grad_inputs):
    step = pl.program_id(0)

    @pl.when(step == 0)
    def _():
        weighted = (modes[...] * mode_weight((2 * MODES, 1))).astype(BF16)
        for at in range(0, TOKENS, CHUNK):
            rows = pl.ds(at, CHUNK)
            wide = volume[rows, :].astype(F32)
            unit, _ = normalise(wide)
            unit_one[rows, :] = unit
            here = wide + dot(table_turned[rows, :], weighted) + unit * gain_one[...]
            mixed[rows, :] = here
            unit, rate = normalise(here)
            unit_two[rows, :] = unit
            rate_two[rows, :] = rate
            rounded = (unit * gain_two[...]).astype(BF16)
            inputs[rows, :] = rounded
            inputs_turned[:, rows] = rounded.T
            cotangent_turned[:, rows] = cotangent[rows, :].T

    hidden_parts, before_parts = [], []
    for at in range(0, TOKENS, CHUNK):
        rows = pl.ds(at, CHUNK)
        before = dot(inputs[rows, :], up[...]) + up_bias[...]
        grad_hidden = dot_nt(cotangent[rows, :], down[...])
        active, slope = gelu_parts(before)
        hidden = active.astype(BF16)
        grad_before = (grad_hidden * slope).astype(BF16)
        hidden_parts.append(hidden)
        before_parts.append(grad_before)
        part = dot(hidden, down[...])
        grad_part = dot_nt(grad_before, up[...])

        @pl.when(step == 0)
        def _():
            total[rows, :] = part
            grad_inputs[rows, :] = grad_part

        @pl.when(step > 0)
        def _():
            total[rows, :] += part
            grad_inputs[rows, :] += grad_part

    hidden = jnp.concatenate(hidden_parts, axis=0)
    grad_before = jnp.concatenate(before_parts, axis=0)
    grad_up_bias[...] = jnp.sum(grad_before.astype(F32), axis=0, keepdims=True)
    grad_weights[:, :WIDTH] = dot(inputs_turned[...], grad_before).T
    grad_weights[:, WIDTH:] = dot(cotangent_turned[...], hidden).T

    @pl.when(step == HIDDEN // HBLOCK - 1)
    def _():
        gain_sum = jnp.zeros((1, WIDTH), F32)
        one_sum = jnp.zeros((1, WIDTH), F32)
        down_sum = jnp.zeros((1, WIDTH), F32)
        spectrum = jnp.zeros((2 * MODES, WIDTH), F32)
        for at in range(0, TOKENS, CHUNK):
            rows = pl.ds(at, CHUNK)
            result[rows, :] = (mixed[rows, :] + total[rows, :] + down_bias[...]).astype(BF16)
            grad = grad_inputs[rows, :]
            unit = unit_two[rows, :]
            gain_sum += jnp.sum(grad * unit, axis=0, keepdims=True)
            upstream = cotangent[rows, :].astype(F32)
            down_sum += jnp.sum(upstream, axis=0, keepdims=True)
            here = upstream + norm_back(grad * gain_two[...], unit, rate_two[rows, :])
            one_sum += jnp.sum(here * unit_one[rows, :], axis=0, keepdims=True)
            grad_mixed[rows, :] = here
            spectrum += dot(table[:, rows], here.astype(BF16))
        sent[...] = spectrum * mode_weight((2 * MODES, 1))
        sums[0:1, :] = gain_sum
        sums[1:2, :] = one_sum
        sums[2:3, :] = down_sum


def last_kernel(volume, modes, table_turned, gain_one, grad_mixed, out):
    rounded = modes[...].astype(BF16)
    for at in range(0, TOKENS, CHUNK):
        rows = pl.ds(at, CHUNK)
        unit, rate = normalise(volume[rows, :].astype(F32))
        here = grad_mixed[rows, :]
        grad = dot(table_turned[rows, :], rounded) + here
        out[rows, :] = (here + norm_back(grad * gain_one[...], unit, rate)).astype(BF16)


def call(kernel, out, *operands):
    return pl.pallas_call(
        kernel,
        out_shape=out,
        compiler_params=pltpu.CompilerParams(vmem_limit_bytes=VMEM),
    )(*operands)


def exchange(value):
    out = lax.all_to_all(value.reshape(GX, 2 * OWN, WIDTH), "space", split_axis=0, concat_axis=0, tiled=True)
    return out.reshape(2 * MODES, WIDTH)


def paired(weight):
    zero = jnp.zeros((PAIRS, BLOCK, BLOCK), F32)
    even, odd = weight[:, 0::2], weight[:, 1::2]

    def wide(index):
        top = jnp.concatenate([even[index], zero], axis=2)
        return jnp.concatenate([top, jnp.concatenate([zero, odd[index]], axis=2)], axis=1)

    real, imag = wide(0), wide(1)
    return jnp.concatenate([jnp.concatenate([real, imag], axis=2), jnp.concatenate([-imag, real], axis=2)], axis=1)


def paired_bias(bias):
    return bias.reshape(2, PAIRS, 2 * BLOCK).transpose(1, 0, 2).reshape(PAIRS, 1, 4 * BLOCK)


def unpaired(grad):
    return grad.reshape(PAIRS, 2, BLOCK, 2, BLOCK).transpose(1, 0, 3, 2, 4).reshape(2, BLOCKS, BLOCK, BLOCK)


def unpaired_bias(grad):
    return grad.reshape(PAIRS, 2, 2, BLOCK).transpose(1, 0, 2, 3).reshape(2, BLOCKS, BLOCK)


def local(volume, gain_one, gain_two, w_in, b_in, w_out, b_out, up, up_bias, down, down_bias, cotangent):
    shape = volume.shape
    volume = volume.reshape(TOKENS, WIDTH)
    cotangent = cotangent.reshape(TOKENS, WIDTH)
    gain_one, gain_two, down_bias = (value.reshape(1, WIDTH) for value in (gain_one, gain_two, down_bias))
    slab = slab_table()
    slab_high, slab_low = (jnp.asarray(part) for part in halves(slab))
    slab_turned = jnp.asarray(halves(slab.T)[0])
    cross = cross_table()
    cross_high, cross_low = (jnp.asarray(part) for part in halves(cross))
    back_high, back_low = (jnp.asarray(part) for part in halves(cross.T))
    w_in, w_out, b_in, b_out = paired(w_in), paired(w_out), paired_bias(b_in), paired_bias(b_out)

    def sds(*dims, dtype=F32):
        return jax.ShapeDtypeStruct(dims, dtype)

    modes = call(first_kernel, sds(2 * MODES, WIDTH), volume, slab_high, slab_low)
    modes = exchange(modes)
    wide = sds(PAIRS, GX * OWN, 4 * BLOCK)
    modes, spectrum, inner, outer = call(
        filter_kernel,
        (sds(2 * MODES, WIDTH), sds(2 * MODES, WIDTH), wide, wide),
        modes, cross_high, cross_low, back_high, back_low, gain_one, w_in, b_in, w_out, b_out,
    )
    modes = exchange(modes)

    def whole(*dims):
        return pl.BlockSpec(dims, lambda step: (0,) * len(dims))

    steps = HIDDEN // HBLOCK
    result, grad_mixed, modes, grad_weights, grad_up_bias, sums = pl.pallas_call(
        mlp_kernel,
        grid=(steps,),
        in_specs=[
            whole(TOKENS, WIDTH), whole(TOKENS, WIDTH), whole(2 * MODES, WIDTH), whole(2 * MODES, TOKENS), whole(TOKENS, 2 * MODES),
            whole(1, WIDTH), whole(1, WIDTH),
            pl.BlockSpec((WIDTH, HBLOCK), lambda step: (0, step)),
            pl.BlockSpec((1, HBLOCK), lambda step: (0, step)),
            pl.BlockSpec((HBLOCK, WIDTH), lambda step: (step, 0)),
            whole(1, WIDTH),
        ],
        out_specs=(
            whole(TOKENS, WIDTH), whole(TOKENS, WIDTH), whole(2 * MODES, WIDTH),
            pl.BlockSpec((HBLOCK, 2 * WIDTH), lambda step: (step, 0)),
            pl.BlockSpec((1, HBLOCK), lambda step: (0, step)),
            whole(8, WIDTH),
        ),
        out_shape=(
            sds(TOKENS, WIDTH, dtype=BF16), sds(TOKENS, WIDTH), sds(2 * MODES, WIDTH),
            sds(HIDDEN, 2 * WIDTH), sds(1, HIDDEN), sds(8, WIDTH),
        ),
        scratch_shapes=[
            pltpu.VMEM((TOKENS, WIDTH), F32), pltpu.VMEM((TOKENS, WIDTH), F32), pltpu.VMEM((TOKENS, WIDTH), F32),
            pltpu.VMEM((TOKENS, 1), F32), pltpu.VMEM((TOKENS, WIDTH), BF16),
            pltpu.VMEM((WIDTH, TOKENS), BF16), pltpu.VMEM((WIDTH, TOKENS), BF16),
            pltpu.VMEM((TOKENS, WIDTH), F32), pltpu.VMEM((TOKENS, WIDTH), F32),
        ],
        compiler_params=pltpu.CompilerParams(vmem_limit_bytes=VMEM),
    )(volume, cotangent, modes, slab_high, slab_turned, gain_one, gain_two, up, up_bias.reshape(1, HIDDEN), down, down_bias)

    grad_weights = lax.psum_scatter(grad_weights, "space", scatter_dimension=0, tiled=True)
    modes = exchange(modes)
    packed = sds(PAIRS, 2, BLOCK, 2 * BLOCK)
    row = sds(PAIRS, 1, 4 * BLOCK)
    modes, grad_w_in, grad_w_out, grad_b_in, grad_b_out, grad_gain = call(
        filter_back_kernel,
        (sds(2 * MODES, WIDTH), packed, packed, row, row, sds(1, WIDTH)),
        modes, cross_high, cross_low, back_high, back_low, gain_one, w_in, w_out, spectrum, inner, outer,
    )
    modes = exchange(modes)
    grad_volume = call(last_kernel, sds(TOKENS, WIDTH, dtype=BF16), volume, modes, slab_turned, gain_one, grad_mixed)
    grad_weights = lax.psum(grad_weights, "dp")
    summed = lax.psum(
        (grad_w_in, grad_w_out, grad_b_in, grad_b_out, grad_gain[0] + sums[1], sums[0], sums[2], grad_up_bias[0]), ("dp", "space")
    )
    return (
        result.reshape(shape),
        grad_volume.reshape(shape),
        summed[4],
        summed[5],
        unpaired(summed[0]),
        unpaired_bias(summed[2]),
        unpaired(summed[1]),
        unpaired_bias(summed[3]),
        grad_weights[:, :WIDTH].T,
        summed[7],
        grad_weights[:, WIDTH:],
        summed[6],
    )


def solution(mesh):
    field = P("dp", "space", None, None, None)
    return jax.shard_map(
        local,
        mesh=mesh,
        in_specs=(field,) + (P(),) * 10 + (field,),
        out_specs=(field, field) + (P(),) * 6 + (P(None, "space"), P(), P("space", None), P()),
        check_vma=False,
    )
```

time: 526 us -> 538 us (1.023)
  matrix products: 77.5 us -> 0 us
  waiting for transfers between devices: 280 us -> 342 us
  Pallas kernels: 0 us -> 43.5 us
  blocking collectives: 75.9 us -> 96.4 us
  other arithmetic: 17.3 us -> 4.2 us
  local copies, waits for them, and re-layouts: 25.2 us -> 15.6 us
    psum x2, waiting for transfers between devices: 144 us -> 248 us  [the longest x1 248 us: local(): lax.psum((grad_w_in, grad_w_out, grad_b_in, grad_b_out, grad_gain[0] + su...]
    dot_general x70 -> x0, matrix products: 77.5 us -> none  [the longest x16 8.22 us: apply_table(): return jnp.einsum('kx,bxmc->bkmc', table, part, precision=PRECISE)]
    pallas_call x0 -> x5, Pallas kernels: none -> 43.5 us  [the longest x1 27 us: local(): pl.pallas_call(mlp_kernel, grid=(steps,), in_specs=[whole(TOKENS, WIDTH),...]
    reduce_scatter x2 -> x1, waiting for transfers between devices: 92.7 us -> 67.6 us  [local(): lax.psum_scatter(grad_weights, 'space', scatter_dimension=0, tiled=True)]
    all_to_all x0 -> x1, blocking collectives: none -> 20 us  [exchange(): lax.all_to_all(value.reshape(GX, 2 * OWN, WIDTH), 'space', split_axis=0,...]
    all_to_all x4 -> x3, waiting for transfers between devices: 43.6 us -> 26.5 us  [exchange(): lax.all_to_all(value.reshape(GX, 2 * OWN, WIDTH), 'space', split_axis=0,...]
    reduce_sum x9 -> x0, other arithmetic: 9.27 us -> none  [the longest x3 3.16 us: layer_norm(): return center * lax.rsqrt(spread + EPSILON) * gain]
    another operation x19 -> x0, local copies, waits for them, and re-layouts: 7.68 us -> none
  transfers between devices with their start and end apart: 8 -> 6, of which waited for: 7 -> 4; matrix products, arithmetic and copies ran while one was open for 13% -> 2% of each run, Pallas kernels for 0% -> 2%
where the time goes in v1:
time: 538 us; the launch traced here: 534 us
  waiting for transfers between devices  342 us (64%)
  blocking collectives  96.4 us (18%)
  Pallas kernels  43.5 us (8%)
  starting transfers between devices  18.6 us (3%)
  local copies, waits for them, and re-layouts  15.6 us (3%)
  between operations  14 us (3%)
    psum x1, waiting for transfers between devices, local(): lax.psum((grad_w_in, grad_w_out, grad_b_in, grad_b_out, grad_gain[0] + su...  248 us
    psum x1, blocking collectives, local(): lax.psum((grad_w_in, grad_w_out, grad_b_in, grad_b_out, grad_gain[0] + su...  76.4 us
    reduce_scatter x1, waiting for transfers between devices, local(): lax.psum_scatter(grad_weights, 'space', scatter_dimension=0, tiled=True)  67.6 us
    pallas_call x1, Pallas kernels, local(): pl.pallas_call(mlp_kernel, grid=(steps,), in_specs=[whole(TOKENS, WIDTH),...  27 us
    all_to_all x3, waiting for transfers between devices, exchange(): lax.all_to_all(value.reshape(GX, 2 * OWN, WIDTH), 'space', split_axis=0,...  26.5 us
    all_to_all x1, blocking collectives, exchange(): lax.all_to_all(value.reshape(GX, 2 * OWN, WIDTH), 'space', split_axis=0,...  20 us
    all_to_all x3, starting transfers between devices, exchange(): lax.all_to_all(value.reshape(GX, 2 * OWN, WIDTH), 'space', split_axis=0,...  18.5 us
    pallas_call x4, Pallas kernels, call(): pl.pallas_call(kernel, out_shape=out, compiler_params=pltpu.CompilerParam...  16.5 us
  transfers between devices with their start and end apart: 6, of which 4 were waited for; matrix products, arithmetic and copies ran while one was open for 2% of the time, Pallas kernels for 2%

profile of v1, /device:TPU:32, one launch (start us, length us, event | category | flops | bytes accessed | tf_op | source)
XLA Modules:
  0.0 534.2 jit_solution(15200512333876108472)
XLA Ops:
  7.2 3.8 shard_map.274
  11.0 10.5 %all-to-all-start = ((f32[32,8,384]{2,1,0:T(8,128)}), f32[32,8,384]{2,1,0:T(8,128)S(1)}, u32[]{:S(2)}, u32[]{:S(2)}) async-start(f32[32,8,384]{2,1,0:T(8,128)} %bitcast.56), calls=%async_computation | async-start | bytes 786432 | tf_op jit(solution)/shard_map/all_to_all | solution.py:272
  21.7 0.6 reshape.113.gain.gain_one
  22.2 0.1 reshape.114
  22.3 0.6 copy.36
  22.9 0.1 reshape.116
  23.0 0.6 copy.38
  23.6 0.1 concatenate.58
  23.7 0.1 concatenate.55
  23.8 0.1 concatenate.67
  23.9 0.1 concatenate.64
  24.1 0.9 maximum_maximum_fusion.w_in
  25.0 1.0 maximum_maximum_fusion.1.w_out
  26.0 11.9 %all-to-all-done = f32[32,8,384]{2,1,0:T(8,128)S(1)} async-done(((f32[32,8,384]{2,1,0:T(8,128)}), f32[32,8,384]{2,1,0:T(8,128)S(1)}, u32[]{:S(2)}, u32[]{:S(2)}) %all-to-all-start) | async-done | bytes 393248 | tf_op jit(solution)/shard_map/all_to_all | solution.py:272
  37.9 0.7 copy-done.2
  38.6 4.4 shard_map.275
  43.0 3.9 all-to-all-start.1
  46.9 0.0 reduce-scatter.2.cloned.1.call-start
  47.0 0.6 reshape.120.gain_two
  47.6 0.6 reshape.122.down_bias
  48.1 0.6 reshape.121.up_bias
  48.7 14.6 %all-to-all-done.1 = f32[32,8,384]{2,1,0:T(8,128)S(1)} async-done(((f32[32,8,384]{2,1,0:T(8,128)}), f32[32,8,384]{2,1,0:T(8,128)S(1)}, u32[]{:S(2)}, u32[]{:S(2)}) %all-to-all-start.1) | async-done | bytes 393248 | tf_op jit(solution)/shard_map/all_to_all | solution.py:272
  63.3 0.7 copy-done.1
  64.1 27.0 %shard_map.276 = (bf16[1024,384]{1,0:T(8,128)(2,1)}, f32[1024,384]{1,0:T(8,128)}, f32[256,384]{1,0:T(8,128)}, f32[1536,768]{1,0:T(8,128)}, f32[1,1536]{1,0:T(1,128)}, /*index=5*/f32[8,384]{1,0:T(8,128)}) custom-call(bf16[1024,384]{1,0:T(8,128)(2,1)} %bitcast.47, bf16[1024,384]{1,0:T(8,128)(2,1)} %bitcast.58, f32[256,384]{1,0:T(8,128)} %bitcast.52, ...), custom_call_target="tpu_custom_call" | custom-call | tf_op jit(solution)/shard_map/pallas_call | solution.py:330
  91.0 0.0 reduce-scatter.2.cloned.1.call-update
  91.1 1.0 copy-done.5
  92.0 20.0 %all_to_all.20 = f32[32,8,384]{2,1,0:T(8,128)} all-to-all(f32[32,8,384]{2,1,0:T(8,128)S(1)} %bitcast.61), channel_id=1, replica_groups=mesh['dp'=8,'space'=32] {'space'}, dimensions={0} | all-to-all | bytes 786432 | tf_op jit(solution)/shard_map/all_to_all | solution.py:272
  112.0 4.3 shard_map.277
  116.4 4.0 all-to-all-start.3
  120.4 0.0 all-reduce.13.cloned.1.call-start
  120.4 67.6 %reduce-scatter.2.cloned.1.call-done = f32[48,768]{1,0:T(8,128)} async-done(((f32[1536,768]{1,0:T(8,128)}), f32[48,768]{1,0:T(8,128)}) %reduce-scatter.2.cloned.1.call-update) | async-done | bytes 147472 | tf_op jit(solution)/shard_map/reduce_scatter | solution.py:360
  188.1 0.0 all-reduce.15.cloned.1.call-start
  188.2 0.7 reduce.2
  188.9 0.7 reduce.3
  189.6 0.1 reshape.135
  189.7 0.1 reshape.131
  189.8 1.2 reshape.129
  191.0 0.8 copy.39
  191.7 0.2 reshape.133
  192.0 0.8 copy.41
  192.8 0.8 slice_reduce_fusion
  193.7 76.4 %all-reduce.8 = (f32[384]{0:T(512)}, f32[384]{0:T(512)}, f32[2,6,64]{2,0,1:T(2,128)}, f32[2,6,64]{2,0,1:T(2,128)}, f32[1536]{0:T(1024)}, /*index=5*/f32[384]{0:T(512)}) all-reduce(f32[384]{0:T(512)S(1)} %get-tuple-element.46, f32[384]{0:T(512)S(1)} %get-tuple-element.45, ...), channel_id=1, replica_groups=mesh['dp'=8,'space'=32] {'dp','space'}, use_global_device_ids=true, to_apply=%region_0.0 | all-reduce | flops 4224 | bytes 33792 | tf_op jit(solution)/shard_map/psum | solution.py:372
  270.0 0.7 copy-done
  270.8 4.0 shard_map.278
  274.8 1.6 fusion.2
  276.4 247.7 %all-reduce.15.cloned.1.call-done = (f32[2,6,64,64]{3,2,1,0:T(8,128)}, f32[2,6,64,64]{3,2,1,0:T(8,128)}) async-done(((f32[2,6,64,64]{3,2,1,0:T(8,128)}, f32[2,6,64,64]{3,2,1,0:T(8,128)}), (f32[2,6,64,64]{3,2,1,0:T(8,128)}, f32[2,6,64,64]{3,2,1,0:T(8,128)})) %all-reduce.15.cloned.1.call-update) | async-done | bytes 393232 | tf_op jit(solution)/shard_map/psum | solution.py:372
  524.1 1.8 copy.46
  525.9 1.8 copy.47
  (45 shorter events, 0.3 us)
Async XLA Ops:
  7.2 14.4 %copy-start.3 = (f32[2,6,64,64]{3,2,1,0:T(8,128)S(1)}, f32[2,6,64,64]{3,2,1,0:T(8,128)}, u32[]{:S(2)}) copy-start(f32[2,6,64,64]{3,2,1,0:T(8,128)} %param.22) | copy-start | bytes 589828
  7.2 14.4 %copy-start.4 = (f32[2,6,64,64]{3,2,1,0:T(8,128)S(1)}, f32[2,6,64,64]{3,2,1,0:T(8,128)}, u32[]{:S(2)}) copy-start(f32[2,6,64,64]{3,2,1,0:T(8,128)} %param.24) | copy-start | bytes 589828
  11.0 10.7 %copy-start.11 = (f32[384]{0:T(512)S(1)}, f32[384]{0:T(512)}, u32[]{:S(2)}) copy-start(f32[384]{0:T(512)} %param.20) | copy-start | bytes 4612
  11.0 11.3 %copy-start.8 = (f32[2,6,64]{2,0,1:T(2,128)S(1)}, f32[2,6,64]{2,0,1:T(2,128)}, u32[]{:S(2)}) copy-start(f32[2,6,64]{2,0,1:T(2,128)} %param.23) | copy-start | bytes 9220
  11.0 11.9 %copy-start.9 = (f32[2,6,64]{2,0,1:T(2,128)S(1)}, f32[2,6,64]{2,0,1:T(2,128)}, u32[]{:S(2)}) copy-start(f32[2,6,64]{2,0,1:T(2,128)} %param.25) | copy-start | bytes 9220
  11.0 26.9 %all-to-all-start = ((f32[32,8,384]{2,1,0:T(8,128)}), f32[32,8,384]{2,1,0:T(8,128)S(1)}, u32[]{:S(2)}, u32[]{:S(2)}) async-start(f32[32,8,384]{2,1,0:T(8,128)} %bitcast.56), calls=%async_computation | async-start | bytes 786432 | tf_op jit(solution)/shard_map/all_to_all | solution.py:272
  37.9 0.7 copy-start.2
  38.6 8.3 %copy-start.12 = (f32[384]{0:T(512)S(1)}, f32[384]{0:T(512)}, u32[]{:S(2)}) copy-start(f32[384]{0:T(512)} %param.21) | copy-start | bytes 4612
  38.6 8.9 %copy-start.13 = (f32[384]{0:T(512)S(1)}, f32[384]{0:T(512)}, u32[]{:S(2)}) copy-start(f32[384]{0:T(512)} %param.29) | copy-start | bytes 4612
  38.6 9.5 %copy-start.7 = (f32[1536]{0:T(1024)S(1)}, f32[1536]{0:T(1024)}, u32[]{:S(2)}) copy-start(f32[1536]{0:T(1024)} %param.27) | copy-start | bytes 18436
  43.0 20.3 %all-to-all-start.1 = ((f32[32,8,384]{2,1,0:T(8,128)}), f32[32,8,384]{2,1,0:T(8,128)S(1)}, u32[]{:S(2)}, u32[]{:S(2)}) async-start(f32[32,8,384]{2,1,0:T(8,128)} %bitcast.62), calls=%async_computation.1 | async-start | bytes 786432 | tf_op jit(solution)/shard_map/all_to_all | solution.py:272
  46.9 141.1 %reduce-scatter.2.cloned.1.call-start = ((), (), s32[]{:S(2)}) async-start(), calls=%async_computation.5 | async-start | bytes 4866048 | tf_op jit(solution)/shard_map/reduce_scatter | solution.py:360
  63.3 0.7 copy-start.1
  91.0 1.0 copy-start.5
  112.0 76.1 %copy-start.10 = (f32[1,1536]{1,0:T(1,128)S(1)}, f32[1,1536]{1,0:T(1,128)}, u32[]{:S(2)}) copy-start(f32[1,1536]{1,0:T(1,128)} %get-tuple-element.43) | copy-start | bytes 18436
  116.4 75.4 %copy-start.6 = (f32[3,2,64,128]{3,2,1,0:T(8,128)S(1)}, f32[3,2,64,128]{3,2,1,0:T(8,128)}, u32[]{:S(2)}) copy-start(f32[3,2,64,128]{3,2,1,0:T(8,128)} %get-tuple-element.40) | copy-start | bytes 589828
  116.4 153.7 %all-to-all-start.3 = ((f32[32,8,384]{2,1,0:T(8,128)}), f32[32,8,384]{2,1,0:T(8,128)S(1)}, u32[]{:S(2)}, u32[]{:S(2)}) async-start(f32[32,8,384]{2,1,0:T(8,128)} %bitcast.60), calls=%async_computation.3 | async-start | bytes 786432 | tf_op jit(solution)/shard_map/all_to_all | solution.py:272
  120.4 154.4 %all-reduce.13.cloned.1.call-start = ((), (), s32[]{:S(2)}) async-start(), calls=%async_computation.6 | async-start | bytes 294912 | tf_op jit(solution)/shard_map/psum | solution.py:371
  188.1 336.0 %all-reduce.15.cloned.1.call-start = ((), (), s32[]{:S(2)}) async-start(), calls=%async_computation.7 | async-start | bytes 1572864 | tf_op jit(solution)/shard_map/psum | solution.py:372
  190.9 1.9 copy-start.14
  270.0 0.7 copy-start
Sparse Core Ops, SparseCore 0:
  91.2 96.8 reduce-scatter.1
  190.9 73.5 all-reduce.12
  270.7 253.3 all-reduce.14

commit v2 on v1

v2 whole, which is shorter than its diff:
```python
import functools
import math

import jax
import jax.numpy as jnp
import ml_dtypes
import numpy as np
from jax import lax
from jax.experimental import pallas as pl
from jax.experimental.pallas import tpu as pltpu
from jax.sharding import PartitionSpec as P

WIDTH = 384
BLOCKS = 6
BLOCK = 64
HIDDEN = 1536
GX = 32
GY = 32
GZ = 32
KEEP_Y = 16
KEEP_Z = 8
MODES = KEEP_Y * KEEP_Z
OWN = MODES // GX
TOKENS = GY * GZ
PAIRS = BLOCKS // 2
HBLOCK = 256
CHUNK = 256

Y_CORE = [
    [(y * 2 + low) * GX + place * 2 + core for y in range(4) for core in range(2)] for low in range(2) for place in range(GX // 2)
]
X_Z = [[place * 2 + core for place in range(GX // 2)] for core in range(2)]

EPSILON = 1e-05
SHRINK = 0.01
ROOT = math.sqrt(2.0 / math.pi)
CUBIC = 0.044715 * ROOT
MIB = 1024 * 1024

BF16 = jnp.bfloat16
F32 = jnp.float32


def halves(table):
    high = table.astype(np.float32).astype(ml_dtypes.bfloat16)
    low = (table - high.astype(np.float64)).astype(np.float32).astype(ml_dtypes.bfloat16)
    return high, low


def slab_table():
    kept = np.concatenate([np.arange(KEEP_Y // 2), np.arange(GY - KEEP_Y // 2, GY)])
    ky, kz = np.repeat(kept, KEEP_Z), np.tile(np.arange(KEEP_Z), KEEP_Y)
    y, z = np.repeat(np.arange(GY), GZ), np.tile(np.arange(GZ), GY)
    steps = (ky[:, None] * y[None, :] * (GZ // math.gcd(GY, GZ)) + kz[:, None] * z[None, :] * (GY // math.gcd(GY, GZ))) % GY
    angle = 2.0 * np.pi * steps / GY
    both = np.stack([np.cos(angle), -np.sin(angle)]).reshape(2, GX, OWN, TOKENS)
    return both.transpose(1, 0, 2, 3).reshape(2 * MODES, TOKENS) / math.sqrt(TOKENS)


def cross_table():
    angle = 2.0 * np.pi * (np.outer(np.arange(GX), np.arange(GX)) % GX) / GX
    cos, sin = np.cos(angle), np.sin(angle)
    table = np.stack([np.stack([cos, sin], -1), np.stack([-sin, cos], -1)])
    full = np.einsum("rkxi,mn->rkmxin", table, np.eye(OWN))
    return full.reshape(2 * GX * OWN, GX * 2 * OWN) / math.sqrt(GX)


def dot(a, b):
    return jnp.dot(a, b, preferred_element_type=F32)


def dot_nt(a, b):
    return lax.dot_general(a, b, (((1,), (1,)), ((), ())), preferred_element_type=F32)


def dot_tn(a, b):
    return lax.dot_general(a, b, (((0,), (0,)), ((), ())), preferred_element_type=F32)


def split(value):
    high = value.astype(BF16)
    return high, (value - high.astype(F32)).astype(BF16)


def dot3(table_high, table_low, value):
    high, low = split(value)
    return dot(table_high, high) + (dot(table_low, high) + dot(table_high, low))


def dot6(a, b):
    return jnp.dot(a, b, preferred_element_type=F32, precision=lax.Precision.HIGHEST)


def normalise(values):
    center = values - jnp.mean(values, axis=-1, keepdims=True)
    rate = lax.rsqrt(jnp.mean(center * center, axis=-1, keepdims=True) + EPSILON)
    return center * rate, rate


def norm_back(grad, unit, rate):
    first = jnp.mean(grad, axis=-1, keepdims=True)
    second = jnp.mean(grad * unit, axis=-1, keepdims=True)
    return rate * (grad - first - unit * second)


def gelu_parts(value):
    square = value * value
    gate = 0.5 + 0.5 * jnp.tanh(value * (ROOT + CUBIC * square))
    active = value * gate
    slope = gate + (active - active * gate) * (2.0 * ROOT + (6.0 * CUBIC) * square)
    return active, slope


def gelu(value):
    return value * (0.5 + 0.5 * jnp.tanh(value * (ROOT + CUBIC * (value * value))))


def mode_weight(shape):
    place = lax.broadcasted_iota(jnp.int32, shape, 0) & (4 * OWN - 1)
    return jnp.where((place == 0) | (place == OWN), 1.0, 2.0).astype(F32)


def first_kernel(volume, table_high, table_low, out):
    unit, _ = normalise(volume[...].astype(F32))
    out[...] = dot3(table_high[...], table_low[...], unit)


def pair_of(value, pair):
    cut = slice(2 * BLOCK * pair, 2 * BLOCK * (pair + 1))
    return jnp.concatenate([value[: GX * OWN, cut], value[GX * OWN :, cut]], axis=1)


def filter_kernel(received, cross_high, cross_low, back_high, back_low, gain, w_in, b_in, w_out, b_out, sent, spectrum, inner, outer):
    unit_spectrum = dot3(cross_high[...], cross_low[...], received[...])
    spectrum[...] = unit_spectrum
    scaled = unit_spectrum * gain[...]
    real, imag = [], []
    for pair in range(PAIRS):
        before = dot6(pair_of(scaled, pair), w_in[pair]) + b_in[pair]
        inner[pair] = before
        after = dot6(gelu(before), w_out[pair]) + b_out[pair]
        outer[pair] = after
        shrunk = after - jnp.clip(after, -SHRINK, SHRINK)
        real.append(shrunk[:, : 2 * BLOCK])
        imag.append(shrunk[:, 2 * BLOCK :])
    filtered = jnp.concatenate([jnp.concatenate(real, axis=1), jnp.concatenate(imag, axis=1)], axis=0)
    sent[...] = dot3(back_high[...], back_low[...], filtered)


def packed_weight(grad):
    half = 2 * BLOCK
    real = grad[:half, :half] + grad[half:, half:]
    imag = grad[:half, half:] - grad[half:, :half]
    lane = lax.broadcasted_iota(jnp.int32, (BLOCK, half), 1)
    return [jnp.where(lane < BLOCK, part[:BLOCK], part[BLOCK:]) for part in (real, imag)]


SMALL = 40


def filter_back_kernel(received, cross_high, cross_low, back_high, back_low, gain, w_in, w_out, spectrum, inner, outer, sums, up_sum, sent, small):
    half = 2 * BLOCK
    grad_spectrum = dot3(cross_high[...], cross_low[...], received[...])
    unit_spectrum = spectrum[...]
    scaled = unit_spectrum * gain[...]
    real, imag, weights = [], [], [[], []]
    small[...] = jnp.zeros((GX * 8, half), F32)
    for pair in range(PAIRS):
        after = outer[pair]
        grad_out = jnp.where(jnp.abs(after) > SHRINK, pair_of(grad_spectrum, pair), 0.0)
        active, slope = gelu_parts(inner[pair])
        bias = jnp.sum(grad_out, axis=0, keepdims=True)
        small[6 + 2 * pair : 7 + 2 * pair, :] = bias[:, :half]
        small[7 + 2 * pair : 8 + 2 * pair, :] = bias[:, half:]
        grad_out = grad_out.astype(BF16)
        weights[1] += packed_weight(dot_tn(active.astype(BF16), grad_out))
        grad_in = dot_nt(grad_out, w_out[pair].astype(BF16)) * slope
        bias = jnp.sum(grad_in, axis=0, keepdims=True)
        small[2 * pair : 1 + 2 * pair, :] = bias[:, :half]
        small[1 + 2 * pair : 2 + 2 * pair, :] = bias[:, half:]
        grad_in = grad_in.astype(BF16)
        weights[0] += packed_weight(dot_tn(pair_of(scaled, pair).astype(BF16), grad_in))
        grad_part = dot_nt(grad_in, w_in[pair].astype(BF16))
        real.append(grad_part[:, :half])
        imag.append(grad_part[:, half:])
    grad = jnp.concatenate([jnp.concatenate(real, axis=1), jnp.concatenate(imag, axis=1)], axis=0)
    gain_grad = jnp.sum(grad * unit_spectrum, axis=0, keepdims=True) + sums[1:2, :]
    for at in range(3):
        lanes = slice(at * half, (at + 1) * half)
        small[12 + at : 13 + at, :] = gain_grad[:, lanes]
        small[15 + at : 16 + at, :] = sums[0:1, lanes]
        small[18 + at : 19 + at, :] = sums[2:3, lanes]
    for at in range(HIDDEN // half):
        small[21 + at : 22 + at, :] = up_sum[0:1, at * half : (at + 1) * half]
    sent[:, :, :WIDTH] = dot3(back_high[...], back_low[...], grad).reshape(GX, 8, WIDTH)
    for which in range(2):
        for at, part in enumerate(weights[which]):
            for group in range(8):
                place = (which * 2 * PAIRS + at) * 8 + group
                lanes = WIDTH + (place % 3) * half
                sent[place // 3, :, lanes : lanes + half] = part[group * 8 : group * 8 + 8, :]
    sent[:, :, WIDTH + 3 * half :] = small[...].reshape(GX, 8, half)


def mlp_kernel(volume, cotangent, modes, table, table_turned, gain_one, gain_two, up, up_bias, down,
               mixed, inputs, hidden, grad_before, grad_mixed, sent, up_sum, sums, weighted):
    step = pl.program_id(0)

    @pl.when(step == 0)
    def _():
        weighted[...] = (modes[...] * mode_weight((2 * MODES, 1))).astype(BF16)
        sent[...] = jnp.zeros_like(sent)
        up_sum[...] = jnp.zeros_like(up_sum)
        sums[...] = jnp.zeros_like(sums)

    wide = volume[...].astype(F32)
    unit_one, _ = normalise(wide)
    mixed_here = wide + dot(table_turned[...], weighted[...]) + unit_one * gain_one[...]
    mixed[...] = mixed_here
    unit_two, rate_two = normalise(mixed_here)
    inputs_here = (unit_two * gain_two[...]).astype(BF16)
    inputs[...] = inputs_here
    upstream = cotangent[...]
    grad = jnp.zeros((CHUNK, WIDTH), F32)
    for at in range(0, HIDDEN, HBLOCK):
        cut = slice(at, at + HBLOCK)
        before = dot(inputs_here, up[:, cut]) + up_bias[:, cut]
        active, slope = gelu_parts(before)
        hidden[:, cut] = active.astype(BF16)
        back = (dot_nt(upstream, down[cut, :]) * slope).astype(BF16)
        grad_before[:, cut] = back
        up_sum[0:1, cut] += jnp.sum(back.astype(F32), axis=0, keepdims=True)
    grad = dot_nt(grad_before[...], up[...])
    upstream = upstream.astype(F32)
    grad_here = upstream + norm_back(grad * gain_two[...], unit_two, rate_two)
    grad_mixed[...] = grad_here
    sums[0:1, :] += jnp.sum(grad * unit_two, axis=0, keepdims=True)
    sums[1:2, :] += jnp.sum(grad_here * unit_one, axis=0, keepdims=True)
    sums[2:3, :] += jnp.sum(upstream, axis=0, keepdims=True)
    sent[...] += dot(table[...], grad_here.astype(BF16)) * mode_weight((2 * MODES, 1))


WBLOCK = 768


def weight_kernel(mixed, inputs, cotangent, hidden, grad_before, down, down_bias, result, terms, total):
    step = pl.program_id(0)
    part = dot(hidden[...], down[...])

    @pl.when(step == 0)
    def _():
        total[...] = mixed[...] + down_bias[...] + part

    @pl.when(step == HIDDEN // WBLOCK - 1)
    def _():
        result[...] = (total[...] + part).astype(BF16)

    for which, (left, right) in enumerate(((grad_before, inputs), (hidden, cotangent))):
        term = dot_tn(left[...], right[...])
        for place in range(WBLOCK // 96):
            for core in range(2):
                for half in range(2):
                    at = place * 96 + core * 48 + half * 24
                    terms[which * 2 + half, core, place] = term[at : at + 24, :]


def last_kernel(volume, received, table_turned, gain_one, grad_mixed, out, rounded):
    @pl.when(pl.program_id(0) == 0)
    def _():
        rounded[...] = received[:, :, :WIDTH].reshape(2 * MODES, WIDTH).astype(BF16)

    unit, rate = normalise(volume[...].astype(F32))
    here = grad_mixed[...]
    grad = dot(table_turned[...], rounded[...]) + here
    out[...] = (here + norm_back(grad * gain_one[...], unit, rate)).astype(BF16)


def first_sum_kernel(received, out):
    total = jnp.sum(received[:, :, WIDTH:], axis=0)
    for copy in range(8):
        out[copy] = total


def second_sum_kernel(received, terms, out):
    total = jnp.sum(received[...], axis=0)
    for place in range(GX // 2):
        for group in range(3):
            out[place, :, group * WIDTH : (group + 1) * WIDTH] = terms[place, group * 8 : group * 8 + 8, :]
        out[place, :, 3 * WIDTH :] = total


def third_sum_kernel(received, out, slices):
    for group in range(3):
        total = jnp.sum(received[:, :, group * WIDTH : (group + 1) * WIDTH], axis=0)
        for copy in range(8):
            out[copy, group * 8 : group * 8 + 8, :] = total
    slices[...] = received[:, :, 3 * WIDTH :]


def final_kernel(core, received, mine, other, grad_up, grad_down, grad_w_in, grad_w_out, grad_b_in, grad_b_out, grad_one, grad_two, grad_down_bias, grad_up_bias, small):
    half = 2 * BLOCK
    parts = [received[2 * y] + received[2 * y + 1] for y in range(4)]
    grad_up[...] = jnp.concatenate(parts[:2], axis=0)
    grad_down[...] = jnp.concatenate(parts[2:], axis=0)
    first = core[0] == 0
    even = jnp.where(first, mine[...], other[...])
    odd = jnp.where(first, other[...], mine[...])
    both = (even, odd)
    for which, out in enumerate((grad_w_in, grad_w_out)):
        for at in range(2 * PAIRS):
            for group in range(8):
                place = (which * 2 * PAIRS + at) * 8 + group
                owner, lanes = place // 3, (place % 3) * half
                tile = both[owner % 2][owner // 2, :, lanes : lanes + half]
                rows = slice(group * 8, group * 8 + 8)
                out[at % 2, 2 * (at // 2), rows, :] = tile[:, :BLOCK]
                out[at % 2, 2 * (at // 2) + 1, rows, :] = tile[:, BLOCK:]
    for owner in range(SMALL // 8):
        small[owner * 8 : owner * 8 + 8, :] = both[owner % 2][owner // 2, :, 3 * half :]
    for first, out in ((0, grad_b_in), (6, grad_b_out)):
        for pair in range(PAIRS):
            for part in range(2):
                row = small[first + 2 * pair + part : first + 2 * pair + part + 1, :]
                out[2 * pair, part : part + 1, :] = row[:, :BLOCK]
                out[2 * pair + 1, part : part + 1, :] = row[:, BLOCK:]
    for first, out in ((12, grad_one), (15, grad_two), (18, grad_down_bias), (21, grad_up_bias)):
        for at in range(out.shape[0] // half):
            out[at * half : (at + 1) * half] = small[first + at, :]


def limit(mib):
    return pltpu.CompilerParams(vmem_limit_bytes=mib * MIB)


def call(kernel, out, *operands):
    return pl.pallas_call(kernel, out_shape=out, compiler_params=limit(12))(*operands)


def exchange(value, axis, groups=None):
    return lax.all_to_all(value, axis, split_axis=0, concat_axis=0, axis_index_groups=groups, tiled=True)


def paired(weight):
    zero = jnp.zeros((PAIRS, BLOCK, BLOCK), F32)
    even, odd = weight[:, 0::2], weight[:, 1::2]

    def wide(index):
        top = jnp.concatenate([even[index], zero], axis=2)
        return jnp.concatenate([top, jnp.concatenate([zero, odd[index]], axis=2)], axis=1)

    real, imag = wide(0), wide(1)
    return jnp.concatenate([jnp.concatenate([real, imag], axis=2), jnp.concatenate([-imag, real], axis=2)], axis=1)


def paired_bias(bias):
    return bias.reshape(2, PAIRS, 2 * BLOCK).transpose(1, 0, 2).reshape(PAIRS, 1, 4 * BLOCK)


def local(volume, gain_one, gain_two, w_in, b_in, w_out, b_out, up, up_bias, down, down_bias, cotangent):
    shape = volume.shape
    volume = volume.reshape(TOKENS, WIDTH)
    cotangent = cotangent.reshape(TOKENS, WIDTH)
    gain_one, gain_two, down_bias = (value.reshape(1, WIDTH) for value in (gain_one, gain_two, down_bias))
    slab = slab_table()
    slab_high, slab_low = (jnp.asarray(part) for part in halves(slab))
    slab_turned = jnp.asarray(halves(slab.T)[0])
    cross = cross_table()
    cross_high, cross_low = (jnp.asarray(part) for part in halves(cross))
    back_high, back_low = (jnp.asarray(part) for part in halves(cross.T))
    w_in, w_out, b_in, b_out = paired(w_in), paired(w_out), paired_bias(b_in), paired_bias(b_out)

    def sds(*dims, dtype=F32):
        return jax.ShapeDtypeStruct(dims, dtype)

    def slab(value):
        return value.reshape(GX, 2 * OWN, WIDTH)

    def rows(value):
        return value.reshape(2 * MODES, WIDTH)

    modes = call(first_kernel, sds(2 * MODES, WIDTH), volume, slab_high, slab_low)
    modes = rows(exchange(slab(modes), "space"))
    wide = sds(PAIRS, GX * OWN, 4 * BLOCK)
    modes, spectrum, inner, outer = call(
        filter_kernel,
        (sds(2 * MODES, WIDTH), sds(2 * MODES, WIDTH), wide, wide),
        modes, cross_high, cross_low, back_high, back_low, gain_one, w_in, b_in, w_out, b_out,
    )
    modes = rows(exchange(slab(modes), "space"))

    def whole(*dims):
        return pl.BlockSpec(dims, lambda step: (0,) * len(dims))

    def chunk(*dims):
        return pl.BlockSpec(dims, lambda step: (step, 0))

    def across(*dims):
        return pl.BlockSpec(dims, lambda step: (0, step))

    mixed, inputs, hidden, grad_before, grad_mixed, modes, up_sum, sums = pl.pallas_call(
        mlp_kernel,
        grid=(TOKENS // CHUNK,),
        in_specs=[
            chunk(CHUNK, WIDTH), chunk(CHUNK, WIDTH), whole(2 * MODES, WIDTH), across(2 * MODES, CHUNK), chunk(CHUNK, 2 * MODES),
            whole(1, WIDTH), whole(1, WIDTH), whole(WIDTH, HIDDEN), whole(1, HIDDEN), whole(HIDDEN, WIDTH),
        ],
        out_specs=(
            chunk(CHUNK, WIDTH), chunk(CHUNK, WIDTH), chunk(CHUNK, HIDDEN), chunk(CHUNK, HIDDEN), chunk(CHUNK, WIDTH),
            whole(2 * MODES, WIDTH), whole(8, HIDDEN), whole(8, WIDTH),
        ),
        out_shape=(
            sds(TOKENS, WIDTH), sds(TOKENS, WIDTH, dtype=BF16), sds(TOKENS, HIDDEN, dtype=BF16), sds(TOKENS, HIDDEN, dtype=BF16),
            sds(TOKENS, WIDTH), sds(2 * MODES, WIDTH), sds(8, HIDDEN), sds(8, WIDTH),
        ),
        scratch_shapes=[pltpu.VMEM((2 * MODES, WIDTH), BF16)],
        compiler_params=limit(60),
    )(volume, cotangent, modes, slab_high, slab_turned, gain_one, gain_two, up, up_bias.reshape(1, HIDDEN), down)

    places = GX // 2
    result, terms = pl.pallas_call(
        weight_kernel,
        grid=(HIDDEN // WBLOCK,),
        in_specs=[
            whole(TOKENS, WIDTH), whole(TOKENS, WIDTH), whole(TOKENS, WIDTH), across(TOKENS, WBLOCK), across(TOKENS, WBLOCK),
            chunk(WBLOCK, WIDTH), whole(1, WIDTH),
        ],
        out_specs=(
            whole(TOKENS, WIDTH),
            pl.BlockSpec((4, 2, WBLOCK // 96, 24, WIDTH), lambda step: (0, 0, step, 0, 0)),
        ),
        out_shape=(sds(TOKENS, WIDTH, dtype=BF16), sds(4, 2, places, 24, WIDTH)),
        scratch_shapes=[pltpu.VMEM((TOKENS, WIDTH), F32)],
        compiler_params=limit(60),
        cost_estimate=pl.CostEstimate(flops=6 * TOKENS * WIDTH * HIDDEN, bytes_accessed=16 * 1024 * 1024, transcendentals=0),
    )(mixed, inputs, cotangent, hidden, grad_before, down, down_bias)

    modes = exchange(slab(modes), "space")
    terms, modes = lax.optimization_barrier((terms, modes))
    terms = lax.psum_scatter(
        terms.reshape(8, places * 24, WIDTH), ("dp", "space"), scatter_dimension=0, axis_index_groups=Y_CORE, tiled=True
    ).reshape(places, 24, WIDTH)
    modes = rows(modes)
    carried = 3 * 2 * BLOCK + 2 * BLOCK
    sent = pl.pallas_call(
        filter_back_kernel,
        out_shape=sds(GX, 8, WIDTH + carried),
        scratch_shapes=[pltpu.VMEM((GX * 8, 2 * BLOCK), F32)],
        compiler_params=limit(12),
    )(modes, cross_high, cross_low, back_high, back_low, gain_one, w_in, w_out, spectrum, inner, outer, sums, up_sum)
    received = exchange(sent, "space")
    shared = exchange(call(first_sum_kernel, sds(8, 8, carried), received), "dp")
    grad_volume = pl.pallas_call(
        last_kernel,
        grid=(TOKENS // CHUNK,),
        in_specs=[
            chunk(CHUNK, WIDTH), pl.BlockSpec((GX, 8, WIDTH + carried), lambda step: (0, 0, 0)), chunk(CHUNK, 2 * MODES), whole(1, WIDTH), chunk(CHUNK, WIDTH),
        ],
        out_specs=chunk(CHUNK, WIDTH),
        out_shape=sds(TOKENS, WIDTH, dtype=BF16),
        scratch_shapes=[pltpu.VMEM((2 * MODES, WIDTH), BF16)],
        compiler_params=limit(12),
        cost_estimate=pl.CostEstimate(flops=TOKENS * WIDTH * 1024, bytes_accessed=8 * 1024 * 1024, transcendentals=0),
    )(volume, received, slab_turned, gain_one, grad_mixed)
    gathered = exchange(call(second_sum_kernel, sds(places, 8, 3 * WIDTH + carried), shared, terms), "space", X_Z)
    copies, mine = call(third_sum_kernel, (sds(8, 24, WIDTH), sds(places, 8, carried)), gathered)
    other = lax.ppermute(mine, "space", [(at, at ^ 1) for at in range(GX)])
    copies = exchange(copies, "dp")
    core = (lax.axis_index("space") & 1).reshape(1)
    square = sds(2, BLOCKS, BLOCK, BLOCK)
    vmem = pl.BlockSpec(memory_space=pltpu.VMEM)
    tall = sds(BLOCKS, 2, BLOCK)
    row = sds(WIDTH)
    grad_up, grad_down, grad_w_in, grad_w_out, grad_b_in, grad_b_out, grad_one, grad_two, grad_down_bias, grad_up_bias = pl.pallas_call(
        final_kernel,
        in_specs=[pl.BlockSpec(memory_space=pltpu.SMEM), vmem, vmem, vmem],
        out_shape=(sds(48, WIDTH), sds(48, WIDTH), square, square, tall, tall, row, row, row, sds(HIDDEN)),
        scratch_shapes=[pltpu.VMEM((SMALL, 2 * BLOCK), F32)],
        compiler_params=limit(8),
    )(core, copies, mine, other)
    return (
        result.reshape(shape),
        grad_volume.reshape(shape),
        grad_one,
        grad_two,
        grad_w_in,
        grad_b_in.transpose(1, 0, 2),
        grad_w_out,
        grad_b_out.transpose(1, 0, 2),
        grad_up.T,
        grad_up_bias,
        grad_down,
        grad_down_bias,
    )


def solution(mesh):
    field = P("dp", "space", None, None, None)
    return jax.shard_map(
        local,
        mesh=mesh,
        in_specs=(field,) + (P(),) * 10 + (field,),
        out_specs=(field, field) + (P(),) * 6 + (P(None, "space"), P(), P("space", None), P()),
        check_vma=False,
    )
```

time: 538 us -> 195 us (0.36)
  waiting for transfers between devices: 342 us -> 37.3 us
  blocking collectives: 96.4 us -> 68.9 us
  Pallas kernels: 43.5 us -> 34.7 us
  starting transfers between devices: 18.6 us -> 25.8 us
    psum x2 -> x0, waiting for transfers between devices: 248 us -> none  [the longest x1 248 us: local(): lax.psum((grad_w_in, grad_w_out, grad_b_in, grad_b_out, grad_gain[0] + su...]
    psum x1 -> x0, blocking collectives: 76.4 us -> none  [local(): lax.psum((grad_w_in, grad_w_out, grad_b_in, grad_b_out, grad_gain[0] + su...]
    reduce_scatter x1, waiting for transfers between devices: 67.6 us -> 0.01 us  [local(): lax.psum_scatter(terms.reshape(8, places * 24, WIDTH), ('dp', 'space'), s...]
    all_to_all x1 -> x3, blocking collectives: 20 us -> 68.9 us  [exchange(): lax.all_to_all(value, axis, split_axis=0, concat_axis=0, axis_index_group...]
    all_to_all x3 -> x4, waiting for transfers between devices: 26.5 us -> 37.3 us  [exchange(): lax.all_to_all(value, axis, split_axis=0, concat_axis=0, axis_index_group...]
    pallas_call x5 -> x10, Pallas kernels: 43.5 us -> 34.7 us  [the longest x1 13.6 us: local(): pl.pallas_call(mlp_kernel, grid=(TOKENS // CHUNK,), in_specs=[chunk(CHUNK...]
    all_to_all x3 -> x4, starting transfers between devices: 18.5 us -> 25.8 us  [exchange(): lax.all_to_all(value, axis, split_axis=0, concat_axis=0, axis_index_group...]
  transfers between devices with their start and end apart: 6 -> 6, of which waited for: 4 -> 4; matrix products, arithmetic and copies ran while one was open for 2% -> 1% of each run, Pallas kernels for 2% -> 8%
where the time goes in v2:
time: 195 us; the launch traced here: 194 us
  blocking collectives  68.9 us (35%)
  waiting for transfers between devices  37.3 us (19%)
  Pallas kernels  34.7 us (18%)
  starting transfers between devices  25.8 us (13%)
  between operations  14.4 us (7%)
  local copies, waits for them, and re-layouts  12.3 us (6%)
    all_to_all x3, blocking collectives, exchange(): lax.all_to_all(value, axis, split_axis=0, concat_axis=0, axis_index_group...  68.9 us
    all_to_all x4, waiting for transfers between devices, exchange(): lax.all_to_all(value, axis, split_axis=0, concat_axis=0, axis_index_group...  37.3 us
    all_to_all x4, starting transfers between devices, exchange(): lax.all_to_all(value, axis, split_axis=0, concat_axis=0, axis_index_group...  25.8 us
    pallas_call x1, Pallas kernels, local(): pl.pallas_call(mlp_kernel, grid=(TOKENS // CHUNK,), in_specs=[chunk(CHUNK...  13.6 us
    pallas_call x1, Pallas kernels, local(): pl.pallas_call(weight_kernel, grid=(HIDDEN // WBLOCK,), in_specs=[whole(T...  11.2 us
    unnamed x56, local copies, waits for them, and re-layouts  9.93 us
    pallas_call x5, Pallas kernels, call(): pl.pallas_call(kernel, out_shape=out, compiler_params=limit(12))(*operands)  5.02 us
  transfers between devices with their start and end apart: 6, of which 4 were waited for; matrix products, arithmetic and copies ran while one was open for 1% of the time, Pallas kernels for 8%

profile of v2, /device:TPU:32, one launch (start us, length us, event | category | flops | bytes accessed | tf_op | source)
XLA Modules:
  0.0 193.6 jit_solution(15539003039703076311)
XLA Ops:
  7.2 1.1 copy-done
  8.3 1.0 copy-done.2
  9.4 1.0 copy-done.6
  10.4 2.3 %shard_map.274 = f32[256,384]{1,0:T(8,128)} custom-call(bf16[1024,384]{1,0:T(8,128)(2,1)S(1)} %bitcast.37, bf16[256,1024]{1,0:T(8,128)(2,1)S(1)} %copy-done.2, bf16[256,1024]{1,0:T(8,128)(2,1)S(1)} %copy-done.6), custom_call_target="tpu_custom_call" | custom-call | tf_op jit(solution)/shard_map/pallas_call | solution.py:336
  12.7 10.4 %all-to-all-start = ((f32[32,8,384]{2,1,0:T(8,128)}), f32[32,8,384]{2,1,0:T(8,128)S(1)}, u32[]{:S(2)}, u32[]{:S(2)}) async-start(f32[32,8,384]{2,1,0:T(8,128)} %bitcast.2), calls=%async_computation | async-start | bytes 786432 | tf_op jit(solution)/shard_map/all_to_all | solution.py:340
  23.3 0.1 concatenate.67
  23.4 0.1 concatenate.64
  23.5 0.1 concatenate.58
  23.6 0.1 concatenate.55
  23.7 0.1 copy-done.24
  23.9 0.0 copy-done.22
  23.9 0.1 reshape.94
  24.0 0.1 reshape.92
  24.1 0.0 copy-start.7
  24.1 0.0 copy-start.8
  24.1 0.0 copy-start.9
  24.2 0.1 maximum_maximum_fusion.1.w_out
  24.2 0.1 maximum_maximum_fusion.w_in
  24.3 15.1 %all-to-all-done = f32[32,8,384]{2,1,0:T(8,128)S(1)} async-done(((f32[32,8,384]{2,1,0:T(8,128)}), f32[32,8,384]{2,1,0:T(8,128)S(1)}, u32[]{:S(2)}, u32[]{:S(2)}) %all-to-all-start) | async-done | bytes 393248 | tf_op jit(solution)/shard_map/all_to_all | solution.py:340
  39.5 1.9 shard_map.275
  41.4 0.7 copy-done.11
  42.1 0.7 copy-done.13
  42.9 3.9 %all-to-all-start.1 = ((f32[32,8,384]{2,1,0:T(8,128)}), f32[32,8,384]{2,1,0:T(8,128)S(1)}, u32[]{:S(2)}, u32[]{:S(2)}) async-start(f32[32,8,384]{2,1,0:T(8,128)} %bitcast.42), calls=%async_computation.1 | async-start | bytes 786432 | tf_op jit(solution)/shard_map/all_to_all | solution.py:340
  46.8 0.6 reshape.99.up_bias
  47.4 0.6 reshape.98.gain_two
  48.0 15.2 %all-to-all-done.1 = f32[32,8,384]{2,1,0:T(8,128)S(1)} async-done(((f32[32,8,384]{2,1,0:T(8,128)}), f32[32,8,384]{2,1,0:T(8,128)S(1)}, u32[]{:S(2)}, u32[]{:S(2)}) %all-to-all-start.1) | async-done | bytes 393248 | tf_op jit(solution)/shard_map/all_to_all | solution.py:340
  63.1 0.7 copy-done.18
  63.9 13.6 %shard_map.276 = (f32[1024,384]{1,0:T(8,128)}, bf16[1024,384]{1,0:T(8,128)(2,1)}, bf16[1024,1536]{1,0:T(8,128)(2,1)}, bf16[1024,1536]{1,0:T(8,128)(2,1)}, f32[10...) custom-call(bf16[1024,384]{1,0:T(8,128)(2,1)} %bitcast.36, ...), custom_call_target="tpu_custom_call" | custom-call | tf_op jit(solution)/shard_map/pallas_call | solution.py:400
  77.4 3.9 %all-to-all-start.2 = ((f32[32,8,384]{2,1,0:T(8,128)}), f32[32,8,384]{2,1,0:T(8,128)S(1)}, u32[]{:S(2)}, u32[]{:S(2)}) async-start(f32[32,8,384]{2,1,0:T(8,128)} %bitcast.50), calls=%async_computation.2 | async-start | bytes 786432 | tf_op jit(solution)/shard_map/all_to_all | solution.py:340
  81.4 0.0 reduce-scatter.2.cloned.1.call-start
  81.4 0.6 reshape.100.down_bias
  82.0 11.2 %shard_map.277 = (bf16[1024,384]{1,0:T(8,128)(2,1)}, f32[4,2,16,24,384]{4,3,2,1,0:T(8,128)}) custom-call(f32[1024,384]{1,0:T(8,128)} %get-tuple-element.41.mixed, bf16[1024,384]{1,0:T(8,128)(2,1)} %get-tuple-element.42.inputs, bf16[1024,384]{1,0:T(8,128)(2,1)} %bitcast.48, bf16[1024,1536]{1,0:T(8,128)(2,1)} %get-tuple-element.43.hidden, ...), custom_call_target="tpu_custom_call" | custom-call | flops 3623878656 | bytes 16777216 | tf_op jit(solution)/shard_map/pallas_call | solution.py:420
  93.2 4.5 %all-to-all-done.2 = f32[32,8,384]{2,1,0:T(8,128)S(1)} async-done(((f32[32,8,384]{2,1,0:T(8,128)}), f32[32,8,384]{2,1,0:T(8,128)S(1)}, u32[]{:S(2)}, u32[]{:S(2)}) %all-to-all-start.2) | async-done | bytes 393248 | tf_op jit(solution)/shard_map/all_to_all | solution.py:340
  97.7 0.0 reduce-scatter.2.cloned.1.call-update
  97.7 0.8 copy-done.14
  98.5 1.0 copy-done.12
  99.5 1.4 shard_map.278
  100.9 31.9 %all_to_all.35.received = f32[32,8,896]{2,1,0:T(8,128)S(1)} all-to-all(f32[32,8,896]{2,1,0:T(8,128)S(1)} %shard_map.278), channel_id=1, replica_groups=mesh['dp'=8,'space'=32] {'space'}, dimensions={0} | all-to-all | bytes 1835008 | tf_op jit(solution)/shard_map/all_to_all | solution.py:340
  132.8 11.5 %all_to_all.36.received = f32[8,8,512]{2,1,0:T(8,128)S(1)} all-to-all(f32[8,8,512]{2,1,0:T(8,128)S(1)} %shard_map.280), channel_id=1, replica_groups=mesh['dp'=8,'space'=32] {'dp'}, dimensions={0} | all-to-all | bytes 262144 | tf_op jit(solution)/shard_map/all_to_all | solution.py:340
  144.3 1.1 copy-done.5
  145.4 0.1 shard_map.281
  145.5 25.6 %all_to_all.37.received = f32[16,8,1664]{2,1,0:T(8,128)S(1)} all-to-all(f32[16,8,1664]{2,1,0:T(8,128)S(1)} %shard_map.281), channel_id=1, replica_groups={{0,2,4,6,8,10,12,14,16,18,20,22,24,26,28,30},{1,3,5,7,9,11,13,15,17,19,..., dimensions={0} | all-to-all | bytes 1703936 | tf_op jit(solution)/shard_map/all_to_all | solution.py:340
  171.0 0.8 shard_map.282
  171.8 7.6 %all-to-all-start.6 = ((f32[8,24,384]{2,1,0:T(8,128)}), f32[8,24,384]{2,1,0:T(8,128)S(1)}, u32[]{:S(2)}, u32[]{:S(2)}) async-start(f32[8,24,384]{2,1,0:T(8,128)} %get-tuple-element.56), calls=%async_computation.7 | async-start | bytes 589824 | tf_op jit(solution)/shard_map/all_to_all | solution.py:340
  179.4 1.4 copy-done.4
  180.8 2.4 %shard_map.279 = bf16[1024,384]{1,0:T(8,128)(2,1)} custom-call(bf16[1024,384]{1,0:T(8,128)(2,1)S(1)} %bitcast.38, f32[32,8,896]{2,1,0:T(8,128)S(1)} %all_to_all.35.received, bf16[1024,256]{1,0:T(8,128)(2,1)S(1)} %copy-done.3, f32[1,384]{1,0:T(1,128)S(1)} %copy-done.16, f32[1024,384]{1,0:T(8,128)S(1)} %copy-done.4), custom_call_target="tpu_custom_call" | custom-call | flops 402653184 | bytes 8388608 | tf_op jit(solution)/shard_map/pallas_call | solution.py:452
  183.3 2.4 %all-to-all-done.6.received = f32[8,24,384]{2,1,0:T(8,128)S(1)} async-done(((f32[8,24,384]{2,1,0:T(8,128)}), f32[8,24,384]{2,1,0:T(8,128)S(1)}, u32[]{:S(2)}, u32[]{:S(2)}) %all-to-all-start.6) | async-done | bytes 294944 | tf_op jit(solution)/shard_map/all_to_all | solution.py:340
  185.7 1.1 shard_map.283
  (58 shorter events, 0.4 us)
Async XLA Ops:
  7.2 1.1 copy-start
  8.3 1.0 copy-start.2
  9.4 1.0 copy-start.6
  10.4 12.7 %copy-start.19 = (f32[2,6,64,64]{3,2,1,0:T(8,128)S(1)}, f32[2,6,64,64]{3,2,1,0:T(8,128)}, u32[]{:S(2)}) copy-start(f32[2,6,64,64]{3,2,1,0:T(8,128)} %param.24) | copy-start | bytes 589828
  10.4 12.7 %copy-start.20 = (f32[2,6,64,64]{3,2,1,0:T(8,128)S(1)}, f32[2,6,64,64]{3,2,1,0:T(8,128)}, u32[]{:S(2)}) copy-start(f32[2,6,64,64]{3,2,1,0:T(8,128)} %param.22) | copy-start | bytes 589828
  12.7 26.8 %all-to-all-start = ((f32[32,8,384]{2,1,0:T(8,128)}), f32[32,8,384]{2,1,0:T(8,128)S(1)}, u32[]{:S(2)}, u32[]{:S(2)}) async-start(f32[32,8,384]{2,1,0:T(8,128)} %bitcast.2), calls=%async_computation | async-start | bytes 786432 | tf_op jit(solution)/shard_map/all_to_all | solution.py:340
  23.2 0.7 copy-start.24
  23.2 0.7 copy-start.22
  23.2 0.8 copy-start.23
  23.9 15.5 %copy-start.15 = (f32[1,384]{1,0:T(1,128)}, f32[1,384]{1,0:T(1,128)S(1)}, u32[]{:S(2)}) copy-start(f32[1,384]{1,0:T(1,128)S(1)} %reshape.91.gain.gain_one) | copy-start | bytes 4612
  24.1 15.3 %copy-start.7 = (bf16[256,256]{1,0:T(8,128)(2,1)S(1)}, bf16[256,256]{1,0:T(8,128)(2,1)}, u32[]{:S(2)}) copy-start(bf16[256,256]{1,0:T(8,128)(2,1)} %constant.25.clone.cross_high) | copy-start | bytes 393220
  24.1 15.3 %copy-start.8 = (bf16[256,256]{1,0:T(8,128)(2,1)S(1)}, bf16[256,256]{1,0:T(8,128)(2,1)}, u32[]{:S(2)}) copy-start(bf16[256,256]{1,0:T(8,128)(2,1)} %constant.26.clone.cross_low) | copy-start | bytes 393220
  24.1 15.3 %copy-start.9 = (bf16[256,256]{1,0:T(8,128)(2,1)S(1)}, bf16[256,256]{1,0:T(8,128)(2,1)}, u32[]{:S(2)}) copy-start(bf16[256,256]{1,0:T(8,128)(2,1)} %constant.27.clone.back_high) | copy-start | bytes 393220
  24.1 15.3 %copy-start.10 = (bf16[256,256]{1,0:T(8,128)(2,1)S(1)}, bf16[256,256]{1,0:T(8,128)(2,1)}, u32[]{:S(2)}) copy-start(bf16[256,256]{1,0:T(8,128)(2,1)} %constant.28.clone.back_low) | copy-start | bytes 393220
  39.5 7.3 %copy-start.21 = (f32[1536]{0:T(1024)S(1)}, f32[1536]{0:T(1024)}, u32[]{:S(2)}) copy-start(f32[1536]{0:T(1024)} %param.27) | copy-start | bytes 18436
  39.5 7.9 %copy-start.25 = (f32[384]{0:T(512)S(1)}, f32[384]{0:T(512)}, u32[]{:S(2)}) copy-start(f32[384]{0:T(512)} %param.21) | copy-start | bytes 4612
  41.4 0.8 copy-start.11
  42.1 0.7 copy-start.13
  42.9 20.2 %all-to-all-start.1 = ((f32[32,8,384]{2,1,0:T(8,128)}), f32[32,8,384]{2,1,0:T(8,128)S(1)}, u32[]{:S(2)}, u32[]{:S(2)}) async-start(f32[32,8,384]{2,1,0:T(8,128)} %bitcast.42), calls=%async_computation.1 | async-start | bytes 786432 | tf_op jit(solution)/shard_map/all_to_all | solution.py:340
  63.1 0.7 copy-start.18
  63.9 17.5 %copy-start.26 = (f32[384]{0:T(512)S(1)}, f32[384]{0:T(512)}, u32[]{:S(2)}) copy-start(f32[384]{0:T(512)} %param.29) | copy-start | bytes 4612
  77.4 20.3 %all-to-all-start.2 = ((f32[32,8,384]{2,1,0:T(8,128)}), f32[32,8,384]{2,1,0:T(8,128)S(1)}, u32[]{:S(2)}, u32[]{:S(2)}) async-start(f32[32,8,384]{2,1,0:T(8,128)} %bitcast.50), calls=%async_computation.2 | async-start | bytes 786432 | tf_op jit(solution)/shard_map/all_to_all | solution.py:340
  81.4 62.9 %reduce-scatter.2.cloned.1.call-start = ((), (), s32[]{:S(2)}) async-start(), calls=%async_computation.8 | async-start | bytes 5308416 | tf_op jit(solution)/shard_map/reduce_scatter | solution.py:439
  97.7 0.8 copy-start.14
  97.7 0.8 copy-start.16
  97.7 0.8 copy-start.17
  98.5 1.0 copy-start.12
  144.3 1.1 copy-start.5
  145.4 34.0 %copy-start.1 = (bf16[1,1,32,32,384]{4,3,2,1,0:T(8,128)(2,1)S(1)}, bf16[1,1,32,32,384]{4,3,2,1,0:T(8,128)(2,1)}, u32[]{:S(2)}) copy-start(bf16[1,1,32,32,384]{4,3,2,1,0:T(8,128)(2,1)} %param.19) | copy-start | bytes 2359300
  145.4 34.0 %copy-start.3 = (bf16[1024,256]{1,0:T(8,128)(2,1)S(1)}, bf16[1024,256]{1,0:T(8,128)(2,1)}, u32[]{:S(2)}) copy-start(bf16[1024,256]{1,0:T(8,128)(2,1)} %constant.24.clone.table_turned) | copy-start | bytes 1572868
  171.8 13.9 %all-to-all-start.6 = ((f32[8,24,384]{2,1,0:T(8,128)}), f32[8,24,384]{2,1,0:T(8,128)S(1)}, u32[]{:S(2)}, u32[]{:S(2)}) async-start(f32[8,24,384]{2,1,0:T(8,128)} %get-tuple-element.56), calls=%async_computation.7 | async-start | bytes 589824 | tf_op jit(solution)/shard_map/all_to_all | solution.py:340
  179.4 3.9 %collective-permute-start = (f32[16,8,512]{2,1,0:T(8,128)S(1)}, f32[16,8,512]{2,1,0:T(8,128)S(1)}, u32[]{:S(2)}, u32[]{:S(2)}) collective-permute-start(f32[16,8,512]{2,1,0:T(8,128)S(1)} %get-tuple-element.57.mine), channel_id=1, source_target_pairs={{0,1},{1,0},{2,3},{3,2},{4,5},{5,4},{6,7},{7,6},{8,9},{9,8},{10,11... | collective-permute-start | bytes 786440 | tf_op jit(solution)/shard_map/ppermute | solution.py:466
  179.4 1.4 copy-start.4
Sparse Core Ops, SparseCore 0:
  97.9 39.6 reduce-scatter.1

commit v3 on v2

v3 whole, which is shorter than its diff:
```python
import functools
import math

import jax
import jax.numpy as jnp
import ml_dtypes
import numpy as np
from jax import lax
from jax.experimental import pallas as pl
from jax.experimental.pallas import tpu as pltpu
from jax.sharding import PartitionSpec as P

WIDTH = 384
BLOCKS = 6
BLOCK = 64
HIDDEN = 1536
GX = 32
GY = 32
GZ = 32
KEEP_Y = 16
KEEP_Z = 8
MODES = KEEP_Y * KEEP_Z
PLACES = GX // 2
OWN = MODES // PLACES
TOKENS = GY * GZ
HALF = BLOCKS // 2
PAIR = 2 * BLOCK
HBLOCK = 256
CHUNK = 512

Y_CORE = [
    [(y * 2 + low) * GX + place * 2 + core for y in range(4) for core in range(2)] for low in range(2) for place in range(GX // 2)
]
X_Z = [[place * 2 + core for place in range(GX // 2)] for core in range(2)]

EPSILON = 1e-05
SHRINK = 0.01
ROOT = math.sqrt(2.0 / math.pi)
CUBIC = 0.044715 * ROOT
MIB = 1024 * 1024
LATE = 200_000_000_000

BF16 = jnp.bfloat16
F32 = jnp.float32


def halves(table):
    high = table.astype(np.float32).astype(ml_dtypes.bfloat16)
    low = (table - high.astype(np.float64)).astype(np.float32).astype(ml_dtypes.bfloat16)
    return high, low


def slab_table():
    kept = np.concatenate([np.arange(KEEP_Y // 2), np.arange(GY - KEEP_Y // 2, GY)])
    ky, kz = np.repeat(kept, KEEP_Z), np.tile(np.arange(KEEP_Z), KEEP_Y)
    y, z = np.repeat(np.arange(GY), GZ), np.tile(np.arange(GZ), GY)
    angle = 2.0 * np.pi * ((ky[:, None] * y[None, :] + kz[:, None] * z[None, :]) % GY) / GY
    both = np.stack([np.cos(angle), -np.sin(angle)]).reshape(2, PLACES, OWN, TOKENS)
    return both.transpose(1, 0, 2, 3).reshape(2 * MODES, TOKENS) / math.sqrt(TOKENS)


def cross_tables():
    angle = 2.0 * np.pi * (np.outer(np.arange(GX), np.arange(GX)) % GX) / GX
    return [np.kron(part(angle), np.eye(OWN)) / math.sqrt(GX) for part in (np.cos, np.sin)]


def dot(a, b):
    return jnp.dot(a, b, preferred_element_type=F32)


def dot_nt(a, b):
    return lax.dot_general(a, b, (((1,), (1,)), ((), ())), preferred_element_type=F32)


def dot_tn(a, b):
    return lax.dot_general(a, b, (((0,), (0,)), ((), ())), preferred_element_type=F32)


def split(value):
    high = value.astype(BF16)
    return high, (value - high.astype(F32)).astype(BF16)


def dot3(table_high, table_low, value):
    high, low = split(value)
    return dot(table_high, high) + (dot(table_low, high) + dot(table_high, low))


def dot6(a, b):
    return jnp.dot(a, b, preferred_element_type=F32, precision=lax.Precision.HIGHEST)


def normalise(values):
    center = values - jnp.mean(values, axis=-1, keepdims=True)
    rate = lax.rsqrt(jnp.mean(center * center, axis=-1, keepdims=True) + EPSILON)
    return center * rate, rate


def norm_back(grad, unit, rate):
    first = jnp.mean(grad, axis=-1, keepdims=True)
    second = jnp.mean(grad * unit, axis=-1, keepdims=True)
    return rate * (grad - first - unit * second)


def gelu_parts(value):
    square = value * value
    gate = 0.5 + 0.5 * jnp.tanh(value * (ROOT + CUBIC * square))
    active = value * gate
    slope = gate + (active - active * gate) * (2.0 * ROOT + (6.0 * CUBIC) * square)
    return active, slope


def gelu(value):
    return value * (0.5 + 0.5 * jnp.tanh(value * (ROOT + CUBIC * (value * value))))


def mode_weight():
    place = lax.broadcasted_iota(jnp.int32, (2 * MODES, 1), 0) & (KEEP_Z - 1)
    return jnp.where(place == 0, 1.0, 2.0).astype(F32)


def low_lanes(rows):
    return lax.broadcasted_iota(jnp.int32, (rows, PAIR), 1) < BLOCK


def turn(tile):
    return pltpu.roll(tile, BLOCK, 1)


def tiles(value):
    return [value[:, at : at + PAIR] for at in range(0, value.shape[1], PAIR)]


def to_owners(value, out):
    value = value.reshape(PLACES, 2, OWN, WIDTH)
    low = low_lanes(MODES)
    for at, (real, imag) in enumerate(zip(tiles(value[:, 0].reshape(MODES, WIDTH)), tiles(value[:, 1].reshape(MODES, WIDTH)))):
        for block, tile in ((2 * at, jnp.where(low, real, turn(imag))), (2 * at + 1, jnp.where(low, turn(real), imag))):
            lanes = (block % HALF) * PAIR
            out[:, block // HALF, :, lanes : lanes + PAIR] = tile.reshape(PLACES, OWN, PAIR)


def from_owners(value):
    low = low_lanes(MODES)
    blocks = [tile for core in range(2) for tile in tiles(value[:, core].reshape(MODES, WIDTH))]
    real = [jnp.where(low, even, turn(odd)) for even, odd in zip(blocks[0::2], blocks[1::2])]
    imag = [jnp.where(low, turn(even), odd) for even, odd in zip(blocks[0::2], blocks[1::2])]
    parts = [jnp.concatenate(part, axis=1).reshape(PLACES, 1, OWN, WIDTH) for part in (real, imag)]
    return jnp.concatenate(parts, axis=1).reshape(2 * MODES, WIDTH)


def times_minus_i(value):
    low = low_lanes(value.shape[0])
    return jnp.concatenate([jnp.where(low, turn(tile), -turn(tile)) for tile in tiles(value)], axis=1)


def along_x(tables, value, sign):
    cos_high, cos_low, sin_high, sin_low = (table[...] for table in tables)
    straight = dot3(cos_high, cos_low, value)
    crossed = dot3(sin_high, sin_low, times_minus_i(value))
    return straight + crossed if sign < 0 else straight - crossed


def first_kernel(volume, table_high, table_low, out):
    unit, _ = normalise(volume[...].astype(F32))
    to_owners(dot3(table_high[...], table_low[...], unit), out)


def filter_kernel(received, cos_high, cos_low, sin_high, sin_low, gain, w_in, b_in, w_out, b_out, sent, spectrum, inner, outer):
    tables = (cos_high, cos_low, sin_high, sin_low)
    unit_spectrum = along_x(tables, received[...], -1)
    spectrum[...] = unit_spectrum
    shrunk = []
    for block, part in enumerate(tiles(unit_spectrum * gain[...])):
        before = dot6(part, w_in[block]) + b_in[block]
        inner[block] = before
        after = dot6(gelu(before), w_out[block]) + b_out[block]
        outer[block] = after
        shrunk.append(after - jnp.clip(after, -SHRINK, SHRINK))
    sent[...] = along_x(tables, jnp.concatenate(shrunk, axis=1), 1)


def packed_weight(grad):
    other = turn(grad[BLOCK:])
    return grad[:BLOCK] + jnp.where(low_lanes(BLOCK), other, -other)


SMALL = 32


def filter_back_kernel(received, cos_high, cos_low, sin_high, sin_low, gain, w_in, w_out, spectrum, inner, outer, sums, up_sum, sent, weights, small):
    tables = (cos_high, cos_low, sin_high, sin_low)
    unit_spectrum = spectrum[...]
    small[...] = jnp.zeros_like(small)
    grads = []
    scaled = tiles(unit_spectrum * gain[...])
    for block, grad_out in enumerate(tiles(along_x(tables, received[...], -1))):
        grad_out = jnp.where(jnp.abs(outer[block]) > SHRINK, grad_out, 0.0)
        active, slope = gelu_parts(inner[block])
        small[HALF + block : HALF + block + 1, :] = jnp.sum(grad_out, axis=0, keepdims=True)
        grad_out = grad_out.astype(BF16)
        weights[HALF + block] = packed_weight(dot_tn(active.astype(BF16), grad_out))
        grad_in = dot_nt(grad_out, w_out[block].astype(BF16)) * slope
        small[block : block + 1, :] = jnp.sum(grad_in, axis=0, keepdims=True)
        grad_in = grad_in.astype(BF16)
        weights[block] = packed_weight(dot_tn(scaled[block].astype(BF16), grad_in))
        grads.append(dot_nt(grad_in, w_in[block].astype(BF16)))
    grad = jnp.concatenate(grads, axis=1)
    for block, part in enumerate(tiles(jnp.sum(grad * unit_spectrum, axis=0, keepdims=True))):
        row = jnp.broadcast_to(part, (8, PAIR))
        small[6 + block : 7 + block, :] = (row + turn(row))[0:1, :]
    for at in range(3):
        lanes = slice(at * PAIR, (at + 1) * PAIR)
        small[9 + at : 10 + at, :] = sums[1:2, lanes]
        small[12 + at : 13 + at, :] = sums[0:1, lanes]
        small[15 + at : 16 + at, :] = sums[2:3, lanes]
    for at in range(HIDDEN // PAIR):
        small[18 + at : 19 + at, :] = up_sum[0:1, at * PAIR : (at + 1) * PAIR]
    sent[:, :, :WIDTH] = along_x(tables, grad, 1).reshape(GX, 8, WIDTH)
    for owner in range(GX):
        at = owner * 8
        sent[owner, :, WIDTH : WIDTH + PAIR] = weights[at // BLOCK, at % BLOCK : at % BLOCK + 8, :]
        at = GX * 8 + owner * 4
        sent[owner, 0:4, WIDTH + PAIR :] = weights[at // BLOCK, at % BLOCK : at % BLOCK + 4, :]
        if owner * 4 < SMALL:
            sent[owner, 4:8, WIDTH + PAIR :] = small[owner * 4 : owner * 4 + 4, :]
        else:
            sent[owner, 4:8, WIDTH + PAIR :] = jnp.zeros((4, PAIR), F32)


def mlp_kernel(volume, cotangent, modes, table, table_turned, gain_one, gain_two, up, up_bias, down,
               mixed, inputs, hidden, grad_before, grad_mixed, sent, up_sum, sums):
    weighted = (from_owners(modes[...]) * mode_weight()).astype(BF16)
    wide = volume[...].astype(F32)
    unit_one, _ = normalise(wide)
    mixed_here = wide + dot(table_turned[...], weighted) + unit_one * gain_one[...]
    mixed[...] = mixed_here
    unit_two, rate_two = normalise(mixed_here)
    inputs_here = (unit_two * gain_two[...]).astype(BF16)
    inputs[...] = inputs_here
    upstream = cotangent[...]
    up_sum[...] = jnp.zeros_like(up_sum)
    for at in range(0, HIDDEN, HBLOCK):
        cut = slice(at, at + HBLOCK)
        before = dot(inputs_here, up[:, cut]) + up_bias[:, cut]
        active, slope = gelu_parts(before)
        hidden[:, cut] = active.astype(BF16)
        back = (dot_nt(upstream, down[cut, :]) * slope).astype(BF16)
        grad_before[:, cut] = back
        up_sum[0:1, cut] = jnp.sum(back.astype(F32), axis=0, keepdims=True)
    grad = dot_nt(grad_before[...], up[...])
    upstream = upstream.astype(F32)
    grad_here = upstream + norm_back(grad * gain_two[...], unit_two, rate_two)
    grad_mixed[...] = grad_here
    sums[...] = jnp.zeros_like(sums)
    sums[0:1, :] = jnp.sum(grad * unit_two, axis=0, keepdims=True)
    sums[1:2, :] = jnp.sum(grad_here * unit_one, axis=0, keepdims=True)
    sums[2:3, :] = jnp.sum(upstream, axis=0, keepdims=True)
    to_owners(dot(table[...], grad_here.astype(BF16)) * mode_weight(), sent)


WBLOCK = 768


def weight_kernel(inputs, cotangent, hidden, grad_before, terms):
    for which, (left, right) in enumerate(((grad_before, inputs), (hidden, cotangent))):
        term = dot_tn(left[...], right[...])
        for place in range(WBLOCK // 96):
            for core in range(2):
                for half in range(2):
                    at = place * 96 + core * 48 + half * 24
                    terms[which * 2 + half, core, place] = term[at : at + 24, :]


def result_kernel(mixed, hidden, down, down_bias, result):
    result[...] = (mixed[...] + down_bias[...] + dot(hidden[...], down[...])).astype(BF16)


def last_kernel(volume, received, table_turned, gain_one, grad_mixed, out, rounded):
    @pl.when(pl.program_id(0) == 0)
    def _():
        rounded[...] = from_owners(received[:, :, :, :WIDTH]).astype(BF16)

    unit, rate = normalise(volume[...].astype(F32))
    here = grad_mixed[...]
    grad = dot(table_turned[...], rounded[...]) + here
    out[...] = (here + norm_back(grad * gain_one[...], unit, rate)).astype(BF16)


def first_sum_kernel(received, out):
    total = jnp.concatenate([jnp.sum(received[:, core, :, WIDTH:], axis=0) for core in range(2)], axis=1)
    for copy in range(8):
        out[copy] = total


def second_sum_kernel(received, terms, out):
    total = jnp.sum(received[...], axis=0)
    for place in range(PLACES):
        for group in range(3):
            out[place, :, group * WIDTH : (group + 1) * WIDTH] = terms[place, group * 8 : group * 8 + 8, :]
        out[place, :, 3 * WIDTH :] = total


def third_sum_kernel(received, out, slices):
    for group in range(3):
        total = jnp.sum(received[:, :, group * WIDTH : (group + 1) * WIDTH], axis=0)
        for copy in range(8):
            out[copy, group * 8 : group * 8 + 8, :] = total
    slices[...] = received[:, :, 3 * WIDTH :]


def final_kernel(core, received, mine, other, grad_up, grad_down, grad_w_in, grad_w_out, grad_b_in, grad_b_out, grad_one, grad_two, grad_down_bias, grad_up_bias, weights, small):
    parts = [received[2 * y] + received[2 * y + 1] for y in range(4)]
    grad_up[...] = jnp.concatenate(parts[:2], axis=0)
    grad_down[...] = jnp.concatenate(parts[2:], axis=0)
    first = core[0] == 0
    both = (jnp.where(first, mine[...], other[...]), jnp.where(first, other[...], mine[...]))
    for owner in range(GX):
        piece = both[owner % 2][owner // 2]
        for half in range(2):
            lanes = 2 * PAIR * half
            weights[half, owner * 8 : owner * 8 + 8, :] = piece[:, lanes : lanes + PAIR]
            at = GX * 8 + owner * 4
            weights[half, at : at + 4, :] = piece[0:4, lanes + PAIR : lanes + 2 * PAIR]
            if owner * 4 < SMALL:
                small[half, owner * 4 : owner * 4 + 4, :] = piece[4:8, lanes + PAIR : lanes + 2 * PAIR]
    for which, out in enumerate((grad_w_in, grad_w_out)):
        for block in range(BLOCKS):
            at = (which * HALF + block % HALF) * BLOCK
            part = weights[block // HALF, at : at + BLOCK, :]
            out[0, block] = part[:, :BLOCK]
            out[1, block] = part[:, BLOCK:]
    for first_row, out in ((0, grad_b_in), (HALF, grad_b_out)):
        for block in range(BLOCKS):
            row = small[block // HALF, first_row + block % HALF : first_row + block % HALF + 1, :]
            out[block, 0:1, :] = row[:, :BLOCK]
            out[block, 1:2, :] = row[:, BLOCK:]
    tokens = small[0] + small[1]
    low = low_lanes(1)
    for at in range(3):
        even, odd = (small[block // HALF, 6 + block % HALF : 7 + block % HALF, :] for block in (2 * at, 2 * at + 1))
        row = tokens[9 + at : 10 + at, :] + jnp.where(low, even, odd)
        grad_one[at * PAIR : (at + 1) * PAIR] = row[0]
    for first_row, out in ((12, grad_two), (15, grad_down_bias), (18, grad_up_bias)):
        for at in range(out.shape[0] // PAIR):
            out[at * PAIR : (at + 1) * PAIR] = tokens[first_row + at]


def limit(mib):
    return pltpu.CompilerParams(vmem_limit_bytes=mib * MIB)


def call(kernel, out, *operands, mib=12):
    return pl.pallas_call(kernel, out_shape=out, compiler_params=limit(mib))(*operands)


def exchange(value, axis, groups=None):
    return lax.all_to_all(value, axis, split_axis=0, concat_axis=0, axis_index_groups=groups, tiled=True)


def paired(weight, core):
    weight = lax.dynamic_slice_in_dim(weight, core * HALF, HALF, 1)
    top = jnp.concatenate([weight[0], weight[1]], axis=2)
    return jnp.concatenate([top, jnp.concatenate([-weight[1], weight[0]], axis=2)], axis=1)


def paired_bias(bias, core):
    bias = lax.dynamic_slice_in_dim(bias, core * HALF, HALF, 1)
    return bias.transpose(1, 0, 2).reshape(HALF, 1, PAIR)


def local(volume, gain_one, gain_two, w_in, b_in, w_out, b_out, up, up_bias, down, down_bias, cotangent):
    shape = volume.shape
    volume = volume.reshape(TOKENS, WIDTH)
    cotangent = cotangent.reshape(TOKENS, WIDTH)
    gain_one, gain_two, down_bias = (value.reshape(1, WIDTH) for value in (gain_one, gain_two, down_bias))
    slab = slab_table()
    slab_high, slab_low = (jnp.asarray(part) for part in halves(slab))
    slab_turned = jnp.asarray(halves(slab.T)[0])
    cross = [jnp.asarray(part) for table in cross_tables() for part in halves(table)]
    core = lax.axis_index("space") & 1
    w_in, w_out, b_in, b_out = paired(w_in, core), paired(w_out, core), paired_bias(b_in, core), paired_bias(b_out, core)
    gain = lax.dynamic_slice_in_dim(gain_one.reshape(BLOCKS, 1, BLOCK), core * HALF, HALF, 0)
    gain = jnp.broadcast_to(gain, (HALF, 2, BLOCK)).reshape(1, WIDTH)

    def sds(*dims, dtype=F32):
        return jax.ShapeDtypeStruct(dims, dtype)

    def rows(value):
        return value.reshape(2 * MODES, WIDTH)

    def places(value):
        return value.reshape(PLACES, 2, OWN, value.shape[-1])

    def owners(value):
        return value.reshape(GX, OWN, WIDTH)

    wave = sds(PLACES, 2, OWN, WIDTH)
    modes = call(first_kernel, wave, volume, slab_high, slab_low, mib=60)
    modes = rows(exchange(owners(modes), "space"))
    wide = sds(HALF, 2 * MODES, PAIR)
    modes, spectrum, inner, outer = call(
        filter_kernel, (sds(2 * MODES, WIDTH), sds(2 * MODES, WIDTH), wide, wide), modes, *cross, gain, w_in, b_in, w_out, b_out
    )
    modes = places(exchange(owners(modes), "space"))

    def whole(*dims):
        return pl.BlockSpec(dims, lambda step: (0,) * len(dims))

    def chunk(*dims):
        return pl.BlockSpec(dims, lambda step: (step, 0))

    def across(*dims):
        return pl.BlockSpec(dims, lambda step: (0, step))

    mixed, inputs, hidden, grad_before, grad_mixed, modes, up_sum, sums = call(
        mlp_kernel,
        (
            sds(TOKENS, WIDTH), sds(TOKENS, WIDTH, dtype=BF16), sds(TOKENS, HIDDEN, dtype=BF16), sds(TOKENS, HIDDEN, dtype=BF16),
            sds(TOKENS, WIDTH), wave, sds(8, HIDDEN), sds(8, WIDTH),
        ),
        volume, cotangent, modes, slab_high, slab_turned, gain_one, gain_two, up, up_bias.reshape(1, HIDDEN), down,
        mib=60,
    )

    terms = pl.pallas_call(
        weight_kernel,
        grid=(HIDDEN // WBLOCK,),
        in_specs=[whole(TOKENS, WIDTH), whole(TOKENS, WIDTH), across(TOKENS, WBLOCK), across(TOKENS, WBLOCK)],
        out_specs=pl.BlockSpec((4, 2, WBLOCK // 96, 24, WIDTH), lambda step: (0, 0, step, 0, 0)),
        out_shape=sds(4, 2, PLACES, 24, WIDTH),
        compiler_params=limit(60),
        cost_estimate=pl.CostEstimate(flops=4 * TOKENS * WIDTH * HIDDEN, bytes_accessed=12 * MIB, transcendentals=0),
    )(inputs, cotangent, hidden, grad_before)
    result = pl.pallas_call(
        result_kernel,
        grid=(TOKENS // CHUNK,),
        in_specs=[chunk(CHUNK, WIDTH), chunk(CHUNK, HIDDEN), whole(HIDDEN, WIDTH), whole(1, WIDTH)],
        out_specs=chunk(CHUNK, WIDTH),
        out_shape=sds(TOKENS, WIDTH, dtype=BF16),
        compiler_params=limit(60),
        cost_estimate=pl.CostEstimate(flops=2 * TOKENS * WIDTH * HIDDEN, bytes_accessed=7 * MIB, transcendentals=0),
    )(mixed, hidden, down, down_bias)

    modes = exchange(owners(modes), "space")
    terms = lax.psum_scatter(
        terms.reshape(8, PLACES * 24, WIDTH), ("dp", "space"), scatter_dimension=0, axis_index_groups=Y_CORE, tiled=True
    ).reshape(PLACES, 24, WIDTH)
    modes = rows(modes)
    carried = 2 * PAIR
    sent = pl.pallas_call(
        filter_back_kernel,
        out_shape=sds(GX, 8, WIDTH + carried),
        scratch_shapes=[pltpu.VMEM((2 * HALF, BLOCK, PAIR), F32), pltpu.VMEM((SMALL, PAIR), F32)],
        compiler_params=limit(12),
        cost_estimate=pl.CostEstimate(flops=LATE, bytes_accessed=8 * MIB, transcendentals=0),
    )(modes, *cross, gain, w_in, w_out, spectrum, inner, outer, sums, up_sum)
    received = places(exchange(sent, "space"))
    shared = exchange(call(first_sum_kernel, sds(8, 8, 2 * carried), received), "dp")
    grad_volume = pl.pallas_call(
        last_kernel,
        grid=(TOKENS // CHUNK,),
        in_specs=[
            chunk(CHUNK, WIDTH), whole(PLACES, 2, OWN, WIDTH + carried), chunk(CHUNK, 2 * MODES), whole(1, WIDTH), chunk(CHUNK, WIDTH),
        ],
        out_specs=chunk(CHUNK, WIDTH),
        out_shape=sds(TOKENS, WIDTH, dtype=BF16),
        scratch_shapes=[pltpu.VMEM((2 * MODES, WIDTH), BF16)],
        compiler_params=limit(12),
        cost_estimate=pl.CostEstimate(flops=TOKENS * WIDTH * 1024, bytes_accessed=8 * 1024 * 1024, transcendentals=0),
    )(volume, received, slab_turned, gain_one, grad_mixed)
    gathered = exchange(call(second_sum_kernel, sds(PLACES, 8, 3 * WIDTH + 2 * carried), shared, terms), "space", X_Z)
    copies, mine = call(third_sum_kernel, (sds(8, 24, WIDTH), sds(PLACES, 8, 2 * carried)), gathered)
    other = lax.ppermute(mine, "space", [(at, at ^ 1) for at in range(GX)])
    copies = exchange(copies, "dp")
    square = sds(2, BLOCKS, BLOCK, BLOCK)
    vmem = pl.BlockSpec(memory_space=pltpu.VMEM)
    tall = sds(BLOCKS, 2, BLOCK)
    row = sds(WIDTH)
    grad_up, grad_down, grad_w_in, grad_w_out, grad_b_in, grad_b_out, grad_one, grad_two, grad_down_bias, grad_up_bias = pl.pallas_call(
        final_kernel,
        in_specs=[pl.BlockSpec(memory_space=pltpu.SMEM), vmem, vmem, vmem],
        out_shape=(sds(48, WIDTH), sds(48, WIDTH), square, square, tall, tall, row, row, row, sds(HIDDEN)),
        scratch_shapes=[pltpu.VMEM((2, 2 * HALF * BLOCK, PAIR), F32), pltpu.VMEM((2, SMALL, PAIR), F32)],
        compiler_params=limit(8),
    )(core.reshape(1), copies, mine, other)
    return (
        result.reshape(shape),
        grad_volume.reshape(shape),
        grad_one,
        grad_two,
        grad_w_in,
        grad_b_in.transpose(1, 0, 2),
        grad_w_out,
        grad_b_out.transpose(1, 0, 2),
        grad_up.T,
        grad_up_bias,
        grad_down,
        grad_down_bias,
    )


def solution(mesh):
    field = P("dp", "space", None, None, None)
    return jax.shard_map(
        local,
        mesh=mesh,
        in_specs=(field,) + (P(),) * 10 + (field,),
        out_specs=(field, field) + (P(),) * 6 + (P(None, "space"), P(), P("space", None), P()),
        check_vma=False,
    )
```

time: 195 us -> 188 us (0.964)
  local copies, waits for them, and re-layouts: 12.3 us -> 4.53 us
  blocking collectives: 68.9 us -> 61.5 us
  Pallas kernels: 34.7 us -> 37.7 us
  starting transfers between devices: 25.8 us -> 28.3 us
    unnamed x56 -> x40, local copies, waits for them, and re-layouts: 9.93 us -> 1.89 us
    all_to_all x3, blocking collectives: 68.9 us -> 61.5 us  [exchange(): lax.all_to_all(value, axis, split_axis=0, concat_axis=0, axis_index_group...]
    pallas_call x6 -> x7, Pallas kernels: 18.6 us -> 24.5 us  [the longest x6 19.6 us: call(): pl.pallas_call(kernel, out_shape=out, compiler_params=limit(mib))(*operands)]
    pallas_call x1, Pallas kernels: 11.2 us -> 7.42 us  [local(): pl.pallas_call(weight_kernel, grid=(HIDDEN // WBLOCK,), in_specs=[whole(T...]
    all_to_all x4, starting transfers between devices: 25.8 us -> 27.8 us  [exchange(): lax.all_to_all(value, axis, split_axis=0, concat_axis=0, axis_index_group...]
  transfers between devices with their start and end apart: 6 -> 6, of which waited for: 4 -> 3; matrix products, arithmetic and copies ran while one was open for 1% -> 2% of each run, Pallas kernels for 8% -> 9%
where the time goes in v3:
time: 188 us; the launch traced here: 186 us
  blocking collectives  61.5 us (33%)
  waiting for transfers between devices  39 us (21%)
  Pallas kernels  37.7 us (20%)
  starting transfers between devices  28.3 us (15%)
  between operations  14.2 us (8%)
  local copies, waits for them, and re-layouts  4.53 us (2%)
    all_to_all x3, blocking collectives, exchange(): lax.all_to_all(value, axis, split_axis=0, concat_axis=0, axis_index_group...  61.5 us
    all_to_all x4, waiting for transfers between devices, exchange(): lax.all_to_all(value, axis, split_axis=0, concat_axis=0, axis_index_group...  39 us
    all_to_all x4, starting transfers between devices, exchange(): lax.all_to_all(value, axis, split_axis=0, concat_axis=0, axis_index_group...  27.8 us
    pallas_call x6, Pallas kernels, call(): pl.pallas_call(kernel, out_shape=out, compiler_params=limit(mib))(*operands)  19.6 us
    pallas_call x1, Pallas kernels, local(): pl.pallas_call(weight_kernel, grid=(HIDDEN // WBLOCK,), in_specs=[whole(T...  7.42 us
    pallas_call x1, Pallas kernels, local(): pl.pallas_call(result_kernel, grid=(TOKENS // CHUNK,), in_specs=[chunk(CH...  4.9 us
  transfers between devices with their start and end apart: 6, of which 3 were waited for; matrix products, arithmetic and copies ran while one was open for 2% of the time, Pallas kernels for 9%

profile of v3, /device:TPU:32, one launch (start us, length us, event | category | flops | bytes accessed | tf_op | source)
XLA Modules:
  0.0 185.5 jit_solution(14040234885691405557)
XLA Ops:
  7.2 0.0 copy-start.14
  7.2 0.0 copy-start.18
  7.2 0.0 copy-start.19
  7.2 3.9 %shard_map.274 = f32[16,2,8,384]{3,2,1,0:T(8,128)} custom-call(bf16[1024,384]{1,0:T(8,128)(2,1)} %bitcast.33, bf16[256,1024]{1,0:T(8,128)(2,1)} %constant.26.clone.table_high.table, bf16[256,1024]{1,0:T(8,128)(2,1)} %constant.27.clone.table_low), custom_call_target="tpu_custom_call" | custom-call | tf_op jit(solution)/shard_map/pallas_call | solution.py:354
  11.1 10.6 %all-to-all-start = ((f32[32,8,384]{2,1,0:T(8,128)}), f32[32,8,384]{2,1,0:T(8,128)S(1)}, u32[]{:S(2)}, u32[]{:S(2)}) async-start(f32[32,8,384]{2,1,0:T(8,128)} %bitcast.45), calls=%async_computation | async-start | bytes 786432 | tf_op jit(solution)/shard_map/all_to_all | solution.py:358
  21.7 0.1 reshape_reshape.3
  21.8 0.1 reshape.91.gain
  21.9 0.1 reshape.92.b_in
  22.0 0.1 reshape.93.b_out
  22.1 0.0 copy-start.16
  22.1 0.0 copy-start.15
  22.2 0.1 maximum_maximum_fusion.w_in
  22.3 0.1 maximum_maximum_fusion.1.w_out
  22.4 15.7 %all-to-all-done = f32[32,8,384]{2,1,0:T(8,128)S(1)} async-done(((f32[32,8,384]{2,1,0:T(8,128)}), f32[32,8,384]{2,1,0:T(8,128)S(1)}, u32[]{:S(2)}, u32[]{:S(2)}) %all-to-all-start) | async-done | bytes 393248 | tf_op jit(solution)/shard_map/all_to_all | solution.py:358
  38.1 0.0 copy-done.5
  38.1 2.9 %shard_map.275 = (f32[256,384]{1,0:T(8,128)}, f32[256,384]{1,0:T(8,128)S(1)}, f32[3,256,128]{2,1,0:T(8,128)S(1)}, f32[3,256,128]{2,1,0:T(8,128)S(1)}) custom-call(f32[256,384]{1,0:T(8,128)S(1)} %bitcast.38, bf16[256,256]{1,0:T(8,128)(2,1)S(1)} %copy-done.4, bf16[256,256]{1,0:T(8,128)(2,1)S(1)} %copy-done.5, bf16[256,256]{1,0:T(8,128)(2,1)S(1)} %copy-done.6, ...), custom_call_target="tpu_custom_call" | custom-call | tf_op jit(solution)/shard_map/pallas_call | solution.py:354
  41.0 4.1 %all-to-all-start.1 = ((f32[32,8,384]{2,1,0:T(8,128)}), f32[32,8,384]{2,1,0:T(8,128)S(1)}, u32[]{:S(2)}, u32[]{:S(2)}) async-start(f32[32,8,384]{2,1,0:T(8,128)} %bitcast.11), calls=%async_computation.1 | async-start | bytes 786432 | tf_op jit(solution)/shard_map/all_to_all | solution.py:358
  45.1 0.6 reshape.96.gain_one
  45.7 0.6 reshape.97.gain_two
  46.2 0.0 copy-done.15
  46.2 0.6 reshape.98.up_bias
  46.8 14.4 %all-to-all-done.1 = f32[32,8,384]{2,1,0:T(8,128)S(1)} async-done(((f32[32,8,384]{2,1,0:T(8,128)}), f32[32,8,384]{2,1,0:T(8,128)S(1)}, u32[]{:S(2)}, u32[]{:S(2)}) %all-to-all-start.1) | async-done | bytes 393248 | tf_op jit(solution)/shard_map/all_to_all | solution.py:358
  61.3 0.7 copy-done.11
  62.0 11.9 %shard_map.276 = (f32[1024,384]{1,0:T(8,128)}, bf16[1024,384]{1,0:T(8,128)(2,1)}, bf16[1024,1536]{1,0:T(8,128)(2,1)}, bf16[1024,1536]{1,0:T(8,128)(2,1)}, f32[10...) custom-call(bf16[1024,384]{1,0:T(8,128)(2,1)} %bitcast.34, ...), custom_call_target="tpu_custom_call" | custom-call | tf_op jit(solution)/shard_map/pallas_call | solution.py:354
  73.9 3.9 %all-to-all-start.2 = ((f32[32,8,384]{2,1,0:T(8,128)}), f32[32,8,384]{2,1,0:T(8,128)S(1)}, u32[]{:S(2)}, u32[]{:S(2)}) async-start(f32[32,8,384]{2,1,0:T(8,128)} %bitcast.48), calls=%async_computation.2 | async-start | bytes 786432 | tf_op jit(solution)/shard_map/all_to_all | solution.py:358
  77.8 0.0 reduce-scatter.2.cloned.1.call-start
  77.8 7.4 %shard_map.281 = f32[4,2,16,24,384]{4,3,2,1,0:T(8,128)} custom-call(bf16[1024,384]{1,0:T(8,128)(2,1)} %get-tuple-element.46.inputs, bf16[1024,384]{1,0:T(8,128)(2,1)} %bitcast.43, bf16[1024,1536]{1,0:T(8,128)(2,1)} %get-tuple-element.38.hidden, bf16[1024,1536]{1,0:T(8,128)(2,1)} %get-tuple-element.47.grad_before), custom_call_target="tpu_custom_call" | custom-call | flops 2415919104 | bytes 12582912 | tf_op jit(solution)/shard_map/pallas_call | solution.py:426
  85.3 0.0 reduce-scatter.2.cloned.1.call-update
  85.3 8.9 %all-to-all-done.2 = f32[32,8,384]{2,1,0:T(8,128)S(1)} async-done(((f32[32,8,384]{2,1,0:T(8,128)}), f32[32,8,384]{2,1,0:T(8,128)S(1)}, u32[]{:S(2)}, u32[]{:S(2)}) %all-to-all-start.2) | async-done | bytes 393248 | tf_op jit(solution)/shard_map/all_to_all | solution.py:358
  94.2 0.0 copy-done.10
  94.2 1.7 shard_map.278
  95.9 25.0 %all_to_all.35 = f32[32,8,640]{2,1,0:T(8,128)S(1)} all-to-all(f32[32,8,640]{2,1,0:T(8,128)S(1)} %shard_map.278), channel_id=1, replica_groups=mesh['dp'=8,'space'=32] {'space'}, dimensions={0} | all-to-all | bytes 1310720 | tf_op jit(solution)/shard_map/all_to_all | solution.py:358
  120.9 11.2 %all_to_all.36.received = f32[8,8,512]{2,1,0:T(8,128)S(1)} all-to-all(f32[8,8,512]{2,1,0:T(8,128)S(1)} %shard_map.280), channel_id=1, replica_groups=mesh['dp'=8,'space'=32] {'dp'}, dimensions={0} | all-to-all | bytes 262144 | tf_op jit(solution)/shard_map/all_to_all | solution.py:358
  132.1 1.1 copy-done.3
  133.2 0.1 shard_map.282
  133.2 0.0 copy-start.17
  133.3 25.3 %all_to_all.37.received = f32[16,8,1664]{2,1,0:T(8,128)S(1)} all-to-all(f32[16,8,1664]{2,1,0:T(8,128)S(1)} %shard_map.282), channel_id=1, replica_groups={{0,2,4,6,8,10,12,14,16,18,20,22,24,26,28,30},{1,3,5,7,9,11,13,15,17,19,..., dimensions={0} | all-to-all | bytes 1703936 | tf_op jit(solution)/shard_map/all_to_all | solution.py:358
  158.6 0.8 shard_map.283
  159.4 9.3 %all-to-all-start.6 = ((f32[8,24,384]{2,1,0:T(8,128)}), f32[8,24,384]{2,1,0:T(8,128)S(1)}, u32[]{:S(2)}, u32[]{:S(2)}) async-start(f32[8,24,384]{2,1,0:T(8,128)} %get-tuple-element.48), calls=%async_computation.7 | async-start | bytes 589824 | tf_op jit(solution)/shard_map/all_to_all | solution.py:358
  168.7 0.4 collective-permute-start
  169.1 0.6 reshape.99.down_bias
  169.7 4.9 %shard_map.277 = bf16[1024,384]{1,0:T(8,128)(2,1)} custom-call(f32[1024,384]{1,0:T(8,128)} %get-tuple-element.37.mixed, bf16[1024,1536]{1,0:T(8,128)(2,1)} %get-tuple-element.38.hidden, bf16[1536,384]{1,0:T(8,128)(2,1)} %down.3, f32[1,384]{1,0:T(1,128)} %reshape.99.down_bias), custom_call_target="tpu_custom_call" | custom-call | flops 1207959552 | bytes 7340032 | tf_op jit(solution)/shard_map/pallas_call | solution.py:435
  174.6 0.0 copy-done.2
  174.6 0.0 copy-done.8
  174.6 2.1 %shard_map.279 = bf16[1024,384]{1,0:T(8,128)(2,1)} custom-call(bf16[1024,384]{1,0:T(8,128)(2,1)S(1)} %bitcast.35, f32[16,2,8,640]{3,2,1,0:T(8,128)S(1)} %bitcast.37, bf16[1024,256]{1,0:T(8,128)(2,1)S(1)} %copy-done.1, f32[1,384]{1,0:T(1,128)S(1)} %copy-done.8, f32[1024,384]{1,0:T(8,128)S(1)} %copy-done.2), custom_call_target="tpu_custom_call" | custom-call | flops 402653184 | bytes 8388608 | tf_op jit(solution)/shard_map/pallas_call | solution.py:460
  176.7 0.0 collective-permute-done.other
  176.7 0.0 all-to-all-done.6.received
  176.7 2.0 %shard_map.284 = (f32[48,384]{1,0:T(8,128)}, f32[48,384]{1,0:T(8,128)}, f32[2,6,64,64]{3,2,1,0:T(8,128)}, f32[2,6,64,64]{3,2,1,0:T(8,128)}, f32[6,2,64]{2,1,0:T(...) custom-call(s32[1]{0:T(128)} %bitcast.18.core, ...), custom_call_target="tpu_custom_call" | custom-call | tf_op jit(solution)/shard_map/pallas_call | solution.py:480
  (34 shorter events, 0.1 us)
Async XLA Ops:
  7.2 14.5 %copy-start.14 = (f32[384]{0:T(512)S(1)}, f32[384]{0:T(512)}, u32[]{:S(2)}) copy-start(f32[384]{0:T(512)} %param.20) | copy-start | bytes 4612
  7.2 14.7 %copy-start.18 = (f32[2,6,64]{2,0,1:T(2,128)S(1)}, f32[2,6,64]{2,0,1:T(2,128)}, u32[]{:S(2)}) copy-start(f32[2,6,64]{2,0,1:T(2,128)} %param.25) | copy-start | bytes 9220
  7.2 14.7 %copy-start.19 = (f32[2,6,64]{2,0,1:T(2,128)S(1)}, f32[2,6,64]{2,0,1:T(2,128)}, u32[]{:S(2)}) copy-start(f32[2,6,64]{2,0,1:T(2,128)} %param.23) | copy-start | bytes 9220
  7.2 14.9 %copy-start.12 = (f32[2,6,64,64]{3,2,1,0:T(8,128)S(1)}, f32[2,6,64,64]{3,2,1,0:T(8,128)}, u32[]{:S(2)}) copy-start(f32[2,6,64,64]{3,2,1,0:T(8,128)} %param.24) | copy-start | bytes 589828
  7.2 14.8 %copy-start.13 = (f32[2,6,64,64]{3,2,1,0:T(8,128)S(1)}, f32[2,6,64,64]{3,2,1,0:T(8,128)}, u32[]{:S(2)}) copy-start(f32[2,6,64,64]{3,2,1,0:T(8,128)} %param.22) | copy-start | bytes 589828
  11.1 27.0 %copy-start.4 = (bf16[256,256]{1,0:T(8,128)(2,1)S(1)}, bf16[256,256]{1,0:T(8,128)(2,1)}, u32[]{:S(2)}) copy-start(bf16[256,256]{1,0:T(8,128)(2,1)} %constant.29.clone.cos_high) | copy-start | bytes 393220
  11.1 27.0 %copy-start.5 = (bf16[256,256]{1,0:T(8,128)(2,1)S(1)}, bf16[256,256]{1,0:T(8,128)(2,1)}, u32[]{:S(2)}) copy-start(bf16[256,256]{1,0:T(8,128)(2,1)} %constant.30.clone.cos_low) | copy-start | bytes 393220
  11.1 27.0 %copy-start.6 = (bf16[256,256]{1,0:T(8,128)(2,1)S(1)}, bf16[256,256]{1,0:T(8,128)(2,1)}, u32[]{:S(2)}) copy-start(bf16[256,256]{1,0:T(8,128)(2,1)} %constant.31.clone.sin_high) | copy-start | bytes 393220
  11.1 27.0 %copy-start.7 = (bf16[256,256]{1,0:T(8,128)(2,1)S(1)}, bf16[256,256]{1,0:T(8,128)(2,1)}, u32[]{:S(2)}) copy-start(bf16[256,256]{1,0:T(8,128)(2,1)} %constant.32.clone.sin_low) | copy-start | bytes 393220
  11.1 27.0 %all-to-all-start = ((f32[32,8,384]{2,1,0:T(8,128)}), f32[32,8,384]{2,1,0:T(8,128)S(1)}, u32[]{:S(2)}, u32[]{:S(2)}) async-start(f32[32,8,384]{2,1,0:T(8,128)} %bitcast.45), calls=%async_computation | async-start | bytes 786432 | tf_op jit(solution)/shard_map/all_to_all | solution.py:358
  22.1 23.5 %copy-start.16 = (f32[384]{0:T(512)S(1)}, f32[384]{0:T(512)}, u32[]{:S(2)}) copy-start(f32[384]{0:T(512)} %param.21) | copy-start | bytes 4612
  22.1 24.1 %copy-start.15 = (f32[1536]{0:T(1024)S(1)}, f32[1536]{0:T(1024)}, u32[]{:S(2)}) copy-start(f32[1536]{0:T(1024)} %param.27) | copy-start | bytes 18436
  41.0 20.2 %all-to-all-start.1 = ((f32[32,8,384]{2,1,0:T(8,128)}), f32[32,8,384]{2,1,0:T(8,128)S(1)}, u32[]{:S(2)}, u32[]{:S(2)}) async-start(f32[32,8,384]{2,1,0:T(8,128)} %bitcast.11), calls=%async_computation.1 | async-start | bytes 786432 | tf_op jit(solution)/shard_map/all_to_all | solution.py:358
  61.3 0.7 copy-start.11
  73.9 20.3 %all-to-all-start.2 = ((f32[32,8,384]{2,1,0:T(8,128)}), f32[32,8,384]{2,1,0:T(8,128)S(1)}, u32[]{:S(2)}, u32[]{:S(2)}) async-start(f32[32,8,384]{2,1,0:T(8,128)} %bitcast.48), calls=%async_computation.2 | async-start | bytes 786432 | tf_op jit(solution)/shard_map/all_to_all | solution.py:358
  77.8 54.3 %reduce-scatter.2.cloned.1.call-start = ((), (), s32[]{:S(2)}) async-start(), calls=%async_computation.8 | async-start | bytes 5308416 | tf_op jit(solution)/shard_map/reduce_scatter | solution.py:446
  85.3 8.9 %copy-start.9 = (f32[8,1536]{1,0:T(8,128)S(1)}, f32[8,1536]{1,0:T(8,128)}, u32[]{:S(2)}) copy-start(f32[8,1536]{1,0:T(8,128)} %get-tuple-element.44.up_sum) | copy-start | bytes 147460
  85.3 8.9 %copy-start.10 = (f32[8,384]{1,0:T(8,128)S(1)}, f32[8,384]{1,0:T(8,128)}, u32[]{:S(2)}) copy-start(f32[8,384]{1,0:T(8,128)} %get-tuple-element.43.sums) | copy-start | bytes 36868
  132.1 1.1 copy-start.3
  133.2 35.9 %copy-start.17 = (f32[384]{0:T(512)S(1)}, f32[384]{0:T(512)}, u32[]{:S(2)}) copy-start(f32[384]{0:T(512)} %param.29) | copy-start | bytes 4612
  159.4 17.3 %all-to-all-start.6 = ((f32[8,24,384]{2,1,0:T(8,128)}), f32[8,24,384]{2,1,0:T(8,128)S(1)}, u32[]{:S(2)}, u32[]{:S(2)}) async-start(f32[8,24,384]{2,1,0:T(8,128)} %get-tuple-element.48), calls=%async_computation.7 | async-start | bytes 589824 | tf_op jit(solution)/shard_map/all_to_all | solution.py:358
  168.7 8.0 %collective-permute-start = (f32[16,8,512]{2,1,0:T(8,128)S(1)}, f32[16,8,512]{2,1,0:T(8,128)}, u32[]{:S(2)}, u32[]{:S(2)}) collective-permute-start(f32[16,8,512]{2,1,0:T(8,128)S(1)} %get-tuple-element.49.mine), channel_id=1, source_target_pairs={{0,1},{1,0},{2,3},{3,2},{4,5},{5,4},{6,7},{7,6},{8,9},{9,8},{10,11... | collective-permute-start | bytes 786440 | tf_op jit(solution)/shard_map/ppermute | solution.py:474
  169.7 4.9 %copy-start = (bf16[1,1,32,32,384]{4,3,2,1,0:T(8,128)(2,1)S(1)}, bf16[1,1,32,32,384]{4,3,2,1,0:T(8,128)(2,1)}, u32[]{:S(2)}) copy-start(bf16[1,1,32,32,384]{4,3,2,1,0:T(8,128)(2,1)} %param.19) | copy-start | bytes 2359300
  169.7 4.9 %copy-start.1 = (bf16[1024,256]{1,0:T(8,128)(2,1)S(1)}, bf16[1024,256]{1,0:T(8,128)(2,1)}, u32[]{:S(2)}) copy-start(bf16[1024,256]{1,0:T(8,128)(2,1)} %constant.28.clone.table_turned) | copy-start | bytes 1572868
  169.7 4.9 %copy-start.2 = (f32[1024,384]{1,0:T(8,128)S(1)}, f32[1024,384]{1,0:T(8,128)}, u32[]{:S(2)}) copy-start(f32[1024,384]{1,0:T(8,128)} %get-tuple-element.45.grad_mixed) | copy-start | bytes 4718596
  169.7 4.9 %copy-start.8 = (f32[1,384]{1,0:T(1,128)S(1)}, f32[1,384]{1,0:T(1,128)}, u32[]{:S(2)}) copy-start(f32[1,384]{1,0:T(1,128)} %reshape.96.gain_one) | copy-start | bytes 4612
Sparse Core Ops, SparseCore 0:
  85.4 44.0 reduce-scatter.1

commit v4 on v3

--- a/solution.py
+++ b/solution.py
@@ -161,6 +161,12 @@
     return straight + crossed if sign < 0 else straight - crossed
 
 
+def along_x_rounded(tables, value, sign):
+    straight = dot(tables[0][...], value.astype(BF16))
+    crossed = dot(tables[1][...], times_minus_i(value).astype(BF16))
+    return straight + crossed if sign < 0 else straight - crossed
+
+
 def first_kernel(volume, table_high, table_low, out):
     unit, _ = normalise(volume[...].astype(F32))
     to_owners(dot3(table_high[...], table_low[...], unit), out)
@@ -177,7 +183,7 @@
         after = dot6(gelu(before), w_out[block]) + b_out[block]
         outer[block] = after
         shrunk.append(after - jnp.clip(after, -SHRINK, SHRINK))
-    sent[...] = along_x(tables, jnp.concatenate(shrunk, axis=1), 1)
+    sent[...] = along_x_rounded((cos_high, sin_high), jnp.concatenate(shrunk, axis=1), 1)
 
 
 def packed_weight(grad):
@@ -188,13 +194,13 @@
 SMALL = 32
 
 
-def filter_back_kernel(received, cos_high, cos_low, sin_high, sin_low, gain, w_in, w_out, spectrum, inner, outer, sums, up_sum, sent, weights, small):
-    tables = (cos_high, cos_low, sin_high, sin_low)
+def filter_back_kernel(received, cos, sin, gain, w_in, w_out, spectrum, inner, outer, sums, up_sum, sent, weights, small):
+    tables = (cos, sin)
     unit_spectrum = spectrum[...]
     small[...] = jnp.zeros_like(small)
     grads = []
     scaled = tiles(unit_spectrum * gain[...])
-    for block, grad_out in enumerate(tiles(along_x(tables, received[...], -1))):
+    for block, grad_out in enumerate(tiles(along_x_rounded(tables, received[...], -1))):
         grad_out = jnp.where(jnp.abs(outer[block]) > SHRINK, grad_out, 0.0)
         active, slope = gelu_parts(inner[block])
         small[HALF + block : HALF + block + 1, :] = jnp.sum(grad_out, axis=0, keepdims=True)
@@ -216,7 +222,7 @@
         small[15 + at : 16 + at, :] = sums[2:3, lanes]
     for at in range(HIDDEN // PAIR):
         small[18 + at : 19 + at, :] = up_sum[0:1, at * PAIR : (at + 1) * PAIR]
-    sent[:, :, :WIDTH] = along_x(tables, grad, 1).reshape(GX, 8, WIDTH)
+    sent[:, :, :WIDTH] = along_x_rounded(tables, grad, 1).reshape(GX, 8, WIDTH)
     for owner in range(GX):
         at = owner * 8
         sent[owner, :, WIDTH : WIDTH + PAIR] = weights[at // BLOCK, at % BLOCK : at % BLOCK + 8, :]
@@ -309,10 +315,13 @@
     slices[...] = received[:, :, 3 * WIDTH :]
 
 
-def final_kernel(core, received, mine, other, grad_up, grad_down, grad_w_in, grad_w_out, grad_b_in, grad_b_out, grad_one, grad_two, grad_down_bias, grad_up_bias, weights, small):
+def weight_sum_kernel(received, grad_up, grad_down):
     parts = [received[2 * y] + received[2 * y + 1] for y in range(4)]
     grad_up[...] = jnp.concatenate(parts[:2], axis=0)
     grad_down[...] = jnp.concatenate(parts[2:], axis=0)
+
+
+def final_kernel(core, mine, other, grad_w_in, grad_w_out, grad_b_in, grad_b_out, grad_one, grad_two, grad_down_bias, grad_up_bias, weights, small):
     first = core[0] == 0
     both = (jnp.where(first, mine[...], other[...]), jnp.where(first, other[...], mine[...]))
     for owner in range(GX):
@@ -454,7 +463,7 @@
         scratch_shapes=[pltpu.VMEM((2 * HALF, BLOCK, PAIR), F32), pltpu.VMEM((SMALL, PAIR), F32)],
         compiler_params=limit(12),
         cost_estimate=pl.CostEstimate(flops=LATE, bytes_accessed=8 * MIB, transcendentals=0),
-    )(modes, *cross, gain, w_in, w_out, spectrum, inner, outer, sums, up_sum)
+    )(modes, cross[0], cross[2], gain, w_in, w_out, spectrum, inner, outer, sums, up_sum)
     received = places(exchange(sent, "space"))
     shared = exchange(call(first_sum_kernel, sds(8, 8, 2 * carried), received), "dp")
     grad_volume = pl.pallas_call(
@@ -469,6 +478,7 @@
         compiler_params=limit(12),
         cost_estimate=pl.CostEstimate(flops=TOKENS * WIDTH * 1024, bytes_accessed=8 * 1024 * 1024, transcendentals=0),
     )(volume, received, slab_turned, gain_one, grad_mixed)
+    shared, result, grad_volume = lax.optimization_barrier((shared, result, grad_volume))
     gathered = exchange(call(second_sum_kernel, sds(PLACES, 8, 3 * WIDTH + 2 * carried), shared, terms), "space", X_Z)
     copies, mine = call(third_sum_kernel, (sds(8, 24, WIDTH), sds(PLACES, 8, 2 * carried)), gathered)
     other = lax.ppermute(mine, "space", [(at, at ^ 1) for at in range(GX)])
@@ -477,13 +487,14 @@
     vmem = pl.BlockSpec(memory_space=pltpu.VMEM)
     tall = sds(BLOCKS, 2, BLOCK)
     row = sds(WIDTH)
-    grad_up, grad_down, grad_w_in, grad_w_out, grad_b_in, grad_b_out, grad_one, grad_two, grad_down_bias, grad_up_bias = pl.pallas_call(
+    grad_up, grad_down = call(weight_sum_kernel, (sds(48, WIDTH), sds(48, WIDTH)), copies)
+    grad_w_in, grad_w_out, grad_b_in, grad_b_out, grad_one, grad_two, grad_down_bias, grad_up_bias = pl.pallas_call(
         final_kernel,
-        in_specs=[pl.BlockSpec(memory_space=pltpu.SMEM), vmem, vmem, vmem],
-        out_shape=(sds(48, WIDTH), sds(48, WIDTH), square, square, tall, tall, row, row, row, sds(HIDDEN)),
+        in_specs=[pl.BlockSpec(memory_space=pltpu.SMEM), vmem, vmem],
+        out_shape=(square, square, tall, tall, row, row, row, sds(HIDDEN)),
         scratch_shapes=[pltpu.VMEM((2, 2 * HALF * BLOCK, PAIR), F32), pltpu.VMEM((2, SMALL, PAIR), F32)],
-        compiler_params=limit(8),
-    )(core.reshape(1), copies, mine, other)
+        compiler_params=limit(60),
+    )(core.reshape(1), mine, other)
     return (
         result.reshape(shape),
         grad_volume.reshape(shape),

time: 188 us -> 185 us (0.984); the launches traced: 186 us -> 185 us
  blocking collectives: 61.5 us -> 53.2 us
  waiting for transfers between devices: 39 us -> 42.5 us
  starting transfers between devices: 28.3 us -> 30.6 us
    all_to_all x3 -> x2, blocking collectives: 61.5 us -> 53.2 us  [exchange(): lax.all_to_all(value, axis, split_axis=0, concat_axis=0, axis_index_group...]
    all_to_all x4 -> x5, starting transfers between devices: 27.8 us -> 30.6 us  [exchange(): lax.all_to_all(value, axis, split_axis=0, concat_axis=0, axis_index_group...]
    all_to_all x4 -> x5, waiting for transfers between devices: 39 us -> 41 us  [exchange(): lax.all_to_all(value, axis, split_axis=0, concat_axis=0, axis_index_group...]
    pallas_call x6 -> x7, Pallas kernels: 19.6 us -> 20.6 us  [call(): pl.pallas_call(kernel, out_shape=out, compiler_params=limit(mib))(*operands)]
  transfers between devices with their start and end apart: 6 -> 7, of which waited for: 3 -> 5; matrix products, arithmetic and copies ran while one was open for 2% -> 2% of each run, Pallas kernels for 9% -> 10%
where the time goes in v4:
time: 185 us
  blocking collectives  53.2 us (29%)
  waiting for transfers between devices  42.5 us (23%)
  Pallas kernels  38.5 us (21%)
  starting transfers between devices  30.6 us (17%)
  between operations  14.2 us (8%)
  local copies, waits for them, and re-layouts  5.24 us (3%)
    all_to_all x2, blocking collectives, exchange(): lax.all_to_all(value, axis, split_axis=0, concat_axis=0, axis_index_group...  53.2 us
    all_to_all x5, waiting for transfers between devices, exchange(): lax.all_to_all(value, axis, split_axis=0, concat_axis=0, axis_index_group...  41 us
    all_to_all x5, starting transfers between devices, exchange(): lax.all_to_all(value, axis, split_axis=0, concat_axis=0, axis_index_group...  30.6 us
    pallas_call x7, Pallas kernels, call(): pl.pallas_call(kernel, out_shape=out, compiler_params=limit(mib))(*operands)  20.6 us
    pallas_call x1, Pallas kernels, local(): pl.pallas_call(weight_kernel, grid=(HIDDEN // WBLOCK,), in_specs=[whole(T...  7.43 us
    pallas_call x1, Pallas kernels, local(): pl.pallas_call(result_kernel, grid=(TOKENS // CHUNK,), in_specs=[chunk(CH...  4.97 us
  transfers between devices with their start and end apart: 7, of which 5 were waited for; matrix products, arithmetic and copies ran while one was open for 2% of the time, Pallas kernels for 10%

profile of v4, /device:TPU:32, one launch (start us, length us, event | category | flops | bytes accessed | tf_op | source)
XLA Modules:
  0.0 184.5 jit_solution(9453989633958316025)
XLA Ops:
  7.2 0.0 copy-start.16
  7.2 0.0 copy-start.20
  7.2 0.0 copy-start.21
  7.2 0.0 copy-start.14
  7.2 3.9 %shard_map.274 = f32[16,2,8,384]{3,2,1,0:T(8,128)} custom-call(bf16[1024,384]{1,0:T(8,128)(2,1)} %bitcast.33, bf16[256,1024]{1,0:T(8,128)(2,1)} %constant.26.clone.table_high.table, bf16[256,1024]{1,0:T(8,128)(2,1)} %constant.27.clone.table_low), custom_call_target="tpu_custom_call" | custom-call | tf_op jit(solution)/shard_map/pallas_call | solution.py:363
  11.1 10.6 %all-to-all-start = ((f32[32,8,384]{2,1,0:T(8,128)}), f32[32,8,384]{2,1,0:T(8,128)S(1)}, u32[]{:S(2)}, u32[]{:S(2)}) async-start(f32[32,8,384]{2,1,0:T(8,128)} %bitcast.45), calls=%async_computation | async-start | bytes 786432 | tf_op jit(solution)/shard_map/all_to_all | solution.py:367
  21.7 0.1 reshape_reshape.3
  21.8 0.1 reshape.91.gain
  21.9 0.1 reshape.93.b_out
  22.0 0.1 reshape.92.b_in
  22.1 0.0 copy-start.18
  22.1 0.0 copy-start.17
  22.2 0.1 maximum_maximum_fusion.1.w_out
  22.3 0.1 maximum_maximum_fusion.w_in
  22.4 15.7 %all-to-all-done = f32[32,8,384]{2,1,0:T(8,128)S(1)} async-done(((f32[32,8,384]{2,1,0:T(8,128)}), f32[32,8,384]{2,1,0:T(8,128)S(1)}, u32[]{:S(2)}, u32[]{:S(2)}) %all-to-all-start) | async-done | bytes 393248 | tf_op jit(solution)/shard_map/all_to_all | solution.py:367
  38.1 2.7 %shard_map.275 = (f32[256,384]{1,0:T(8,128)}, f32[256,384]{1,0:T(8,128)S(1)}, f32[3,256,128]{2,1,0:T(8,128)S(1)}, f32[3,256,128]{2,1,0:T(8,128)S(1)}) custom-call(f32[256,384]{1,0:T(8,128)S(1)} %bitcast.38, bf16[256,256]{1,0:T(8,128)(2,1)S(1)} %copy-done.6, bf16[256,256]{1,0:T(8,128)(2,1)S(1)} %copy-done.8, bf16[256,256]{1,0:T(8,128)(2,1)S(1)} %copy-done.5, ...), custom_call_target="tpu_custom_call" | custom-call | tf_op jit(solution)/shard_map/pallas_call | solution.py:363
  40.8 4.1 %all-to-all-start.1 = ((f32[32,8,384]{2,1,0:T(8,128)}), f32[32,8,384]{2,1,0:T(8,128)S(1)}, u32[]{:S(2)}, u32[]{:S(2)}) async-start(f32[32,8,384]{2,1,0:T(8,128)} %bitcast.11), calls=%async_computation.1 | async-start | bytes 786432 | tf_op jit(solution)/shard_map/all_to_all | solution.py:367
  44.8 0.6 reshape.96.gain_one
  45.4 0.6 reshape.97.gain_two
  46.0 0.6 reshape.98.up_bias
  46.6 14.4 %all-to-all-done.1 = f32[32,8,384]{2,1,0:T(8,128)S(1)} async-done(((f32[32,8,384]{2,1,0:T(8,128)}), f32[32,8,384]{2,1,0:T(8,128)S(1)}, u32[]{:S(2)}, u32[]{:S(2)}) %all-to-all-start.1) | async-done | bytes 393248 | tf_op jit(solution)/shard_map/all_to_all | solution.py:367
  61.0 0.7 copy-done.12
  61.7 11.9 %shard_map.276 = (f32[1024,384]{1,0:T(8,128)}, bf16[1024,384]{1,0:T(8,128)(2,1)}, bf16[1024,1536]{1,0:T(8,128)(2,1)}, bf16[1024,1536]{1,0:T(8,128)(2,1)}, f32[10...) custom-call(bf16[1024,384]{1,0:T(8,128)(2,1)} %bitcast.34, ...), custom_call_target="tpu_custom_call" | custom-call | tf_op jit(solution)/shard_map/pallas_call | solution.py:363
  73.6 3.9 %all-to-all-start.2 = ((f32[32,8,384]{2,1,0:T(8,128)}), f32[32,8,384]{2,1,0:T(8,128)S(1)}, u32[]{:S(2)}, u32[]{:S(2)}) async-start(f32[32,8,384]{2,1,0:T(8,128)} %bitcast.48), calls=%async_computation.2 | async-start | bytes 786432 | tf_op jit(solution)/shard_map/all_to_all | solution.py:367
  77.5 0.0 reduce-scatter.2.cloned.1.call-start
  77.6 7.4 %shard_map.281 = f32[4,2,16,24,384]{4,3,2,1,0:T(8,128)} custom-call(bf16[1024,384]{1,0:T(8,128)(2,1)} %get-tuple-element.52.inputs, bf16[1024,384]{1,0:T(8,128)(2,1)} %bitcast.43, bf16[1024,1536]{1,0:T(8,128)(2,1)} %get-tuple-element.47.hidden, bf16[1024,1536]{1,0:T(8,128)(2,1)} %get-tuple-element.53.grad_before), custom_call_target="tpu_custom_call" | custom-call | flops 2415919104 | bytes 12582912 | tf_op jit(solution)/shard_map/pallas_call | solution.py:435
  85.0 0.0 reduce-scatter.2.cloned.1.call-update
  85.0 8.8 %all-to-all-done.2 = f32[32,8,384]{2,1,0:T(8,128)S(1)} async-done(((f32[32,8,384]{2,1,0:T(8,128)}), f32[32,8,384]{2,1,0:T(8,128)S(1)}, u32[]{:S(2)}, u32[]{:S(2)}) %all-to-all-start.2) | async-done | bytes 393248 | tf_op jit(solution)/shard_map/all_to_all | solution.py:367
  93.9 1.3 shard_map.277
  95.1 0.0 copy-start.19
  95.2 24.8 %all_to_all.35 = f32[32,8,640]{2,1,0:T(8,128)S(1)} all-to-all(f32[32,8,640]{2,1,0:T(8,128)S(1)} %shard_map.277), channel_id=1, replica_groups=mesh['dp'=8,'space'=32] {'space'}, dimensions={0} | all-to-all | bytes 1310720 | tf_op jit(solution)/shard_map/all_to_all | solution.py:367
  119.9 0.7 shard_map.278
  120.6 5.9 %all-to-all-start.4 = ((f32[8,8,512]{2,1,0:T(8,128)}), f32[8,8,512]{2,1,0:T(8,128)S(1)}, u32[]{:S(2)}, u32[]{:S(2)}) async-start(f32[8,8,512]{2,1,0:T(8,128)} %shard_map.278), calls=%async_computation.4 | async-start | bytes 262144 | tf_op jit(solution)/shard_map/all_to_all | solution.py:367
  126.6 0.6 reshape.102.down_bias
  127.1 5.0 %shard_map.279 = bf16[1024,384]{1,0:T(8,128)(2,1)} custom-call(f32[1024,384]{1,0:T(8,128)} %get-tuple-element.46.mixed, bf16[1024,1536]{1,0:T(8,128)(2,1)} %get-tuple-element.47.hidden, bf16[1536,384]{1,0:T(8,128)(2,1)} %down.3, f32[1,384]{1,0:T(1,128)} %reshape.102.down_bias), custom_call_target="tpu_custom_call" | custom-call | flops 1207959552 | bytes 7340032 | tf_op jit(solution)/shard_map/pallas_call | solution.py:444
  132.1 2.2 %shard_map.280 = bf16[1024,384]{1,0:T(8,128)(2,1)} custom-call(bf16[1024,384]{1,0:T(8,128)(2,1)S(1)} %bitcast.35, f32[16,2,8,640]{3,2,1,0:T(8,128)S(1)} %bitcast.37, bf16[1024,256]{1,0:T(8,128)(2,1)S(1)} %copy-done.1, f32[1,384]{1,0:T(1,128)S(1)} %copy-done.9, f32[1024,384]{1,0:T(8,128)S(1)} %copy-done.2), custom_call_target="tpu_custom_call" | custom-call | flops 402653184 | bytes 8388608 | tf_op jit(solution)/shard_map/pallas_call | solution.py:469
  134.3 0.0 all-to-all-done.4.received
  134.3 1.1 copy-done.3
  135.4 0.1 shard_map.282
  135.4 28.4 %all_to_all.36.received = f32[16,8,1664]{2,1,0:T(8,128)S(1)} all-to-all(f32[16,8,1664]{2,1,0:T(8,128)S(1)} %shard_map.282), channel_id=1, replica_groups={{0,2,4,6,8,10,12,14,16,18,20,22,24,26,28,30},{1,3,5,7,9,11,13,15,17,19,..., dimensions={0} | all-to-all | bytes 1703936 | tf_op jit(solution)/shard_map/all_to_all | solution.py:367
  163.8 0.8 shard_map.283
  164.6 6.1 %all-to-all-start.6 = ((f32[8,24,384]{2,1,0:T(8,128)}), f32[8,24,384]{2,1,0:T(8,128)S(1)}, u32[]{:S(2)}, u32[]{:S(2)}) async-start(f32[8,24,384]{2,1,0:T(8,128)} %get-tuple-element.61), calls=%async_computation.7 | async-start | bytes 589824 | tf_op jit(solution)/shard_map/all_to_all | solution.py:367
  170.7 0.0 collective-permute-start
  170.7 1.5 collective-permute-done.other
  172.3 0.7 copy-done.13
  173.0 2.0 %shard_map.284 = (f32[2,6,64,64]{3,2,1,0:T(8,128)}, f32[2,6,64,64]{3,2,1,0:T(8,128)}, f32[6,2,64]{2,1,0:T(2,128)}, f32[6,2,64]{2,1,0:T(2,128)}, f32[384]{0:T(512...) custom-call(s32[1]{0:T(128)} %bitcast.18.core, f32[16,8,512]{2,1,0:T(8,128)} %copy-done.4, f32[16,8,512]{2,1,0:T(8,128)} %copy-done.13), custom_call_target="tpu_custom_call" | custom-call | tf_op jit(solution)/shard_map/pallas_call | solution.py:491
  175.0 2.0 %all-to-all-done.6.received = f32[8,24,384]{2,1,0:T(8,128)S(1)} async-done(((f32[8,24,384]{2,1,0:T(8,128)}), f32[8,24,384]{2,1,0:T(8,128)S(1)}, u32[]{:S(2)}, u32[]{:S(2)}) %all-to-all-start.6) | async-done | bytes 294944 | tf_op jit(solution)/shard_map/all_to_all | solution.py:367
  177.0 0.7 shard_map.285
  (40 shorter events, 0.1 us)
Async XLA Ops:
  7.2 14.5 %copy-start.16 = (f32[384]{0:T(512)S(1)}, f32[384]{0:T(512)}, u32[]{:S(2)}) copy-start(f32[384]{0:T(512)} %param.20) | copy-start | bytes 4612
  7.2 14.7 %copy-start.20 = (f32[2,6,64]{2,0,1:T(2,128)S(1)}, f32[2,6,64]{2,0,1:T(2,128)}, u32[]{:S(2)}) copy-start(f32[2,6,64]{2,0,1:T(2,128)} %param.25) | copy-start | bytes 9220
  7.2 14.7 %copy-start.21 = (f32[2,6,64]{2,0,1:T(2,128)S(1)}, f32[2,6,64]{2,0,1:T(2,128)}, u32[]{:S(2)}) copy-start(f32[2,6,64]{2,0,1:T(2,128)} %param.23) | copy-start | bytes 9220
  7.2 14.9 %copy-start.14 = (f32[2,6,64,64]{3,2,1,0:T(8,128)S(1)}, f32[2,6,64,64]{3,2,1,0:T(8,128)}, u32[]{:S(2)}) copy-start(f32[2,6,64,64]{3,2,1,0:T(8,128)} %param.24) | copy-start | bytes 589828
  7.2 14.8 %copy-start.15 = (f32[2,6,64,64]{3,2,1,0:T(8,128)S(1)}, f32[2,6,64,64]{3,2,1,0:T(8,128)}, u32[]{:S(2)}) copy-start(f32[2,6,64,64]{3,2,1,0:T(8,128)} %param.22) | copy-start | bytes 589828
  11.1 27.0 %copy-start.5 = (bf16[256,256]{1,0:T(8,128)(2,1)S(1)}, bf16[256,256]{1,0:T(8,128)(2,1)}, u32[]{:S(2)}) copy-start(bf16[256,256]{1,0:T(8,128)(2,1)} %constant.31.clone.sin_high.sin) | copy-start | bytes 393220
  11.1 27.0 %copy-start.6 = (bf16[256,256]{1,0:T(8,128)(2,1)S(1)}, bf16[256,256]{1,0:T(8,128)(2,1)}, u32[]{:S(2)}) copy-start(bf16[256,256]{1,0:T(8,128)(2,1)} %constant.29.clone.cos_high.cos) | copy-start | bytes 393220
  11.1 27.0 %copy-start.7 = (bf16[256,256]{1,0:T(8,128)(2,1)S(1)}, bf16[256,256]{1,0:T(8,128)(2,1)}, u32[]{:S(2)}) copy-start(bf16[256,256]{1,0:T(8,128)(2,1)} %constant.32.clone.sin_low) | copy-start | bytes 393220
  11.1 27.0 %copy-start.8 = (bf16[256,256]{1,0:T(8,128)(2,1)S(1)}, bf16[256,256]{1,0:T(8,128)(2,1)}, u32[]{:S(2)}) copy-start(bf16[256,256]{1,0:T(8,128)(2,1)} %constant.30.clone.cos_low) | copy-start | bytes 393220
  11.1 27.0 %all-to-all-start = ((f32[32,8,384]{2,1,0:T(8,128)}), f32[32,8,384]{2,1,0:T(8,128)S(1)}, u32[]{:S(2)}, u32[]{:S(2)}) async-start(f32[32,8,384]{2,1,0:T(8,128)} %bitcast.45), calls=%async_computation | async-start | bytes 786432 | tf_op jit(solution)/shard_map/all_to_all | solution.py:367
  22.1 23.3 %copy-start.18 = (f32[384]{0:T(512)S(1)}, f32[384]{0:T(512)}, u32[]{:S(2)}) copy-start(f32[384]{0:T(512)} %param.21) | copy-start | bytes 4612
  22.1 23.8 %copy-start.17 = (f32[1536]{0:T(1024)S(1)}, f32[1536]{0:T(1024)}, u32[]{:S(2)}) copy-start(f32[1536]{0:T(1024)} %param.27) | copy-start | bytes 18436
  40.8 20.2 %all-to-all-start.1 = ((f32[32,8,384]{2,1,0:T(8,128)}), f32[32,8,384]{2,1,0:T(8,128)S(1)}, u32[]{:S(2)}, u32[]{:S(2)}) async-start(f32[32,8,384]{2,1,0:T(8,128)} %bitcast.11), calls=%async_computation.1 | async-start | bytes 786432 | tf_op jit(solution)/shard_map/all_to_all | solution.py:367
  61.0 0.7 copy-start.12
  73.6 20.2 %all-to-all-start.2 = ((f32[32,8,384]{2,1,0:T(8,128)}), f32[32,8,384]{2,1,0:T(8,128)S(1)}, u32[]{:S(2)}, u32[]{:S(2)}) async-start(f32[32,8,384]{2,1,0:T(8,128)} %bitcast.48), calls=%async_computation.2 | async-start | bytes 786432 | tf_op jit(solution)/shard_map/all_to_all | solution.py:367
  77.5 56.8 %reduce-scatter.2.cloned.1.call-start = ((), (), s32[]{:S(2)}) async-start(), calls=%async_computation.8 | async-start | bytes 5308416 | tf_op jit(solution)/shard_map/reduce_scatter | solution.py:455
  85.0 8.9 %copy-start.10 = (f32[8,1536]{1,0:T(8,128)S(1)}, f32[8,1536]{1,0:T(8,128)}, u32[]{:S(2)}) copy-start(f32[8,1536]{1,0:T(8,128)} %get-tuple-element.45.up_sum) | copy-start | bytes 147460
  85.0 8.9 %copy-start.11 = (f32[8,384]{1,0:T(8,128)S(1)}, f32[8,384]{1,0:T(8,128)}, u32[]{:S(2)}) copy-start(f32[8,384]{1,0:T(8,128)} %get-tuple-element.44.sums) | copy-start | bytes 36868
  95.1 31.4 %copy-start.19 = (f32[384]{0:T(512)S(1)}, f32[384]{0:T(512)}, u32[]{:S(2)}) copy-start(f32[384]{0:T(512)} %param.29) | copy-start | bytes 4612
  120.6 13.7 %all-to-all-start.4 = ((f32[8,8,512]{2,1,0:T(8,128)}), f32[8,8,512]{2,1,0:T(8,128)S(1)}, u32[]{:S(2)}, u32[]{:S(2)}) async-start(f32[8,8,512]{2,1,0:T(8,128)} %shard_map.278), calls=%async_computation.4 | async-start | bytes 262144 | tf_op jit(solution)/shard_map/all_to_all | solution.py:367
  127.1 5.0 %copy-start = (bf16[1,1,32,32,384]{4,3,2,1,0:T(8,128)(2,1)S(1)}, bf16[1,1,32,32,384]{4,3,2,1,0:T(8,128)(2,1)}, u32[]{:S(2)}) copy-start(bf16[1,1,32,32,384]{4,3,2,1,0:T(8,128)(2,1)} %param.19) | copy-start | bytes 2359300
  127.1 5.0 %copy-start.1 = (bf16[1024,256]{1,0:T(8,128)(2,1)S(1)}, bf16[1024,256]{1,0:T(8,128)(2,1)}, u32[]{:S(2)}) copy-start(bf16[1024,256]{1,0:T(8,128)(2,1)} %constant.28.clone.table_turned) | copy-start | bytes 1572868
  127.1 5.0 %copy-start.2 = (f32[1024,384]{1,0:T(8,128)S(1)}, f32[1024,384]{1,0:T(8,128)}, u32[]{:S(2)}) copy-start(f32[1024,384]{1,0:T(8,128)} %get-tuple-element.48.grad_mixed) | copy-start | bytes 4718596
  127.1 5.0 %copy-start.9 = (f32[1,384]{1,0:T(1,128)S(1)}, f32[1,384]{1,0:T(1,128)}, u32[]{:S(2)}) copy-start(f32[1,384]{1,0:T(1,128)} %reshape.96.gain_one) | copy-start | bytes 4612
  134.3 1.1 copy-start.3
  164.6 7.7 %copy-start.4 = (f32[16,8,512]{2,1,0:T(8,128)}, f32[16,8,512]{2,1,0:T(8,128)S(1)}, u32[]{:S(2)}) copy-start(f32[16,8,512]{2,1,0:T(8,128)S(1)} %get-tuple-element.54.mine) | copy-start | bytes 786436
  164.6 12.4 %all-to-all-start.6 = ((f32[8,24,384]{2,1,0:T(8,128)}), f32[8,24,384]{2,1,0:T(8,128)S(1)}, u32[]{:S(2)}, u32[]{:S(2)}) async-start(f32[8,24,384]{2,1,0:T(8,128)} %get-tuple-element.61), calls=%async_computation.7 | async-start | bytes 589824 | tf_op jit(solution)/shard_map/all_to_all | solution.py:367
  170.7 1.5 collective-permute-start
  172.3 0.7 copy-start.13
Sparse Core Ops, SparseCore 0:
  85.2 44.0 reduce-scatter.1

commit v5 on v4

--- a/solution.py
+++ b/solution.py
@@ -25,7 +25,7 @@
 TOKENS = GY * GZ
 HALF = BLOCKS // 2
 PAIR = 2 * BLOCK
-HBLOCK = 256
+HBLOCK = 768
 CHUNK = 512
 
 Y_CORE = [
@@ -81,9 +81,11 @@
     return high, (value - high.astype(F32)).astype(BF16)
 
 
-def dot3(table_high, table_low, value):
+def dot3(table, value):
     high, low = split(value)
-    return dot(table_high, high) + (dot(table_low, high) + dot(table_high, low))
+    rows = table.shape[0] // 2
+    both = dot(table, high)
+    return both[:rows] + (both[rows:] + dot(table[:rows], low))
 
 
 def dot6(a, b):
@@ -155,9 +157,8 @@
 
 
 def along_x(tables, value, sign):
-    cos_high, cos_low, sin_high, sin_low = (table[...] for table in tables)
-    straight = dot3(cos_high, cos_low, value)
-    crossed = dot3(sin_high, sin_low, times_minus_i(value))
+    straight = dot3(tables[0][...], value)
+    crossed = dot3(tables[1][...], times_minus_i(value))
     return straight + crossed if sign < 0 else straight - crossed
 
 
@@ -167,13 +168,13 @@
     return straight + crossed if sign < 0 else straight - crossed
 
 
-def first_kernel(volume, table_high, table_low, out):
+def first_kernel(volume, table, out):
     unit, _ = normalise(volume[...].astype(F32))
-    to_owners(dot3(table_high[...], table_low[...], unit), out)
-
-
-def filter_kernel(received, cos_high, cos_low, sin_high, sin_low, gain, w_in, b_in, w_out, b_out, sent, spectrum, inner, outer):
-    tables = (cos_high, cos_low, sin_high, sin_low)
+    to_owners(dot3(table[...], unit), out)
+
+
+def filter_kernel(received, cos, sin, gain, w_in, b_in, w_out, b_out, sent, spectrum, inner, outer):
+    tables = (cos, sin)
     unit_spectrum = along_x(tables, received[...], -1)
     spectrum[...] = unit_spectrum
     shrunk = []
@@ -183,7 +184,7 @@
         after = dot6(gelu(before), w_out[block]) + b_out[block]
         outer[block] = after
         shrunk.append(after - jnp.clip(after, -SHRINK, SHRINK))
-    sent[...] = along_x_rounded((cos_high, sin_high), jnp.concatenate(shrunk, axis=1), 1)
+    sent[...] = along_x_rounded([table[: 2 * MODES] for table in tables], jnp.concatenate(shrunk, axis=1), 1)
 
 
 def packed_weight(grad):
@@ -384,9 +385,10 @@
     cotangent = cotangent.reshape(TOKENS, WIDTH)
     gain_one, gain_two, down_bias = (value.reshape(1, WIDTH) for value in (gain_one, gain_two, down_bias))
     slab = slab_table()
-    slab_high, slab_low = (jnp.asarray(part) for part in halves(slab))
+    slab_high, slab_both = jnp.asarray(halves(slab)[0]), jnp.asarray(np.concatenate(halves(slab)))
     slab_turned = jnp.asarray(halves(slab.T)[0])
-    cross = [jnp.asarray(part) for table in cross_tables() for part in halves(table)]
+    cross = [jnp.asarray(np.concatenate(halves(table))) for table in cross_tables()]
+    cross_high = [jnp.asarray(halves(table)[0]) for table in cross_tables()]
     core = lax.axis_index("space") & 1
     w_in, w_out, b_in, b_out = paired(w_in, core), paired(w_out, core), paired_bias(b_in, core), paired_bias(b_out, core)
     gain = lax.dynamic_slice_in_dim(gain_one.reshape(BLOCKS, 1, BLOCK), core * HALF, HALF, 0)
@@ -405,7 +407,7 @@
         return value.reshape(GX, OWN, WIDTH)
 
     wave = sds(PLACES, 2, OWN, WIDTH)
-    modes = call(first_kernel, wave, volume, slab_high, slab_low, mib=60)
+    modes = call(first_kernel, wave, volume, slab_both, mib=60)
     modes = rows(exchange(owners(modes), "space"))
     wide = sds(HALF, 2 * MODES, PAIR)
     modes, spectrum, inner, outer = call(
@@ -463,7 +465,7 @@
         scratch_shapes=[pltpu.VMEM((2 * HALF, BLOCK, PAIR), F32), pltpu.VMEM((SMALL, PAIR), F32)],
         compiler_params=limit(12),
         cost_estimate=pl.CostEstimate(flops=LATE, bytes_accessed=8 * MIB, transcendentals=0),
-    )(modes, cross[0], cross[2], gain, w_in, w_out, spectrum, inner, outer, sums, up_sum)
+    )(modes, *cross_high, gain, w_in, w_out, spectrum, inner, outer, sums, up_sum)
     received = places(exchange(sent, "space"))
     shared = exchange(call(first_sum_kernel, sds(8, 8, 2 * carried), received), "dp")
     grad_volume = pl.pallas_call(

time: 185 us -> 185 us (level)
  no operation moved by 1% of the time
where the time goes in v5:
time: 185 us; the launch traced here: 184 us
  blocking collectives  53.3 us (29%)
  waiting for transfers between devices  42.5 us (23%)
  Pallas kernels  38.2 us (21%)
  starting transfers between devices  30.5 us (16%)
  between operations  14.3 us (8%)
  local copies, waits for them, and re-layouts  5.24 us (3%)
    all_to_all x2, blocking collectives, exchange(): lax.all_to_all(value, axis, split_axis=0, concat_axis=0, axis_index_group...  53.3 us
    all_to_all x5, waiting for transfers between devices, exchange(): lax.all_to_all(value, axis, split_axis=0, concat_axis=0, axis_index_group...  40.9 us
    all_to_all x5, starting transfers between devices, exchange(): lax.all_to_all(value, axis, split_axis=0, concat_axis=0, axis_index_group...  30.5 us
    pallas_call x7, Pallas kernels, call(): pl.pallas_call(kernel, out_shape=out, compiler_params=limit(mib))(*operands)  20.4 us
    pallas_call x1, Pallas kernels, local(): pl.pallas_call(weight_kernel, grid=(HIDDEN // WBLOCK,), in_specs=[whole(T...  7.43 us
    pallas_call x1, Pallas kernels, local(): pl.pallas_call(result_kernel, grid=(TOKENS // CHUNK,), in_specs=[chunk(CH...  4.97 us
  transfers between devices with their start and end apart: 7, of which 5 were waited for; matrix products, arithmetic and copies ran while one was open for 2% of the time, Pallas kernels for 10%

profile of v5, /device:TPU:32, one launch (start us, length us, event | category | flops | bytes accessed | tf_op | source)
XLA Modules:
  0.0 184.3 jit_solution(5328800350589889629)
XLA Ops:
  7.2 0.0 copy-start.16
  7.2 0.0 copy-start.20
  7.2 0.0 copy-start.21
  7.2 3.7 %shard_map.274 = f32[16,2,8,384]{3,2,1,0:T(8,128)} custom-call(bf16[1024,384]{1,0:T(8,128)(2,1)} %bitcast.33, bf16[512,1024]{1,0:T(8,128)(2,1)} %constant.27.clone.table), custom_call_target="tpu_custom_call" | custom-call | tf_op jit(solution)/shard_map/pallas_call | solution.py:364
  10.9 10.5 %all-to-all-start = ((f32[32,8,384]{2,1,0:T(8,128)}), f32[32,8,384]{2,1,0:T(8,128)S(1)}, u32[]{:S(2)}, u32[]{:S(2)}) async-start(f32[32,8,384]{2,1,0:T(8,128)} %bitcast.45), calls=%async_computation | async-start | bytes 786432 | tf_op jit(solution)/shard_map/all_to_all | solution.py:368
  21.5 0.1 reshape_reshape.3
  21.6 0.1 reshape.91.gain
  21.7 0.1 reshape.93.b_out
  21.7 0.1 reshape.92.b_in
  21.9 0.0 copy-start.18
  21.9 0.0 copy-start.17
  21.9 0.1 maximum_maximum_fusion.1.w_out
  22.0 0.1 maximum_maximum_fusion.w_in
  22.2 15.7 %all-to-all-done = f32[32,8,384]{2,1,0:T(8,128)S(1)} async-done(((f32[32,8,384]{2,1,0:T(8,128)}), f32[32,8,384]{2,1,0:T(8,128)S(1)}, u32[]{:S(2)}, u32[]{:S(2)}) %all-to-all-start) | async-done | bytes 393248 | tf_op jit(solution)/shard_map/all_to_all | solution.py:368
  37.9 2.6 %shard_map.275 = (f32[256,384]{1,0:T(8,128)}, f32[256,384]{1,0:T(8,128)S(1)}, f32[3,256,128]{2,1,0:T(8,128)S(1)}, f32[3,256,128]{2,1,0:T(8,128)S(1)}) custom-call(f32[256,384]{1,0:T(8,128)S(1)} %bitcast.38, bf16[512,256]{1,0:T(8,128)(2,1)S(1)} %copy-done.5, bf16[512,256]{1,0:T(8,128)(2,1)S(1)} %copy-done.4, f32[1,384]{1,0:T(1,128)S(1)} %reshape.91.gain, ...), custom_call_target="tpu_custom_call" | custom-call | tf_op jit(solution)/shard_map/pallas_call | solution.py:364
  40.5 4.1 %all-to-all-start.1 = ((f32[32,8,384]{2,1,0:T(8,128)}), f32[32,8,384]{2,1,0:T(8,128)S(1)}, u32[]{:S(2)}, u32[]{:S(2)}) async-start(f32[32,8,384]{2,1,0:T(8,128)} %bitcast.11), calls=%async_computation.1 | async-start | bytes 786432 | tf_op jit(solution)/shard_map/all_to_all | solution.py:368
  44.5 0.6 reshape.96.gain_one
  45.1 0.6 reshape.97.gain_two
  45.7 0.6 reshape.98.up_bias
  46.3 14.4 %all-to-all-done.1 = f32[32,8,384]{2,1,0:T(8,128)S(1)} async-done(((f32[32,8,384]{2,1,0:T(8,128)}), f32[32,8,384]{2,1,0:T(8,128)S(1)}, u32[]{:S(2)}, u32[]{:S(2)}) %all-to-all-start.1) | async-done | bytes 393248 | tf_op jit(solution)/shard_map/all_to_all | solution.py:368
  60.7 0.7 copy-done.12
  61.4 11.9 %shard_map.276 = (f32[1024,384]{1,0:T(8,128)}, bf16[1024,384]{1,0:T(8,128)(2,1)}, bf16[1024,1536]{1,0:T(8,128)(2,1)}, bf16[1024,1536]{1,0:T(8,128)(2,1)}, f32[10...) custom-call(bf16[1024,384]{1,0:T(8,128)(2,1)} %bitcast.34, ...), custom_call_target="tpu_custom_call" | custom-call | tf_op jit(solution)/shard_map/pallas_call | solution.py:364
  73.4 3.9 %all-to-all-start.2 = ((f32[32,8,384]{2,1,0:T(8,128)}), f32[32,8,384]{2,1,0:T(8,128)S(1)}, u32[]{:S(2)}, u32[]{:S(2)}) async-start(f32[32,8,384]{2,1,0:T(8,128)} %bitcast.48), calls=%async_computation.2 | async-start | bytes 786432 | tf_op jit(solution)/shard_map/all_to_all | solution.py:368
  77.2 0.0 reduce-scatter.2.cloned.1.call-start
  77.3 7.4 %shard_map.281 = f32[4,2,16,24,384]{4,3,2,1,0:T(8,128)} custom-call(bf16[1024,384]{1,0:T(8,128)(2,1)} %get-tuple-element.52.inputs, bf16[1024,384]{1,0:T(8,128)(2,1)} %bitcast.43, bf16[1024,1536]{1,0:T(8,128)(2,1)} %get-tuple-element.47.hidden, bf16[1024,1536]{1,0:T(8,128)(2,1)} %get-tuple-element.53.grad_before), custom_call_target="tpu_custom_call" | custom-call | flops 2415919104 | bytes 12582912 | tf_op jit(solution)/shard_map/pallas_call | solution.py:437
  84.7 0.0 copy-start.11
  84.7 0.0 reduce-scatter.2.cloned.1.call-update
  84.8 8.8 %all-to-all-done.2 = f32[32,8,384]{2,1,0:T(8,128)S(1)} async-done(((f32[32,8,384]{2,1,0:T(8,128)}), f32[32,8,384]{2,1,0:T(8,128)S(1)}, u32[]{:S(2)}, u32[]{:S(2)}) %all-to-all-start.2) | async-done | bytes 393248 | tf_op jit(solution)/shard_map/all_to_all | solution.py:368
  93.6 1.3 shard_map.277
  94.9 0.0 copy-start.19
  94.9 24.9 %all_to_all.35 = f32[32,8,640]{2,1,0:T(8,128)S(1)} all-to-all(f32[32,8,640]{2,1,0:T(8,128)S(1)} %shard_map.277), channel_id=1, replica_groups=mesh['dp'=8,'space'=32] {'space'}, dimensions={0} | all-to-all | bytes 1310720 | tf_op jit(solution)/shard_map/all_to_all | solution.py:368
  119.8 0.7 shard_map.278
  120.4 5.9 %all-to-all-start.4 = ((f32[8,8,512]{2,1,0:T(8,128)}), f32[8,8,512]{2,1,0:T(8,128)S(1)}, u32[]{:S(2)}, u32[]{:S(2)}) async-start(f32[8,8,512]{2,1,0:T(8,128)} %shard_map.278), calls=%async_computation.4 | async-start | bytes 262144 | tf_op jit(solution)/shard_map/all_to_all | solution.py:368
  126.3 0.6 reshape.102.down_bias
  126.9 5.0 %shard_map.279 = bf16[1024,384]{1,0:T(8,128)(2,1)} custom-call(f32[1024,384]{1,0:T(8,128)} %get-tuple-element.46.mixed, bf16[1024,1536]{1,0:T(8,128)(2,1)} %get-tuple-element.47.hidden, bf16[1536,384]{1,0:T(8,128)(2,1)} %down.3, f32[1,384]{1,0:T(1,128)} %reshape.102.down_bias), custom_call_target="tpu_custom_call" | custom-call | flops 1207959552 | bytes 7340032 | tf_op jit(solution)/shard_map/pallas_call | solution.py:446
  131.9 2.2 %shard_map.280 = bf16[1024,384]{1,0:T(8,128)(2,1)} custom-call(bf16[1024,384]{1,0:T(8,128)(2,1)S(1)} %bitcast.35, f32[16,2,8,640]{3,2,1,0:T(8,128)S(1)} %bitcast.37, bf16[1024,256]{1,0:T(8,128)(2,1)S(1)} %copy-done.1, f32[1,384]{1,0:T(1,128)S(1)} %copy-done.7, f32[1024,384]{1,0:T(8,128)S(1)} %copy-done.2), custom_call_target="tpu_custom_call" | custom-call | flops 402653184 | bytes 8388608 | tf_op jit(solution)/shard_map/pallas_call | solution.py:471
  134.0 0.0 all-to-all-done.4.received
  134.1 1.1 copy-done.3
  135.1 0.1 shard_map.282
  135.2 28.4 %all_to_all.36.received = f32[16,8,1664]{2,1,0:T(8,128)S(1)} all-to-all(f32[16,8,1664]{2,1,0:T(8,128)S(1)} %shard_map.282), channel_id=1, replica_groups={{0,2,4,6,8,10,12,14,16,18,20,22,24,26,28,30},{1,3,5,7,9,11,13,15,17,19,..., dimensions={0} | all-to-all | bytes 1703936 | tf_op jit(solution)/shard_map/all_to_all | solution.py:368
  163.6 0.8 shard_map.283
  164.3 6.1 %all-to-all-start.6 = ((f32[8,24,384]{2,1,0:T(8,128)}), f32[8,24,384]{2,1,0:T(8,128)S(1)}, u32[]{:S(2)}, u32[]{:S(2)}) async-start(f32[8,24,384]{2,1,0:T(8,128)} %get-tuple-element.61), calls=%async_computation.7 | async-start | bytes 589824 | tf_op jit(solution)/shard_map/all_to_all | solution.py:368
  170.5 0.0 collective-permute-start
  170.5 1.5 collective-permute-done.other
  172.0 0.7 copy-done.13
  172.7 2.0 %shard_map.284 = (f32[2,6,64,64]{3,2,1,0:T(8,128)}, f32[2,6,64,64]{3,2,1,0:T(8,128)}, f32[6,2,64]{2,1,0:T(2,128)}, f32[6,2,64]{2,1,0:T(2,128)}, f32[384]{0:T(512...) custom-call(s32[1]{0:T(128)} %bitcast.18.core, f32[16,8,512]{2,1,0:T(8,128)} %copy-done.6, f32[16,8,512]{2,1,0:T(8,128)} %copy-done.13), custom_call_target="tpu_custom_call" | custom-call | tf_op jit(solution)/shard_map/pallas_call | solution.py:493
  174.8 2.0 %all-to-all-done.6.received = f32[8,24,384]{2,1,0:T(8,128)S(1)} async-done(((f32[8,24,384]{2,1,0:T(8,128)}), f32[8,24,384]{2,1,0:T(8,128)S(1)}, u32[]{:S(2)}, u32[]{:S(2)}) %all-to-all-start.6) | async-done | bytes 294944 | tf_op jit(solution)/shard_map/all_to_all | solution.py:368
  176.8 0.7 shard_map.285
  (40 shorter events, 0.1 us)
Async XLA Ops:
  7.2 14.3 %copy-start.16 = (f32[384]{0:T(512)S(1)}, f32[384]{0:T(512)}, u32[]{:S(2)}) copy-start(f32[384]{0:T(512)} %param.20) | copy-start | bytes 4612
  7.2 14.5 %copy-start.20 = (f32[2,6,64]{2,0,1:T(2,128)S(1)}, f32[2,6,64]{2,0,1:T(2,128)}, u32[]{:S(2)}) copy-start(f32[2,6,64]{2,0,1:T(2,128)} %param.25) | copy-start | bytes 9220
  7.2 14.5 %copy-start.21 = (f32[2,6,64]{2,0,1:T(2,128)S(1)}, f32[2,6,64]{2,0,1:T(2,128)}, u32[]{:S(2)}) copy-start(f32[2,6,64]{2,0,1:T(2,128)} %param.23) | copy-start | bytes 9220
  7.2 14.6 %copy-start.14 = (f32[2,6,64,64]{3,2,1,0:T(8,128)S(1)}, f32[2,6,64,64]{3,2,1,0:T(8,128)}, u32[]{:S(2)}) copy-start(f32[2,6,64,64]{3,2,1,0:T(8,128)} %param.24) | copy-start | bytes 589828
  7.2 14.6 %copy-start.15 = (f32[2,6,64,64]{3,2,1,0:T(8,128)S(1)}, f32[2,6,64,64]{3,2,1,0:T(8,128)}, u32[]{:S(2)}) copy-start(f32[2,6,64,64]{3,2,1,0:T(8,128)} %param.22) | copy-start | bytes 589828
  10.9 27.0 %copy-start.4 = (bf16[512,256]{1,0:T(8,128)(2,1)S(1)}, bf16[512,256]{1,0:T(8,128)(2,1)}, u32[]{:S(2)}) copy-start(bf16[512,256]{1,0:T(8,128)(2,1)} %constant.30.clone.sin) | copy-start | bytes 786436
  10.9 27.0 %copy-start.5 = (bf16[512,256]{1,0:T(8,128)(2,1)S(1)}, bf16[512,256]{1,0:T(8,128)(2,1)}, u32[]{:S(2)}) copy-start(bf16[512,256]{1,0:T(8,128)(2,1)} %constant.29.clone.cos) | copy-start | bytes 786436
  10.9 26.9 %all-to-all-start = ((f32[32,8,384]{2,1,0:T(8,128)}), f32[32,8,384]{2,1,0:T(8,128)S(1)}, u32[]{:S(2)}, u32[]{:S(2)}) async-start(f32[32,8,384]{2,1,0:T(8,128)} %bitcast.45), calls=%async_computation | async-start | bytes 786432 | tf_op jit(solution)/shard_map/all_to_all | solution.py:368
  21.9 23.2 %copy-start.18 = (f32[384]{0:T(512)S(1)}, f32[384]{0:T(512)}, u32[]{:S(2)}) copy-start(f32[384]{0:T(512)} %param.21) | copy-start | bytes 4612
  21.9 23.8 %copy-start.17 = (f32[1536]{0:T(1024)S(1)}, f32[1536]{0:T(1024)}, u32[]{:S(2)}) copy-start(f32[1536]{0:T(1024)} %param.27) | copy-start | bytes 18436
  40.5 20.2 %all-to-all-start.1 = ((f32[32,8,384]{2,1,0:T(8,128)}), f32[32,8,384]{2,1,0:T(8,128)S(1)}, u32[]{:S(2)}, u32[]{:S(2)}) async-start(f32[32,8,384]{2,1,0:T(8,128)} %bitcast.11), calls=%async_computation.1 | async-start | bytes 786432 | tf_op jit(solution)/shard_map/all_to_all | solution.py:368
  60.7 0.7 copy-start.12
  73.4 20.2 %all-to-all-start.2 = ((f32[32,8,384]{2,1,0:T(8,128)}), f32[32,8,384]{2,1,0:T(8,128)S(1)}, u32[]{:S(2)}, u32[]{:S(2)}) async-start(f32[32,8,384]{2,1,0:T(8,128)} %bitcast.48), calls=%async_computation.2 | async-start | bytes 786432 | tf_op jit(solution)/shard_map/all_to_all | solution.py:368
  77.2 56.8 %reduce-scatter.2.cloned.1.call-start = ((), (), s32[]{:S(2)}) async-start(), calls=%async_computation.8 | async-start | bytes 5308416 | tf_op jit(solution)/shard_map/reduce_scatter | solution.py:457
  84.7 8.8 %copy-start.8 = (f32[8,1536]{1,0:T(8,128)S(1)}, f32[8,1536]{1,0:T(8,128)}, u32[]{:S(2)}) copy-start(f32[8,1536]{1,0:T(8,128)} %get-tuple-element.45.up_sum) | copy-start | bytes 147460
  84.7 8.8 %copy-start.9 = (f32[8,384]{1,0:T(8,128)S(1)}, f32[8,384]{1,0:T(8,128)}, u32[]{:S(2)}) copy-start(f32[8,384]{1,0:T(8,128)} %get-tuple-element.44.sums) | copy-start | bytes 36868
  84.7 8.8 %copy-start.10 = (bf16[256,256]{1,0:T(8,128)(2,1)S(1)}, bf16[256,256]{1,0:T(8,128)(2,1)}, u32[]{:S(2)}) copy-start(bf16[256,256]{1,0:T(8,128)(2,1)} %constant.32.clone.sin) | copy-start | bytes 393220
  84.7 8.8 %copy-start.11 = (bf16[256,256]{1,0:T(8,128)(2,1)S(1)}, bf16[256,256]{1,0:T(8,128)(2,1)}, u32[]{:S(2)}) copy-start(bf16[256,256]{1,0:T(8,128)(2,1)} %constant.31.clone.cos) | copy-start | bytes 393220
  94.9 31.5 %copy-start.19 = (f32[384]{0:T(512)S(1)}, f32[384]{0:T(512)}, u32[]{:S(2)}) copy-start(f32[384]{0:T(512)} %param.29) | copy-start | bytes 4612
  120.4 13.6 %all-to-all-start.4 = ((f32[8,8,512]{2,1,0:T(8,128)}), f32[8,8,512]{2,1,0:T(8,128)S(1)}, u32[]{:S(2)}, u32[]{:S(2)}) async-start(f32[8,8,512]{2,1,0:T(8,128)} %shard_map.278), calls=%async_computation.4 | async-start | bytes 262144 | tf_op jit(solution)/shard_map/all_to_all | solution.py:368
  126.9 5.0 %copy-start = (bf16[1,1,32,32,384]{4,3,2,1,0:T(8,128)(2,1)S(1)}, bf16[1,1,32,32,384]{4,3,2,1,0:T(8,128)(2,1)}, u32[]{:S(2)}) copy-start(bf16[1,1,32,32,384]{4,3,2,1,0:T(8,128)(2,1)} %param.19) | copy-start | bytes 2359300
  126.9 5.0 %copy-start.1 = (bf16[1024,256]{1,0:T(8,128)(2,1)S(1)}, bf16[1024,256]{1,0:T(8,128)(2,1)}, u32[]{:S(2)}) copy-start(bf16[1024,256]{1,0:T(8,128)(2,1)} %constant.28.clone.table_turned) | copy-start | bytes 1572868
  126.9 5.0 %copy-start.2 = (f32[1024,384]{1,0:T(8,128)S(1)}, f32[1024,384]{1,0:T(8,128)}, u32[]{:S(2)}) copy-start(f32[1024,384]{1,0:T(8,128)} %get-tuple-element.48.grad_mixed) | copy-start | bytes 4718596
  126.9 5.0 %copy-start.7 = (f32[1,384]{1,0:T(1,128)S(1)}, f32[1,384]{1,0:T(1,128)}, u32[]{:S(2)}) copy-start(f32[1,384]{1,0:T(1,128)} %reshape.96.gain_one) | copy-start | bytes 4612
  134.1 1.1 copy-start.3
  164.3 7.7 %copy-start.6 = (f32[16,8,512]{2,1,0:T(8,128)}, f32[16,8,512]{2,1,0:T(8,128)S(1)}, u32[]{:S(2)}) copy-start(f32[16,8,512]{2,1,0:T(8,128)S(1)} %get-tuple-element.54.mine) | copy-start | bytes 786436
  164.3 12.4 %all-to-all-start.6 = ((f32[8,24,384]{2,1,0:T(8,128)}), f32[8,24,384]{2,1,0:T(8,128)S(1)}, u32[]{:S(2)}, u32[]{:S(2)}) async-start(f32[8,24,384]{2,1,0:T(8,128)} %get-tuple-element.61), calls=%async_computation.7 | async-start | bytes 589824 | tf_op jit(solution)/shard_map/all_to_all | solution.py:368
  170.5 1.5 collective-permute-start
  172.0 0.7 copy-start.13
Sparse Core Ops, SparseCore 0:
  84.9 44.1 reduce-scatter.1
